TPU v7x, 32 devices: a whole 2x2x4 slice. The times are simulated.
32 devices in a mesh: dp: 16 (over z, y, x), tensor: 2 (over core).
Axes of the slice: x: 2, y: 2, z: 4, core: 2. Of those that a mesh axis runs over, the one named last changes fastest.
Arguments:
- tokens: bfloat16 [12288, 2048], P(('dp', 'tensor')), may hold values from -6 to 6
- cotangent: bfloat16 [12288, 2048], P(('dp', 'tensor')), may hold values from -6 to 6
- segments: int32 [16, 768], P('dp'), may hold values from 0 to 3, never falling along the last dimension, each value on 1 to 576 neighbouring positions
- query_weight: float32 [2048, 2048], P('dp', 'tensor'), may hold values from -0.125 to 0.125
- key_weight: float32 [2048, 256], P('dp', 'tensor'), may hold values from -0.125 to 0.125
- value_weight: float32 [2048, 256], P('dp', 'tensor'), may hold values from -0.125 to 0.125
- out_weight: float32 [2048, 2048], P('dp', 'tensor'), may hold values from -1 to 1
- gate_weight: float32 [2048, 5632], P('dp', 'tensor'), may hold values from -0.125 to 0.125
- up_weight: float32 [2048, 5632], P('dp', 'tensor'), may hold values from -0.125 to 0.125
- down_weight: float32 [2048, 5632], P('dp', 'tensor'), may hold values from -0.078125 to 0.078125
- norm_gains: float32 [2, 2048], P(None, 'dp'), may hold values from 0.5 to 1.5
- query_moment: float32 [2048, 2048], P('dp', 'tensor'), may hold values from -56 to 56
- key_moment: float32 [2048, 256], P('dp', 'tensor'), may hold values from -160 to 160
- value_moment: float32 [2048, 256], P('dp', 'tensor'), may hold values from -160 to 160
- out_moment: float32 [2048, 2048], P('dp', 'tensor'), may hold values from -10 to 10
- gate_moment: float32 [2048, 5632], P('dp', 'tensor'), may hold values from -20 to 20
- up_moment: float32 [2048, 5632], P('dp', 'tensor'), may hold values from -28 to 28
- down_moment: float32 [2048, 5632], P('dp', 'tensor'), may hold values from -40 to 40
- gains_moment: float32 [2, 2048], P(None, 'dp'), may hold values from -64 to 64
- query_square: float32 [2048, 2048], P('dp', 'tensor'), may hold values from 203.9808 to 1646.592
- key_square: float32 [2048, 256], P('dp', 'tensor'), may hold values from 1695.744 to 13639.68
- value_square: float32 [2048, 256], P('dp', 'tensor'), may hold values from 1695.744 to 13639.68
- out_square: float32 [2048, 2048], P('dp', 'tensor'), may hold values from 7.24992 to 57.7536
- gate_square: float32 [2048, 5632], P('dp', 'tensor'), may hold values from 28.2624 to 233.472
- up_square: float32 [2048, 5632], P('dp', 'tensor'), may hold values from 41.7792 to 331.776
- down_square: float32 [2048, 5632], P('dp', 'tensor'), may hold values from 115.5072 to 933.888
- gains_square: float32 [2, 2048], P(None, 'dp'), may hold values from 319.488 to 2580.48
Outputs:
- activations: bfloat16 [12288, 2048], P(('dp', 'tensor'))
- input_grad: float32 [12288, 2048], P(('dp', 'tensor'))
- query_grad: float32 [2048, 2048], P('dp', 'tensor')
- query_moment_new: float32 [2048, 2048], P('dp', 'tensor')
- query_square_new: float32 [2048, 2048], P('dp', 'tensor')
- query_new: float32 [2048, 2048], P('dp', 'tensor')
- key_grad: float32 [2048, 256], P('dp', 'tensor')
- key_moment_new: float32 [2048, 256], P('dp', 'tensor')
- key_square_new: float32 [2048, 256], P('dp', 'tensor')
- key_new: float32 [2048, 256], P('dp', 'tensor')
- value_grad: float32 [2048, 256], P('dp', 'tensor')
- value_moment_new: float32 [2048, 256], P('dp', 'tensor')
- value_square_new: float32 [2048, 256], P('dp', 'tensor')
- value_new: float32 [2048, 256], P('dp', 'tensor')
- out_grad: float32 [2048, 2048], P('dp', 'tensor')
- out_moment_new: float32 [2048, 2048], P('dp', 'tensor')
- out_square_new: float32 [2048, 2048], P('dp', 'tensor')
- out_new: float32 [2048, 2048], P('dp', 'tensor')
- gate_grad: float32 [2048, 5632], P('dp', 'tensor')
- gate_moment_new: float32 [2048, 5632], P('dp', 'tensor')
- gate_square_new: float32 [2048, 5632], P('dp', 'tensor')
- gate_new: float32 [2048, 5632], P('dp', 'tensor')
- up_grad: float32 [2048, 5632], P('dp', 'tensor')
- up_moment_new: float32 [2048, 5632], P('dp', 'tensor')
- up_square_new: float32 [2048, 5632], P('dp', 'tensor')
- up_new: float32 [2048, 5632], P('dp', 'tensor')
- down_grad: float32 [2048, 5632], P('dp', 'tensor')
- down_moment_new: float32 [2048, 5632], P('dp', 'tensor')
- down_square_new: float32 [2048, 5632], P('dp', 'tensor')
- down_new: float32 [2048, 5632], P('dp', 'tensor')
- gains_grad: float32 [2, 2048], P(None, 'dp')
- gains_moment_new: float32 [2, 2048], P(None, 'dp')
- gains_square_new: float32 [2, 2048], P(None, 'dp')
- gains_new: float32 [2, 2048], P(None, 'dp')
Inputs may be any that keep to these rules, and one draw needn't show every extreme that they name: `segments`: within each sequence the numbers never fall, each number marks one document of at most 576 tokens, and one document of every sequence has exactly 576 tokens.
All inputs are finite; a program needn't handle non-finite values.
Results may differ from a plain program's by a relative error of at most 0.014.
The roundings to bfloat16 on the way count: a program that leaves them out, or rounds other values in their place, can miss the bound.
Values may be sent and summed in bfloat16 or wider, within the bound.
No kernel may reach another device: no remote copies, remote signals or barrier semaphores. Data moves between devices by JAX's collectives and lax.ppermute only.
A program may use at most 320 MiB of HBM per device.

v0:
```python
import math

import jax
import jax.numpy as jnp
from jax import lax
from jax.sharding import PartitionSpec as P

HEAD = 64
STEP = 10


NORM_EPS = 1e-05
NEG_LARGE = -1000000000.0
BETA_FIRST = 0.9
BETA_SECOND = 0.95
ADAM_EPS = 1e-08
DECAY_RATE = 0.1
RATE_MAIN = 0.02
RATE_OUT = 0.15
RATE_DOWN = 0.015
RATE_GAINS = 0.6


def rope_tables(segment):
    length = segment.shape[0]
    order = jnp.arange(length, dtype=jnp.int32)
    before = jnp.sum((segment[None, :] < segment[:, None]).astype(jnp.int32), axis=1)
    place = (order - before).astype(jnp.float32)
    half = HEAD // 2
    freq = jnp.exp(jnp.arange(half, dtype=jnp.float32) * (-2.0 * math.log(10000.0) / HEAD))
    angle = place[:, None] * freq[None, :]
    return (jnp.cos(angle)[:, None, :], jnp.sin(angle)[:, None, :])


def allowed_pairs(segment):
    length = segment.shape[0]
    order = jnp.arange(length, dtype=jnp.int32)
    return (segment[:, None] == segment[None, :]) & (order[None, :] <= order[:, None])


def rotate(values, cosine, sine):
    half = HEAD // 2
    first = values[..., :half]
    second = values[..., half:]
    return jnp.concatenate(
        [first * cosine - second * sine, second * cosine + first * sine], axis=-1
    )


def rotate_back(grads, cosine, sine):
    half = HEAD // 2
    first = grads[..., :half]
    second = grads[..., half:]
    return jnp.concatenate(
        [first * cosine + second * sine, second * cosine - first * sine], axis=-1
    )


def norm_back(values, inverse, gain, upstream):
    weighted = gain * upstream
    grad_in = inverse * weighted - values * inverse**3 * jnp.mean(
        weighted * values, axis=1, keepdims=True
    )
    grad_gain = jnp.sum(upstream * values * inverse, axis=0)
    return (grad_in, grad_gain)


def contract_rows(left, right):
    return lax.dot_general(
        left, right, (((0,), (0,)), ((), ())), preferred_element_type=jnp.float32
    )


def contract_cols(left, right):
    return lax.dot_general(
        left, right, (((1,), (1,)), ((), ())), preferred_element_type=jnp.float32
    )


def adam(weight, grad, moment, square, rate, decay):
    moment_new = BETA_FIRST * moment + (1.0 - BETA_FIRST) * grad
    square_new = BETA_SECOND * square + (1.0 - BETA_SECOND) * grad * grad
    direction = (
        moment_new
        / (1.0 - BETA_FIRST**STEP)
        / (jnp.sqrt(square_new / (1.0 - BETA_SECOND**STEP)) + ADAM_EPS)
    )
    return (grad, moment_new, square_new, weight - rate * (direction + decay * weight))


def shards(
    tokens,
    cotangent,
    segments,
    query_weight,
    key_weight,
    value_weight,
    out_weight,
    gate_weight,
    up_weight,
    down_weight,
    norm_gains,
    query_moment,
    key_moment,
    value_moment,
    out_moment,
    gate_moment,
    up_moment,
    down_moment,
    gains_moment,
    query_square,
    key_square,
    value_square,
    out_square,
    gate_square,
    up_square,
    down_square,
    gains_square,
):
    lowtype = jnp.bfloat16
    scale = HEAD ** (-0.5)
    query_all, key_all, value_all, out_all, gain_all = (
        lax.all_gather(query_weight.astype(lowtype), "dp", axis=0, tiled=True),
        lax.all_gather(key_weight.astype(lowtype), "dp", axis=0, tiled=True),
        lax.all_gather(value_weight.astype(lowtype), "dp", axis=0, tiled=True),
        lax.all_gather(out_weight.astype(lowtype), "dp", axis=0, tiled=True),
        lax.all_gather(norm_gains.astype(lowtype), "dp", axis=1, tiled=True),
    )
    gain_one = gain_all[0].astype(jnp.float32)
    gain_two = gain_all[1].astype(jnp.float32)
    inputs = tokens.astype(jnp.float32)
    inverse_one = lax.rsqrt(jnp.mean(inputs * inputs, axis=1, keepdims=True) + NORM_EPS)
    normed_one = (inputs * inverse_one * gain_one).astype(lowtype)
    normed_one_all = lax.all_gather(normed_one, "tensor", axis=0, tiled=True)
    seq_rows = normed_one_all.shape[0]
    segment = segments[0]
    cosine, sine = rope_tables(segment)
    allowed = allowed_pairs(segment)
    heads_here = query_all.shape[1] // HEAD
    groups_here = key_all.shape[1] // HEAD
    ratio = heads_here // groups_here
    query_pre = jnp.dot(normed_one_all, query_all, preferred_element_type=jnp.float32)
    key_pre = jnp.dot(normed_one_all, key_all, preferred_element_type=jnp.float32)
    value_pre = jnp.dot(normed_one_all, value_all, preferred_element_type=jnp.float32)
    queries = rotate(query_pre.reshape(seq_rows, heads_here, HEAD), cosine, sine).astype(lowtype)
    queries = queries.reshape(seq_rows, groups_here, ratio, HEAD)
    keys = rotate(key_pre.reshape(seq_rows, groups_here, HEAD), cosine, sine).astype(lowtype)
    values = value_pre.astype(lowtype).reshape(seq_rows, groups_here, HEAD)

    def scores_of(query_group, key_group):
        raw = jnp.einsum("qrd,kd->rqk", query_group, key_group, preferred_element_type=jnp.float32)
        return jnp.where(allowed[None], raw * scale, NEG_LARGE)

    attended_list = []
    log_totals = []
    for group_index in range(groups_here):
        score = scores_of(queries[:, group_index], keys[:, group_index])
        largest = jnp.max(score, axis=2, keepdims=True)
        expo = jnp.exp(score - largest)
        total = jnp.sum(expo, axis=2, keepdims=True)
        probs_low = (expo / total).astype(lowtype)
        log_totals.append(largest + jnp.log(total))
        attended_list.append(
            jnp.einsum(
                "rqk,kd->qrd", probs_low, values[:, group_index], preferred_element_type=jnp.float32
            )
        )
    attended = jnp.stack(attended_list, axis=1).reshape(seq_rows, heads_here * HEAD).astype(lowtype)
    attn_part = contract_cols(attended, out_all)
    attn_sum = lax.psum_scatter(attn_part, "tensor", scatter_dimension=0, tiled=True)
    hidden_state = inputs + attn_sum
    gate_all, up_all, down_all = (
        lax.all_gather(gate_weight.astype(lowtype), "dp", axis=0, tiled=True),
        lax.all_gather(up_weight.astype(lowtype), "dp", axis=0, tiled=True),
        lax.all_gather(down_weight.astype(lowtype), "dp", axis=0, tiled=True),
    )
    inverse_two = lax.rsqrt(jnp.mean(hidden_state * hidden_state, axis=1, keepdims=True) + NORM_EPS)
    normed_two = (hidden_state * inverse_two * gain_two).astype(lowtype)
    normed_two_all = lax.all_gather(normed_two, "tensor", axis=0, tiled=True)
    gate = jnp.dot(normed_two_all, gate_all, preferred_element_type=jnp.float32)
    upper = jnp.dot(normed_two_all, up_all, preferred_element_type=jnp.float32)
    sigma = jax.nn.sigmoid(gate)
    inner = (gate * sigma * upper).astype(lowtype)
    ffn_part = contract_cols(inner, down_all)
    ffn_sum = lax.psum_scatter(
        ffn_part.astype(jnp.bfloat16), "tensor", scatter_dimension=0, tiled=True
    ).astype(jnp.float32)
    activations = (hidden_state + ffn_sum).astype(lowtype)
    upstream_all = lax.all_gather(cotangent, "tensor", axis=0, tiled=True)
    grad_inner = jnp.dot(upstream_all, down_all, preferred_element_type=jnp.float32)
    down_grad_full = contract_rows(upstream_all, inner)
    grad_gate = (grad_inner * upper * sigma * (1.0 + gate * (1.0 - sigma))).astype(lowtype)
    grad_upper = (grad_inner * gate * sigma).astype(lowtype)
    gate_grad_full = contract_rows(normed_two_all, grad_gate)
    up_grad_full = contract_rows(normed_two_all, grad_upper)
    normed_two_part = contract_cols(grad_gate, gate_all) + contract_cols(grad_upper, up_all)
    grad_normed_two = lax.psum_scatter(normed_two_part, "tensor", scatter_dimension=0, tiled=True)
    hidden_back, gain_two_grad = norm_back(hidden_state, inverse_two, gain_two, grad_normed_two)
    hidden_grad = cotangent.astype(jnp.float32) + hidden_back
    attn_grad_low = hidden_grad.astype(lowtype)
    attn_grad_all = lax.all_gather(attn_grad_low, "tensor", axis=0, tiled=True)
    attended_grad = jnp.dot(attn_grad_all, out_all, preferred_element_type=jnp.float32).astype(
        lowtype
    )
    out_grad_full = contract_rows(attn_grad_all, attended)
    attended_grad = attended_grad.reshape(seq_rows, groups_here, ratio, HEAD)
    query_grads = []
    key_grads = []
    value_grads = []
    for group_index in range(groups_here):
        query_group = queries[:, group_index]
        key_group = keys[:, group_index]
        upstream_group = attended_grad[:, group_index]
        score = scores_of(query_group, key_group)
        probs = jnp.exp(score - log_totals[group_index])
        probs_low = probs.astype(lowtype)
        value_grads.append(
            jnp.einsum("rqk,qrd->kd", probs_low, upstream_group, preferred_element_type=jnp.float32)
        )
        probs_grad = jnp.einsum(
            "qrd,kd->rqk",
            upstream_group,
            values[:, group_index],
            preferred_element_type=jnp.float32,
        )
        delta = jnp.sum(probs * probs_grad, axis=2, keepdims=True)
        score_grad = (probs * (probs_grad - delta) * scale).astype(lowtype)
        query_grads.append(
            jnp.einsum("rqk,kd->qrd", score_grad, key_group, preferred_element_type=jnp.float32)
        )
        key_grads.append(
            jnp.einsum("rqk,qrd->kd", score_grad, query_group, preferred_element_type=jnp.float32)
        )
    query_back = jnp.stack(query_grads, axis=1).reshape(seq_rows, heads_here, HEAD)
    query_back = (
        rotate_back(query_back, cosine, sine).astype(lowtype).reshape(seq_rows, heads_here * HEAD)
    )
    key_back = (
        rotate_back(jnp.stack(key_grads, axis=1), cosine, sine)
        .astype(lowtype)
        .reshape(seq_rows, groups_here * HEAD)
    )
    value_back = (
        jnp.stack(value_grads, axis=1).astype(lowtype).reshape(seq_rows, groups_here * HEAD)
    )
    query_grad_full = contract_rows(normed_one_all, query_back)
    key_grad_full = contract_rows(normed_one_all, key_back)
    value_grad_full = contract_rows(normed_one_all, value_back)
    normed_one_part = (
        contract_cols(query_back, query_all)
        + contract_cols(key_back, key_all)
        + contract_cols(value_back, value_all)
    )
    grad_normed_one = lax.psum_scatter(normed_one_part, "tensor", scatter_dimension=0, tiled=True)
    input_back, gain_one_grad = norm_back(inputs, inverse_one, gain_one, grad_normed_one)
    input_grad = hidden_grad + input_back
    gains_total = lax.psum(jnp.stack([gain_one_grad, gain_two_grad], axis=0), "tensor")
    (
        query_shard,
        key_shard,
        value_shard,
        out_shard,
        gate_shard,
        up_shard,
        down_shard,
        gains_shard,
    ) = (
        lax.psum_scatter(query_grad_full, "dp", scatter_dimension=0, tiled=True),
        lax.psum_scatter(key_grad_full, "dp", scatter_dimension=0, tiled=True),
        lax.psum_scatter(value_grad_full, "dp", scatter_dimension=0, tiled=True),
        lax.psum_scatter(out_grad_full, "dp", scatter_dimension=0, tiled=True),
        lax.psum_scatter(gate_grad_full, "dp", scatter_dimension=0, tiled=True),
        lax.psum_scatter(up_grad_full, "dp", scatter_dimension=0, tiled=True),
        lax.psum_scatter(down_grad_full, "dp", scatter_dimension=0, tiled=True),
        lax.psum_scatter(gains_total, "dp", scatter_dimension=1, tiled=True),
    )
    q_all = adam(query_weight, query_shard, query_moment, query_square, RATE_MAIN, DECAY_RATE)
    k_all = adam(key_weight, key_shard, key_moment, key_square, RATE_MAIN, DECAY_RATE)
    v_all = adam(value_weight, value_shard, value_moment, value_square, RATE_MAIN, DECAY_RATE)
    o_all = adam(out_weight, out_shard, out_moment, out_square, RATE_OUT, DECAY_RATE)
    g_all = adam(gate_weight, gate_shard, gate_moment, gate_square, RATE_MAIN, DECAY_RATE)
    u_all = adam(up_weight, up_shard, up_moment, up_square, RATE_MAIN, DECAY_RATE)
    d_all = adam(down_weight, down_shard, down_moment, down_square, RATE_DOWN, DECAY_RATE)
    n_all = adam(norm_gains, gains_shard, gains_moment, gains_square, RATE_GAINS, 0.0)
    return (
        activations,
        input_grad,
        q_all[0],
        q_all[1],
        q_all[2],
        q_all[3],
        k_all[0],
        k_all[1],
        k_all[2],
        k_all[3],
        v_all[0],
        v_all[1],
        v_all[2],
        v_all[3],
        o_all[0],
        o_all[1],
        o_all[2],
        o_all[3],
        g_all[0],
        g_all[1],
        g_all[2],
        g_all[3],
        u_all[0],
        u_all[1],
        u_all[2],
        u_all[3],
        d_all[0],
        d_all[1],
        d_all[2],
        d_all[3],
        n_all[0],
        n_all[1],
        n_all[2],
        n_all[3],
    )


def solution(mesh):
    in_specs = (
        P(("dp", "tensor"), None),
        P(("dp", "tensor"), None),
        P("dp", None),
        P("dp", "tensor"),
        P("dp", "tensor"),
        P("dp", "tensor"),
        P("dp", "tensor"),
        P("dp", "tensor"),
        P("dp", "tensor"),
        P("dp", "tensor"),
        P(None, "dp"),
        P("dp", "tensor"),
        P("dp", "tensor"),
        P("dp", "tensor"),
        P("dp", "tensor"),
        P("dp", "tensor"),
        P("dp", "tensor"),
        P("dp", "tensor"),
        P(None, "dp"),
        P("dp", "tensor"),
        P("dp", "tensor"),
        P("dp", "tensor"),
        P("dp", "tensor"),
        P("dp", "tensor"),
        P("dp", "tensor"),
        P("dp", "tensor"),
        P(None, "dp"),
    )
    out_specs = (
        P(("dp", "tensor"), None),
        P(("dp", "tensor"), None),
        P("dp", "tensor"),
        P("dp", "tensor"),
        P("dp", "tensor"),
        P("dp", "tensor"),
        P("dp", "tensor"),
        P("dp", "tensor"),
        P("dp", "tensor"),
        P("dp", "tensor"),
        P("dp", "tensor"),
        P("dp", "tensor"),
        P("dp", "tensor"),
        P("dp", "tensor"),
        P("dp", "tensor"),
        P("dp", "tensor"),
        P("dp", "tensor"),
        P("dp", "tensor"),
        P("dp", "tensor"),
        P("dp", "tensor"),
        P("dp", "tensor"),
        P("dp", "tensor"),
        P("dp", "tensor"),
        P("dp", "tensor"),
        P("dp", "tensor"),
        P("dp", "tensor"),
        P("dp", "tensor"),
        P("dp", "tensor"),
        P("dp", "tensor"),
        P("dp", "tensor"),
        P(None, "dp"),
        P(None, "dp"),
        P(None, "dp"),
        P(None, "dp"),
    )
    return jax.shard_map(shards, mesh=mesh, in_specs=in_specs, out_specs=out_specs, check_vma=False)
```

profile of v0, /device:TPU:0, one launch (start us, length us, event | category | flops | bytes accessed | tf_op | source)
XLA Modules:
  0.0 3047.2 jit_solution(13023432001376095793)
XLA Ops:
  10.4 42.2 %all_gather.36 = bf16[2,2048]{1,0:T(2,128)(2,1)S(1)} all-gather(bf16[2,128]{1,0:T(2,128)(2,1)S(1)} %convert_element_type.118), channel_id=1, replica_groups=mesh['dp'=16,'tensor'=2] {'dp'}, dimensions={1}, use_global_device_ids=true | all-gather | bytes 8704 | tf_op jit(solution)/shard_map/all_gather | solution.py:127
  59.5 42.4 %all_gather.38 = bf16[2048,128]{1,0:T(8,128)(2,1)} all-gather(bf16[128,128]{1,0:T(8,128)(2,1)S(1)} %convert_element_type.120), channel_id=1, replica_groups=mesh['dp'=16,'tensor'=2] {'dp'}, dimensions={0}, use_global_device_ids=true | all-gather | bytes 557056 | tf_op jit(solution)/shard_map/all_gather | solution.py:125
  101.9 46.4 %all_gather.39 = bf16[2048,128]{1,0:T(8,128)(2,1)} all-gather(bf16[128,128]{1,0:T(8,128)(2,1)S(1)} %convert_element_type.122), channel_id=1, replica_groups=mesh['dp'=16,'tensor'=2] {'dp'}, dimensions={0}, use_global_device_ids=true | all-gather | bytes 557056 | tf_op jit(solution)/shard_map/all_gather | solution.py:124
  160.6 8.3 fusion.107
  168.9 8.2 fusion.108
  177.1 9.1 fusion.9
  186.2 9.0 fusion.8
  195.3 9.1 fusion.44
  204.4 8.4 fusion.43
  213.0 16.3 all-gather.14.cloned.1.call-done
  229.2 7.6 fusion.111
  239.2 10.9 reduce-scatter.15.cloned.1.call-done
  260.0 137.0 %all-gather.20.cloned.1.call-done = bf16[2048,2816]{1,0:T(8,128)(2,1)} async-done(((bf16[128,2816]{1,0:T(8,128)(2,1)}), bf16[2048,2816]{1,0:T(8,128)(2,1)}) %all-gather.20.cloned.1.call-update) | async-done | bytes 11534352 | tf_op jit(solution)/shard_map/all_gather | solution.py:174
  397.0 12.4 all-gather.16.cloned.1.call-done
  409.4 16.1 fusion.113
  425.6 130.9 %all-gather.18.cloned.1.call-done = bf16[2048,2816]{1,0:T(8,128)(2,1)} async-done(((bf16[128,2816]{1,0:T(8,128)(2,1)}), bf16[2048,2816]{1,0:T(8,128)(2,1)}) %all-gather.18.cloned.1.call-update) | async-done | bytes 11534352 | tf_op jit(solution)/shard_map/all_gather | solution.py:173
  556.5 15.8 fusion.112
  572.3 143.2 %all-gather.22.cloned.1.call-done = bf16[2048,2816]{1,0:T(8,128)(2,1)} async-done(((bf16[128,2816]{1,0:T(8,128)(2,1)}), bf16[2048,2816]{1,0:T(8,128)(2,1)}) %all-gather.22.cloned.1.call-update) | async-done | bytes 11534352 | tf_op jit(solution)/shard_map/all_gather | solution.py:175
  715.5 22.6 multiply_convert_fusion
  738.1 13.6 fusion.114
  751.7 13.6 convolution_add_fusion
  765.4 14.4 convolution_convert_fusion
  782.5 10.6 reduce-scatter.17.cloned.1.call-done
  793.1 6.7 fusion.106
  800.5 12.7 all-gather.26.cloned.1.call-done
  813.2 6.6 convolution_convert_fusion.1
  820.8 8.1 fusion.69
  828.9 8.7 fusion.62
  837.6 30.2 fusion.45
  867.8 30.4 fusion.36
  898.2 8.1 fusion.68
  906.3 8.6 fusion.59
  914.9 26.6 fusion.46
  941.5 25.7 fusion.37
  984.7 9.8 reduce-scatter.21.cloned.1.call-done
  999.2 9.2 fusion.120
  1008.4 7.1 fusion.117
  1017.5 14.6 fusion.122
  1032.3 14.7 fusion.121
  1048.9 14.6 convolution_bitcast_fusion
  1063.6 13.2 reduce-scatter.27.cloned.1.call-done
  1078.3 75.8 %reduce-scatter.25.cloned.1.call-done = f32[128,128]{1,0:T(8,128)} async-done(((f32[2048,128]{1,0:T(8,128)}), f32[128,128]{1,0:T(8,128)}) %reduce-scatter.25.cloned.1.call-update) | async-done | bytes 65552 | tf_op jit(solution)/shard_map/reduce_scatter | solution.py:269
  1161.1 69.8 %reduce-scatter.37.cloned.1.call-done = f32[128,2]{1,0:T(8,128)} async-done(((f32[2048,2]{1,0:T(8,128)}), f32[128,2]{1,0:T(8,128)}) %reduce-scatter.37.cloned.1.call-update) | async-done | bytes 1040
  1234.9 173.3 %reduce-scatter.29.cloned.1.call-done = f32[128,1024]{1,0:T(8,128)} async-done(((f32[2048,1024]{1,0:T(8,128)}), f32[128,1024]{1,0:T(8,128)}) %reduce-scatter.29.cloned.1.call-update) | async-done | bytes 524304 | tf_op jit(solution)/shard_map/reduce_scatter | solution.py:271
  1410.8 180.5 %reduce-scatter.23.cloned.1.call-done = f32[128,1024]{1,0:T(8,128)} async-done(((f32[2048,1024]{1,0:T(8,128)}), f32[128,1024]{1,0:T(8,128)}) %reduce-scatter.23.cloned.1.call-update) | async-done | bytes 524304 | tf_op jit(solution)/shard_map/reduce_scatter | solution.py:268
  1594.1 475.6 %reduce-scatter.33.cloned.1.call-done = f32[128,2816]{1,0:T(8,128)} async-done(((f32[2048,2816]{1,0:T(8,128)}), f32[128,2816]{1,0:T(8,128)}) %reduce-scatter.33.cloned.1.call-update) | async-done | bytes 1441808 | tf_op jit(solution)/shard_map/reduce_scatter | solution.py:273
  2074.7 477.7 %reduce-scatter.31.cloned.1.call-done = f32[128,2816]{1,0:T(8,128)} async-done(((f32[2048,2816]{1,0:T(8,128)}), f32[128,2816]{1,0:T(8,128)}) %reduce-scatter.31.cloned.1.call-update) | async-done | bytes 1441808 | tf_op jit(solution)/shard_map/reduce_scatter | solution.py:272
  2557.3 477.9 %reduce-scatter.35.cloned.1.call-done = f32[128,2816]{1,0:T(8,128)} async-done(((f32[2048,2816]{1,0:T(8,128)}), f32[128,2816]{1,0:T(8,128)}) %reduce-scatter.35.cloned.1.call-update) | async-done | bytes 1441808 | tf_op jit(solution)/shard_map/reduce_scatter | solution.py:274
  (236 shorter events, 97.8 us)
Async XLA Ops:
  7.2 141.5 %all-gather.10.cloned.1.call-start = ((), (), s32[]{:S(2)}) async-start(), calls=%async_computation.12 | async-start | bytes 4718592 | tf_op jit(solution)/shard_map/all_gather | solution.py:134
  7.9 48.3 %copy-start.21 = (f32[128,1024]{1,0:T(8,128)S(1)}, f32[128,1024]{1,0:T(8,128)}, u32[]{:S(2)}) copy-start(f32[128,1024]{1,0:T(8,128)} %param.30) | copy-start | bytes 1572868
  9.8 47.3 %copy-start.19 = (f32[128,1024]{1,0:T(8,128)S(1)}, f32[128,1024]{1,0:T(8,128)}, u32[]{:S(2)}) copy-start(f32[128,1024]{1,0:T(8,128)} %param.33) | copy-start | bytes 1572868
  10.4 47.5 %copy-start.54 = (f32[384]{0:T(512)}, f32[384]{0:T(512)S(1)}, u32[]{:S(2)}) copy-start(f32[384]{0:T(512)S(1)} %get-tuple-element.83) | copy-start | bytes 4612
  56.2 97.8 %all-gather.12.cloned.1.call-start = ((), (), s32[]{:S(2)}) async-start(), calls=%async_computation.13 | async-start | bytes 4456448 | tf_op jit(solution)/shard_map/all_gather | solution.py:123
  57.0 172.2 %all-gather.14.cloned.1.call-start = ((), (), s32[]{:S(2)}) async-start(), calls=%async_computation.14 | async-start | bytes 4456448 | tf_op jit(solution)/shard_map/all_gather | solution.py:126
  57.9 192.2 %reduce-scatter.15.cloned.1.call-start = ((), (), s32[]{:S(2)}) async-start(), calls=%async_computation.15 | async-start | bytes 9437184 | tf_op jit(solution)/shard_map/reduce_scatter | solution.py:170
  152.2 16.7 copy-start.26
  152.2 16.7 copy-start.28
  168.9 26.4 copy-start.39
  213.0 23.9 copy-start.23
  236.9 160.2 %all-gather.20.cloned.1.call-start = ((), (), s32[]{:S(2)}) async-start(), calls=%async_computation.18 | async-start | bytes 12255232 | tf_op jit(solution)/shard_map/all_gather | solution.py:174
  239.1 170.3 %all-gather.16.cloned.1.call-start = ((), (), s32[]{:S(2)}) async-start(), calls=%async_computation.16 | async-start | bytes 4718592 | tf_op jit(solution)/shard_map/all_gather | solution.py:179
  254.5 302.0 %all-gather.18.cloned.1.call-start = ((), (), s32[]{:S(2)}) async-start(), calls=%async_computation.17 | async-start | bytes 12255232 | tf_op jit(solution)/shard_map/all_gather | solution.py:173
  256.8 315.5 %all-gather.24.cloned.1.call-start = ((), (), s32[]{:S(2)}) async-start(), calls=%async_computation.21 | async-start | bytes 4718592 | tf_op jit(solution)/shard_map/all_gather | solution.py:189
  257.6 457.9 %all-gather.22.cloned.1.call-start = ((), (), s32[]{:S(2)}) async-start(), calls=%async_computation.19 | async-start | bytes 12255232 | tf_op jit(solution)/shard_map/all_gather | solution.py:175
  260.0 519.9 %reduce-scatter.19.cloned.1.call-start = ((), (), s32[]{:S(2)}) async-start(), calls=%async_computation.22 | async-start | bytes 9437184 | tf_op jit(solution)/shard_map/reduce_scatter | solution.py:197
  738.1 13.6 copy-start.65
  765.3 27.8 reduce-scatter.17.cloned.1.call-start
  779.8 33.4 %all-gather.26.cloned.1.call-start = ((), (), s32[]{:S(2)}) async-start(), calls=%async_computation.23 | async-start | bytes 4718592 | tf_op jit(solution)/shard_map/all_gather | solution.py:201
  799.8 194.8 %reduce-scatter.21.cloned.1.call-start = ((), (), s32[]{:S(2)}) async-start(), calls=%async_computation.24 | async-start | bytes 9437184 | tf_op jit(solution)/shard_map/reduce_scatter | solution.py:254
  799.9 29.0 copy-start.43
  837.6 30.2 copy-start.27
  837.6 30.2 copy-start.29
  941.5 25.7 copy-start.25
  978.7 98.1 %reduce-scatter.27.cloned.1.call-start = ((), (), s32[]{:S(2)}) async-start(), calls=%async_computation.27 | async-start | bytes 1114112 | tf_op jit(solution)/shard_map/reduce_scatter | solution.py:270
  982.6 171.5 %reduce-scatter.25.cloned.1.call-start = ((), (), s32[]{:S(2)}) async-start(), calls=%async_computation.26 | async-start | bytes 1114112 | tf_op jit(solution)/shard_map/reduce_scatter | solution.py:269
  984.7 246.2 %reduce-scatter.37.cloned.1.call-start = ((), (), s32[]{:S(2)}) async-start(), calls=%async_computation.32 | async-start | bytes 1114112
  999.2 409.0 %reduce-scatter.29.cloned.1.call-start = ((), (), s32[]{:S(2)}) async-start(), calls=%async_computation.28 | async-start | bytes 8912896 | tf_op jit(solution)/shard_map/reduce_scatter | solution.py:271
  1008.4 582.9 %reduce-scatter.23.cloned.1.call-start = ((), (), s32[]{:S(2)}) async-start(), calls=%async_computation.25 | async-start | bytes 8912896 | tf_op jit(solution)/shard_map/reduce_scatter | solution.py:268
  1015.6 1054.1 %reduce-scatter.33.cloned.1.call-start = ((), (), s32[]{:S(2)}) async-start(), calls=%async_computation.30 | async-start | bytes 24510464 | tf_op jit(solution)/shard_map/reduce_scatter | solution.py:273
  1032.1 1520.3 %reduce-scatter.31.cloned.1.call-start = ((), (), s32[]{:S(2)}) async-start(), calls=%async_computation.29 | async-start | bytes 24510464 | tf_op jit(solution)/shard_map/reduce_scatter | solution.py:272
  1047.0 1988.2 %reduce-scatter.35.cloned.1.call-start = ((), (), s32[]{:S(2)}) async-start(), calls=%async_computation.31 | async-start | bytes 24510464 | tf_op jit(solution)/shard_map/reduce_scatter | solution.py:274
  1063.5 90.6 %copy-start.38 = (f32[128,128]{1,0:T(8,128)S(1)}, f32[128,128]{1,0:T(8,128)}, u32[]{:S(2)}) copy-start(f32[128,128]{1,0:T(8,128)} %param.31) | copy-start | bytes 196612
  1063.5 90.6 %copy-start.52 = (f32[128,128]{1,0:T(8,128)S(1)}, f32[128,128]{1,0:T(8,128)}, u32[]{:S(2)}) copy-start(f32[128,128]{1,0:T(8,128)} %param.47) | copy-start | bytes 196612
  1063.5 90.6 %copy-start.53 = (f32[128,128]{1,0:T(8,128)S(1)}, f32[128,128]{1,0:T(8,128)}, u32[]{:S(2)}) copy-start(f32[128,128]{1,0:T(8,128)} %param.39) | copy-start | bytes 196612
  1063.5 92.1 %copy-start.2 = (bf16[384,2048]{1,0:T(8,128)(2,1)S(1)}, bf16[384,2048]{1,0:T(8,128)(2,1)}, u32[]{:S(2)}) copy-start(bf16[384,2048]{1,0:T(8,128)(2,1)} %param.27) | copy-start | bytes 4718596
  1063.5 92.1 %copy-start.56 = (f32[384]{0:T(512)S(1)}, f32[384]{0:T(512)}, u32[]{:S(2)}) copy-start(f32[384]{0:T(512)} %get-tuple-element.82) | copy-start | bytes 4612
  1155.7 78.6 %copy-start.59 = (f32[2,128]{1,0:T(2,128)S(1)}, f32[2,128]{1,0:T(2,128)}, u32[]{:S(2)}) copy-start(f32[2,128]{1,0:T(2,128)} %param.37) | copy-start | bytes 3076
  1155.7 78.6 %copy-start.60 = (f32[2,128]{1,0:T(2,128)S(1)}, f32[2,128]{1,0:T(2,128)}, u32[]{:S(2)}) copy-start(f32[2,128]{1,0:T(2,128)} %param.53) | copy-start | bytes 3076
  1155.7 78.6 %copy-start.61 = (f32[2,128]{1,0:T(2,128)S(1)}, f32[2,128]{1,0:T(2,128)}, u32[]{:S(2)}) copy-start(f32[2,128]{1,0:T(2,128)} %param.45) | copy-start | bytes 3076
  1155.7 252.5 %copy-start.20 = (f32[128,1024]{1,0:T(8,128)S(1)}, f32[128,1024]{1,0:T(8,128)}, u32[]{:S(2)}) copy-start(f32[128,1024]{1,0:T(8,128)} %param.33) | copy-start | bytes 1572868
  1155.7 252.5 %copy-start.32 = (f32[128,1024]{1,0:T(8,128)S(1)}, f32[128,1024]{1,0:T(8,128)}, u32[]{:S(2)}) copy-start(f32[128,1024]{1,0:T(8,128)} %param.49) | copy-start | bytes 1572868
  1161.1 430.2 %copy-start.22 = (f32[128,1024]{1,0:T(8,128)S(1)}, f32[128,1024]{1,0:T(8,128)}, u32[]{:S(2)}) copy-start(f32[128,1024]{1,0:T(8,128)} %param.30) | copy-start | bytes 1572868
  1234.3 359.8 %copy-start.57 = (f32[2,128]{1,0:T(2,128)}, f32[2,128]{1,0:T(2,128)S(1)}, u32[]{:S(2)}) copy-start(f32[2,128]{1,0:T(2,128)S(1)} %psum.8) | copy-start | bytes 3076
  1234.9 834.8 %copy-start.8 = (f32[128,2816]{1,0:T(8,128)S(1)}, f32[128,2816]{1,0:T(8,128)}, u32[]{:S(2)}) copy-start(f32[128,2816]{1,0:T(8,128)} %param.35) | copy-start | bytes 4325380
  1594.1 958.3 %copy-start.9 = (f32[128,2816]{1,0:T(8,128)S(1)}, f32[128,2816]{1,0:T(8,128)}, u32[]{:S(2)}) copy-start(f32[128,2816]{1,0:T(8,128)} %param.34) | copy-start | bytes 4325380
  2074.7 960.5 %copy-start.10 = (f32[128,2816]{1,0:T(8,128)S(1)}, f32[128,2816]{1,0:T(8,128)}, u32[]{:S(2)}) copy-start(f32[128,2816]{1,0:T(8,128)} %param.36) | copy-start | bytes 4325380
  (39 other events, 221.2 us)
Sparse Core Ops, SparseCore 0:
  56.3 7.9 all-gather.9
  67.7 82.7 all-gather.11
  153.9 75.3 all-gather.13
  237.0 13.0 reduce-scatter.14
  253.7 143.3 all-gather.19
  399.1 10.3 all-gather.15
  413.1 143.3 all-gather.17
  558.1 10.3 all-gather.23
  572.1 143.3 all-gather.21
  765.4 12.6 reduce-scatter.18
  781.0 12.0 reduce-scatter.16
  799.9 13.2 all-gather.25
  978.8 15.6 reduce-scatter.20
  997.8 78.9 reduce-scatter.26
  1080.1 73.9 reduce-scatter.24
  1156.8 74.1 reduce-scatter.36
  1233.8 174.3 reduce-scatter.28
  1411.0 180.2 reduce-scatter.22
  1594.3 475.3 reduce-scatter.32
  2072.5 479.7 reduce-scatter.30
  2555.4 479.7 reduce-scatter.34
where the time goes:
time: 3060 us; the launch traced here: 3050 us
  waiting for transfers between devices  2430 us (79%)
  matrix products  374 us (12%)
  blocking collectives  133 us (4%)
  other arithmetic  81.7 us (3%)
    reduce_scatter x1, waiting for transfers between devices, shards(): lax.psum_scatter(down_grad_full, 'dp', scatter_dimension=0, tiled=True)  478 us
    reduce_scatter x1, waiting for transfers between devices, shards(): lax.psum_scatter(gate_grad_full, 'dp', scatter_dimension=0, tiled=True)  478 us
    reduce_scatter x1, waiting for transfers between devices, shards(): lax.psum_scatter(up_grad_full, 'dp', scatter_dimension=0, tiled=True)  476 us
    reduce_scatter x1, waiting for transfers between devices, shards(): lax.psum_scatter(query_grad_full, 'dp', scatter_dimension=0, tiled=True)  180 us
    reduce_scatter x1, waiting for transfers between devices, shards(): lax.psum_scatter(out_grad_full, 'dp', scatter_dimension=0, tiled=True)  173 us
    all_gather x1, waiting for transfers between devices, shards(): lax.all_gather(down_weight.astype(lowtype), 'dp', axis=0, tiled=True)  143 us
    all_gather x1, waiting for transfers between devices, shards(): lax.all_gather(up_weight.astype(lowtype), 'dp', axis=0, tiled=True)  137 us
    all_gather x1, waiting for transfers between devices, shards(): lax.all_gather(gate_weight.astype(lowtype), 'dp', axis=0, tiled=True)  131 us
  transfers between devices with their start and end apart: 21, of which 17 were waited for; matrix products, arithmetic and copies ran while one was open for 7% of the time, Pallas kernels for 0%

commit v1 on v0

v1 whole, which is shorter than its diff:
```python
import functools
import math

import jax
import jax.numpy as jnp
from jax import lax
from jax.experimental import pallas as pl
from jax.experimental.pallas import tpu as pltpu
from jax.sharding import PartitionSpec as P

HEAD = 64
STEP = 10


NORM_EPS = 1e-05
NEG_LARGE = -1000000000.0
BETA_FIRST = 0.9
BETA_SECOND = 0.95
ADAM_EPS = 1e-08
DECAY_RATE = 0.1
RATE_MAIN = 0.02
RATE_OUT = 0.15
RATE_DOWN = 0.015
RATE_GAINS = 0.6


def rope_tables(segment):
    length = segment.shape[0]
    order = jnp.arange(length, dtype=jnp.int32)
    before = jnp.sum((segment[None, :] < segment[:, None]).astype(jnp.int32), axis=1)
    place = (order - before).astype(jnp.float32)
    half = HEAD // 2
    freq = jnp.exp(jnp.arange(half, dtype=jnp.float32) * (-2.0 * math.log(10000.0) / HEAD))
    angle = place[:, None] * freq[None, :]
    cosine, sine = jnp.cos(angle), jnp.sin(angle)
    return (
        jnp.concatenate([cosine] * 4, axis=1),
        jnp.concatenate([-sine, sine, -sine, sine], axis=1),
    )


def norm_back(values, inverse, gain, upstream):
    weighted = gain * upstream
    grad_in = inverse * weighted - values * inverse**3 * jnp.mean(
        weighted * values, axis=1, keepdims=True
    )
    grad_gain = jnp.sum(upstream * values * inverse, axis=0)
    return (grad_in, grad_gain)


def contract_rows(left, right):
    return lax.dot_general(
        left, right, (((0,), (0,)), ((), ())), preferred_element_type=jnp.float32
    )


def contract_cols(left, right):
    return lax.dot_general(
        left, right, (((1,), (1,)), ((), ())), preferred_element_type=jnp.float32
    )


def adam(weight, grad, moment, square, rate, decay):
    moment_new = BETA_FIRST * moment + (1.0 - BETA_FIRST) * grad
    square_new = BETA_SECOND * square + (1.0 - BETA_SECOND) * grad * grad
    direction = (
        moment_new
        / (1.0 - BETA_FIRST**STEP)
        / (jnp.sqrt(square_new / (1.0 - BETA_SECOND**STEP)) + ADAM_EPS)
    )
    return (grad, moment_new, square_new, weight - rate * (direction + decay * weight))


LOW = jnp.bfloat16
PLANE = 4
LANES = 128
TILE = 256
VMEM_LIMIT = 48 * 1024 * 1024


def swap_cores(block):
    return lax.ppermute(block, "tensor", [(0, 1), (1, 0)])


def lane_of(shape):
    return lax.broadcasted_iota(jnp.int32, shape, len(shape) - 1)


def turn_heads(values, cosine, sine):
    first = lane_of(values.shape) % HEAD < HEAD // 2
    ahead = pltpu.roll(values, LANES - HEAD // 2, 1)
    behind = pltpu.roll(values, HEAD // 2, 1)
    return values * cosine + jnp.where(first, ahead, behind) * sine


def project_kernel(heads, normed_ref, weight_ref, cosine_ref, sine_ref, out_ref):
    part = jnp.dot(normed_ref[...], weight_ref[...], preferred_element_type=jnp.float32)
    cosine, sine = cosine_ref[...], sine_ref[...]
    step = pl.program_id(0)
    for at in range(0, part.shape[1], LANES):
        piece = part[:, at : at + LANES]
        turned = turn_heads(piece, cosine, sine)
        keep = step * part.shape[1] + at >= heads
        out_ref[:, at : at + LANES] = jnp.where(keep, piece, turned).astype(LOW)


def project(normed, weight, cosine, sine, turned):
    rows, depth = normed.shape
    columns = weight.shape[1]
    block = 2 * LANES
    return pl.pallas_call(
        functools.partial(project_kernel, turned),
        grid=(columns // block,),
        in_specs=[
            pl.BlockSpec((rows, depth), lambda i: (0, 0)),
            pl.BlockSpec((depth, block), lambda i: (0, i)),
            pl.BlockSpec((rows, LANES), lambda i: (0, 0)),
            pl.BlockSpec((rows, LANES), lambda i: (0, 0)),
        ],
        out_specs=pl.BlockSpec((rows, block), lambda i: (0, i)),
        out_shape=jax.ShapeDtypeStruct((rows, columns), LOW),
        compiler_params=pltpu.CompilerParams(vmem_limit_bytes=VMEM_LIMIT),
        cost_estimate=pl.CostEstimate(
            flops=2 * rows * depth * columns,
            bytes_accessed=2 * (rows * depth + depth * columns + rows * columns),
            transcendentals=0,
        ),
    )(normed, weight, cosine, sine)


def double(values, group):
    low_half = lane_of(values.shape) < HEAD
    other = pltpu.roll(values.astype(jnp.float32), HEAD, 1).astype(values.dtype)
    return jnp.where(low_half == (group == 0), values, other)


def set_bias(across_ref, down_ref, bias):
    rows = bias.shape[0]
    row = lax.broadcasted_iota(jnp.int32, (rows, rows), 0)
    column = lax.broadcasted_iota(jnp.int32, (rows, rows), 1)
    allowed = (down_ref[...] == across_ref[...]) & (column <= row)
    bias[...] = jnp.where(allowed, 0.0, NEG_LARGE)


def halves_of(block):
    low_half = lane_of(block.shape) < HEAD
    zero = jnp.zeros_like(block)
    return jnp.where(low_half, block, zero), jnp.where(low_half, zero, block)


def dot_last(left, right):
    return lax.dot_general(
        left, right, (((1,), (1,)), ((), ())), preferred_element_type=jnp.float32
    )


def dot_first(left, right):
    return lax.dot_general(
        left, right, (((0,), (0,)), ((), ())), preferred_element_type=jnp.float32
    )


def attend_kernel(
    per_group, query_ref, key_ref, value_ref, across_ref, down_ref, out_ref, total_ref, bias, keys, values
):
    step = pl.program_id(0)
    rows = query_ref.shape[0]

    @pl.when(step == 0)
    def _():
        set_bias(across_ref, down_ref, bias)
        total_ref[...] = jnp.zeros_like(total_ref)

    @pl.when(step % per_group == 0)
    def _():
        group = step // per_group
        keys[...] = double(key_ref[...], group)
        values[...] = double(value_ref[...], group)

    for start in range(0, rows, TILE):
        stop = start + TILE
        query = query_ref[start:stop, :] * jnp.asarray(HEAD**-0.5, LOW)
        key, value = keys[:stop, :], values[:stop, :]
        shade = bias[start:stop, :stop]
        outs = []
        lane = lane_of((TILE, LANES))
        totals = total_ref[start:stop, :]
        for side, part in enumerate(halves_of(query)):
            score = dot_last(part, key) + shade
            largest = jnp.max(score, axis=1, keepdims=True)
            expo = jnp.exp(score - largest)
            total = jnp.sum(expo, axis=1, keepdims=True)
            probs = (expo * (1.0 / total)).astype(LOW)
            outs.append(jnp.dot(probs, value, preferred_element_type=jnp.float32))
            totals = jnp.where(lane == 2 * step + side, largest + jnp.log(total), totals)
        total_ref[start:stop, :] = totals
        out_ref[start:stop, :] = jnp.where(lane < HEAD, outs[0], outs[1]).astype(LOW)


def attend(into, segment, query_cols):
    rows = into.shape[0]
    pairs = query_cols // LANES
    return pl.pallas_call(
        functools.partial(attend_kernel, pairs // 2),
        grid=(pairs,),
        in_specs=[
            pl.BlockSpec((rows, LANES), lambda i: (0, i)),
            pl.BlockSpec((rows, LANES), lambda i: (0, pairs)),
            pl.BlockSpec((rows, LANES), lambda i: (0, pairs + 1)),
            pl.BlockSpec((1, rows), lambda i: (0, 0)),
            pl.BlockSpec((rows, 1), lambda i: (0, 0)),
        ],
        out_specs=[
            pl.BlockSpec((rows, LANES), lambda i: (0, i)),
            pl.BlockSpec((rows, LANES), lambda i: (0, 0)),
        ],
        out_shape=[
            jax.ShapeDtypeStruct((rows, query_cols), LOW),
            jax.ShapeDtypeStruct((rows, LANES), jnp.float32),
        ],
        scratch_shapes=[
            pltpu.VMEM((rows, rows), jnp.float32),
            pltpu.VMEM((rows, LANES), LOW),
            pltpu.VMEM((rows, LANES), LOW),
        ],
        compiler_params=pltpu.CompilerParams(vmem_limit_bytes=VMEM_LIMIT),
        cost_estimate=pl.CostEstimate(
            flops=8 * rows * rows * query_cols,
            bytes_accessed=6 * rows * query_cols,
            transcendentals=rows * rows * query_cols // HEAD,
        ),
    )(into, into, into, segment[None, :], segment[:, None])


def attend_back_kernel(
    per_group,
    query_ref,
    key_ref,
    value_ref,
    upstream_ref,
    total_ref,
    cosine_ref,
    sine_ref,
    across_ref,
    down_ref,
    query_back_ref,
    rest_ref,
    bias,
    keys,
    values,
    key_sum,
    value_sum,
):
    step = pl.program_id(0)
    rows = query_ref.shape[0]
    group = step // per_group

    @pl.when(step == 0)
    def _():
        set_bias(across_ref, down_ref, bias)

    @pl.when(step % per_group == 0)
    def _():
        keys[...] = double(key_ref[...], group)
        values[...] = double(value_ref[...], group)
        key_sum[...] = jnp.zeros_like(key_sum)
        value_sum[...] = jnp.zeros_like(value_sum)

    scale = jnp.asarray(HEAD**-0.5, LOW)
    for start in range(0, rows, TILE):
        stop = start + TILE
        query = query_ref[start:stop, :] * scale
        upstream = upstream_ref[start:stop, :]
        key, value = keys[:stop, :], values[:stop, :]
        shade = bias[start:stop, :stop]
        lane = lane_of((TILE, LANES))
        backs = []
        key_part = value_part = None
        for side, (part, grad) in enumerate(zip(halves_of(query), halves_of(upstream))):
            log_total = jnp.sum(
                jnp.where(lane == 2 * step + side, total_ref[start:stop, :], 0.0),
                axis=1,
                keepdims=True,
            )
            probs = jnp.exp(dot_last(part, key) + shade - log_total)
            value_here = dot_first(probs.astype(LOW), grad)
            probs_grad = dot_last(grad, value)
            delta = jnp.sum(probs * probs_grad, axis=1, keepdims=True)
            score_grad = (probs * (probs_grad - delta)).astype(LOW)
            backs.append(jnp.dot(score_grad, key, preferred_element_type=jnp.float32))
            key_here = dot_first(score_grad, part)
            key_part = key_here if key_part is None else key_part + key_here
            value_part = value_here if value_part is None else value_part + value_here
        key_sum[:stop, :] += key_part
        value_sum[:stop, :] += value_part
        back = jnp.where(lane < HEAD, backs[0], backs[1]) * HEAD**-0.5
        back = turn_heads(back, cosine_ref[start:stop, :], -sine_ref[start:stop, :])
        query_back_ref[start:stop, :] = back.astype(LOW)

    @pl.when(step % per_group == per_group - 1)
    def _():
        key_back = key_sum[...] + pltpu.roll(key_sum[...], HEAD, 1)
        key_back = turn_heads(key_back, cosine_ref[...], -sine_ref[...]).astype(LOW)
        value_back = (value_sum[...] + pltpu.roll(value_sum[...], HEAD, 1)).astype(LOW)

        @pl.when(group == 0)
        def _():
            rest_ref[:, :LANES] = key_back
            rest_ref[:, LANES:] = value_back

        @pl.when(group == 1)
        def _():
            low_half = lane_of(key_back.shape) < HEAD
            rest_ref[:, :LANES] = jnp.where(low_half, rest_ref[:, :LANES], key_back)
            rest_ref[:, LANES:] = jnp.where(low_half, rest_ref[:, LANES:], value_back)


def attend_back(into, upstream, log_totals, cosine, sine, segment):
    rows, query_cols = upstream.shape
    pairs = query_cols // LANES
    whole = lambda width: pl.BlockSpec((rows, width), lambda i: (0, 0))
    return pl.pallas_call(
        functools.partial(attend_back_kernel, pairs // 2),
        grid=(pairs,),
        in_specs=[
            pl.BlockSpec((rows, LANES), lambda i: (0, i)),
            pl.BlockSpec((rows, LANES), lambda i: (0, pairs)),
            pl.BlockSpec((rows, LANES), lambda i: (0, pairs + 1)),
            pl.BlockSpec((rows, LANES), lambda i: (0, i)),
            whole(LANES),
            whole(LANES),
            whole(LANES),
            pl.BlockSpec((1, rows), lambda i: (0, 0)),
            whole(1),
        ],
        out_specs=[pl.BlockSpec((rows, LANES), lambda i: (0, i)), whole(2 * LANES)],
        out_shape=[
            jax.ShapeDtypeStruct((rows, query_cols), LOW),
            jax.ShapeDtypeStruct((rows, 2 * LANES), LOW),
        ],
        scratch_shapes=[
            pltpu.VMEM((rows, rows), jnp.float32),
            pltpu.VMEM((rows, LANES), LOW),
            pltpu.VMEM((rows, LANES), LOW),
            pltpu.VMEM((rows, LANES), jnp.float32),
            pltpu.VMEM((rows, LANES), jnp.float32),
        ],
        compiler_params=pltpu.CompilerParams(vmem_limit_bytes=VMEM_LIMIT),
        cost_estimate=pl.CostEstimate(
            flops=20 * rows * rows * query_cols,
            bytes_accessed=8 * rows * query_cols,
            transcendentals=rows * rows * query_cols // HEAD,
        ),
    )(into, into, into, upstream, log_totals, cosine, sine, segment[None, :], segment[:, None])
def nothing_kernel(*refs):
    del refs


def after(value, *earlier):
    place = pl.BlockSpec(memory_space=pl.ANY)
    return pl.pallas_call(
        nothing_kernel,
        in_specs=[place] * (1 + len(earlier)),
        out_specs=place,
        out_shape=jax.ShapeDtypeStruct(value.shape, value.dtype),
        input_output_aliases={0: 0},
        compiler_params=pltpu.CompilerParams(vmem_limit_bytes=1024 * 1024),
    )(value, *earlier)


def copy_kernel(plan, count, spots_ref, *refs):
    *blocks, sems = refs
    moves = plan(spots_ref, blocks[:count], blocks[count:])
    copies = [
        pltpu.make_async_copy(source, target, sems.at[at])
        for at, (source, target) in enumerate(moves)
    ]
    for copy in copies:
        copy.start()
    for copy in copies:
        copy.wait()


def assemble(plan, moves, spots, blocks, shapes):
    place = pl.BlockSpec(memory_space=pl.ANY)
    return pl.pallas_call(
        functools.partial(copy_kernel, plan, len(blocks)),
        in_specs=[pl.BlockSpec(memory_space=pltpu.SMEM)] + [place] * len(blocks),
        out_specs=[place] * len(shapes),
        out_shape=[jax.ShapeDtypeStruct(shape, LOW) for shape in shapes],
        scratch_shapes=[pltpu.SemaphoreType.DMA((moves,))],
        compiler_params=pltpu.CompilerParams(vmem_limit_bytes=1024 * 1024),
    )(spots, *blocks)


def wide(block):
    return block.astype(jnp.float32)


def low(block):
    return block.astype(LOW)


def order_cores(own, other, axis=0):
    return jnp.where(
        lax.axis_index("tensor") == 0,
        jnp.concatenate([own, other], axis=axis),
        jnp.concatenate([other, own], axis=axis),
    )


class Links:
    def __init__(self, devices):
        self.devices = devices
        self.planes = devices // PLANE
        self.pairs = {
            step: [(index, index ^ step) for index in range(devices)] for step in (1, 2, 3)
        }
        self.columns = [list(range(corner, devices, PLANE)) for corner in range(PLANE)]
        self.ring = [(index, (index + PLANE) % devices) for index in range(devices)]

    def swap(self, block, step):
        return lax.ppermute(block, "dp", self.pairs[step])

    def turn(self, block):
        return lax.ppermute(block, "dp", self.ring)

    def place(self):
        index = lax.axis_index("dp")
        return index // PLANE, index % PLANE

    def plane_gather(self, block):
        half = block.shape[0] // 2
        first = self.swap(block, 1)
        second = self.swap(block, 2)
        far = [self.swap(second[:half], 1), self.swap(first[half:], 2)]
        return [block, first, second, jnp.concatenate(far, axis=0)]

    def plane_sum(self, blocks):
        own, first, second, far = blocks
        half = own.shape[0] // 2
        far_one = self.swap(low(far[:half]), 1)
        far_two = self.swap(low(far[half:]), 2)
        send_one = jnp.concatenate(
            [low(first[:half]), low(wide(first[half:]) + wide(far_two))], axis=0
        )
        send_two = jnp.concatenate(
            [low(wide(second[:half]) + wide(far_one)), low(second[half:])], axis=0
        )
        return wide(own) + wide(self.swap(send_one, 1)) + wide(self.swap(send_two, 2))

    def ring_slots(self, block):
        slots = [block]
        for _ in range(self.planes - 1):
            slots.append(self.turn(slots[-1]))
        return slots

    def ring_sum(self, part_of):
        level, _ = self.place()
        total = part_of((level - 1) % self.planes)
        for step in range(1, self.planes):
            arrived = wide(self.turn(low(total)))
            total = arrived + part_of((level - 1 - step) % self.planes)
        return total

    def gather_rows(self, block, first, begin):
        level, corner = self.place()
        rows, columns = block.shape
        slots = self.ring_slots(block)
        group = max(1, self.planes // 2)
        pieces, spots = [], []
        for start in range(0, self.planes, group):
            bundle = jnp.concatenate(slots[start : start + group], axis=0)
            for other, piece in enumerate(self.plane_gather(after(bundle, begin))):
                pieces.append(piece.reshape(group, rows, columns))
                spots += [
                    ((level - start - step) % self.planes) * PLANE + (corner ^ other)
                    for step in range(group)
                ]
            begin = pieces[-1]

        def plan(spots_ref, sources, targets):
            moves = []
            for at, source in enumerate(sources):
                for step in range(group):
                    spot = spots_ref[at * group + step]
                    moves.append((source.at[step, :, :first], targets[0].at[spot]))
                    moves.append((source.at[step, :, first:], targets[1].at[spot]))
            return moves

        shapes = [(self.devices, rows, first), (self.devices, rows, columns - first)]
        whole = assemble(plan, 2 * len(spots), jnp.stack(spots), pieces, shapes)
        return [part.reshape(-1, part.shape[2]) for part in whole], begin

    def scatter_rows(self, part):
        _, corner = self.place()
        rows, columns = part.shape[0] // self.devices, part.shape[1]
        parts = part.reshape(self.planes, PLANE, rows, columns)
        sums = self.plane_sum(
            [
                lax.dynamic_index_in_dim(parts, corner ^ other, 1, False).reshape(-1, columns)
                for other in range(PLANE)
            ]
        )
        return self.ring_sum(lambda plane: lax.dynamic_slice_in_dim(sums, plane * rows, rows, 0))

    def spread_units(self, weights):
        core = lax.axis_index("tensor")
        _, corner = self.place()
        rows, columns = weights[0].shape
        wanted = columns // 2
        pieces = jnp.stack(
            [
                jnp.concatenate(
                    [low(weight[:, half * wanted : (half + 1) * wanted]) for weight in weights],
                    axis=1,
                )
                for half in range(2)
            ],
            axis=0,
        ).reshape(2, 2, rows // 2, wanted * len(weights))
        keep = lax.dynamic_index_in_dim(pieces, core, 1, False)
        give = lax.dynamic_index_in_dim(pieces, 1 - core, 1, False)
        quarters = order_cores(keep, swap_cores(give))
        arrived = []
        for other in range(PLANE):
            piece = lax.dynamic_slice_in_dim(quarters, corner ^ other, 1, 0)
            arrived.append(self.swap(piece, other) if other else piece)
        width = wanted

        def plan(spots_ref, sources, targets):
            return [
                (
                    source.at[0, :, at * width : (at + 1) * width],
                    targets[at].at[spots_ref[other]],
                )
                for other, source in enumerate(sources)
                for at in range(len(weights))
            ]

        spots = jnp.stack([corner ^ other for other in range(PLANE)])
        shape = (PLANE, rows // 2, width)
        return assemble(plan, PLANE * len(weights), spots, arrived, [shape] * len(weights))

    def gather_units(self, plane):
        core = lax.axis_index("tensor")
        _, rows, columns = plane.shape
        own = lax.all_gather(plane, "dp", axis=0, tiled=True, axis_index_groups=self.columns)

        def plan(spots_ref, sources, targets):
            return [(sources[at], targets[0].at[:, spots_ref[at]]) for at in range(2)]

        (whole,) = assemble(
            plan,
            2,
            jnp.stack([core, 1 - core]),
            [own, swap_cores(own)],
            [(self.devices, 2, rows, columns)],
        )
        return whole.reshape(-1, columns)

    def sum_units(self, part):
        core = lax.axis_index("tensor")
        rows, columns = part.shape[0] // self.devices // 2, part.shape[1]
        parts = part.reshape(self.devices, 2, rows, columns)
        keep = lax.dynamic_index_in_dim(parts, core, 1, False)
        give = low(lax.dynamic_index_in_dim(parts, 1 - core, 1, False))
        sums = low(wide(keep) + wide(swap_cores(give)))
        return lax.psum_scatter(
            sums, "dp", scatter_dimension=0, tiled=True, axis_index_groups=self.columns
        )

    def return_units(self, total):
        core = lax.axis_index("tensor")
        _, corner = self.place()
        _, rows, columns = total.shape
        quarters = jnp.zeros(total.shape, LOW)
        for other in range(PLANE):
            piece = lax.dynamic_slice_in_dim(total, corner ^ other, 1, 0)
            if other:
                piece = self.swap(piece, other)
            quarters = lax.dynamic_update_slice_in_dim(quarters, piece, corner ^ other, 0)
        keep = lax.dynamic_slice_in_dim(quarters, 2 * core, 2, 0)
        give = lax.dynamic_slice_in_dim(quarters, 2 - 2 * core, 2, 0)
        halves = order_cores(keep, swap_cores(give), axis=1)
        return wide(jnp.concatenate([halves[0], halves[1]], axis=1))

    def gather_gains(self, gains):
        level, corner = self.place()
        count, width = gains.shape
        pair = [gains, self.swap(gains, 1)]
        quad = jnp.stack(pair, axis=0)
        quad = jnp.concatenate([quad, self.swap(quad, 2)], axis=0)
        found = jnp.concatenate(self.ring_slots(quad), axis=0)
        found = found.reshape(self.devices, count * width)
        origin = jnp.arange(self.devices, dtype=jnp.int32)
        spot = ((level - origin // PLANE) % self.planes) * PLANE + ((origin % PLANE) ^ corner)
        choose = (spot[:, None] == origin[None, :]).astype(LOW)
        whole = jnp.dot(choose, found, preferred_element_type=jnp.float32)
        return jnp.swapaxes(whole.reshape(self.devices, count, width), 0, 1).reshape(count, -1)

    def sum_gains(self, part):
        total = part + swap_cores(part)
        total = total + self.swap(total, 1)
        total = total + self.swap(total, 2)
        slots = self.ring_slots(total)
        whole = slots[0]
        for slot in slots[1:]:
            whole = whole + slot
        width = whole.shape[1] // self.devices
        return lax.dynamic_slice(whole, (0, lax.axis_index("dp") * width), (part.shape[0], width))


def shards(
    links,
    tokens,
    cotangent,
    segments,
    query_weight,
    key_weight,
    value_weight,
    out_weight,
    gate_weight,
    up_weight,
    down_weight,
    norm_gains,
    query_moment,
    key_moment,
    value_moment,
    out_moment,
    gate_moment,
    up_moment,
    down_moment,
    gains_moment,
    query_square,
    key_square,
    value_square,
    out_square,
    gate_square,
    up_square,
    down_square,
    gains_square,
):
    lowtype = LOW
    core = lax.axis_index("tensor")
    rows = tokens.shape[0]
    seq_rows = 2 * rows

    def rows_of(values, which):
        return lax.dynamic_slice_in_dim(values, which * rows, rows, 0)

    def sum_plane_tokens(part):
        return links.plane_sum([part[rows * k : rows * (k + 1)] for k in range(PLANE)])

    gain_all = links.gather_gains(norm_gains.astype(lowtype))
    gain_one = gain_all[0]
    gain_two = gain_all[1]
    query_cols, key_cols = query_weight.shape[1], key_weight.shape[1]
    into_cols = query_cols + 2 * key_cols
    attn_weight = jnp.concatenate(
        [low(query_weight), low(key_weight), low(value_weight), low(out_weight)], axis=1
    )
    planes = links.spread_units([down_weight, gate_weight, up_weight])
    (into_all, out_all), gathered = links.gather_rows(attn_weight, into_cols, planes[0])
    down_all, gate_all, up_all = [links.gather_units(plane) for plane in planes]
    upstream = jnp.concatenate(links.plane_gather(after(cotangent, gathered)), axis=0)

    inputs = tokens.astype(jnp.float32)
    inverse_one = lax.rsqrt(jnp.mean(inputs * inputs, axis=1, keepdims=True) + NORM_EPS)
    normed_one = (inputs * inverse_one * gain_one).astype(lowtype)
    normed_one_all = order_cores(normed_one, swap_cores(normed_one))
    segment = segments[0]
    cosine, sine = rope_tables(segment)
    into = project(normed_one_all, into_all, cosine, sine, query_cols + key_cols)
    attended, log_totals = attend(into, segment, query_cols)
    attn_other = contract_cols(rows_of(attended, 1 - core), out_all).astype(lowtype)
    attn_own = contract_cols(rows_of(attended, core), out_all)
    hidden_state = inputs + (attn_own + swap_cores(attn_other).astype(jnp.float32))

    inverse_two = lax.rsqrt(jnp.mean(hidden_state * hidden_state, axis=1, keepdims=True) + NORM_EPS)
    normed_two = (hidden_state * inverse_two * gain_two).astype(lowtype)
    normed = jnp.concatenate(links.plane_gather(normed_two), axis=0)
    gate = jnp.dot(normed, gate_all, preferred_element_type=jnp.float32)
    upper = jnp.dot(normed, up_all, preferred_element_type=jnp.float32)
    grad_inner = jnp.dot(upstream, down_all, preferred_element_type=jnp.float32)
    sigma = jax.nn.sigmoid(gate)
    inner = low(gate * sigma * upper)
    grad_gate = low(grad_inner * upper * sigma * (1.0 + gate * (1.0 - sigma)))
    grad_upper = low(grad_inner * gate * sigma)
    grad_normed_two = sum_plane_tokens(
        contract_cols(grad_gate, gate_all) + contract_cols(grad_upper, up_all)
    )
    down_sum = links.sum_units(contract_rows(upstream, inner))
    gate_sum = links.sum_units(contract_rows(normed, grad_gate))
    up_sum = links.sum_units(contract_rows(normed, grad_upper))
    ffn_sum = sum_plane_tokens(after(contract_cols(inner, down_all), grad_normed_two))
    activations = (hidden_state + ffn_sum).astype(lowtype)
    down_shard = links.return_units(down_sum)
    gate_shard = links.return_units(gate_sum)
    up_shard = links.return_units(up_sum)

    hidden_back, gain_two_grad = norm_back(hidden_state, inverse_two, gain_two, grad_normed_two)
    hidden_grad = cotangent.astype(jnp.float32) + hidden_back
    attn_grad_low = hidden_grad.astype(lowtype)
    attn_grad_all = order_cores(attn_grad_low, swap_cores(attn_grad_low))
    attended_grad = jnp.dot(attn_grad_all, out_all, preferred_element_type=jnp.float32).astype(
        lowtype
    )
    out_grad_full = contract_rows(attn_grad_all, attended)
    out_shard = links.scatter_rows(after(out_grad_full, ffn_sum))
    into_back = jnp.concatenate(
        attend_back(into, attended_grad, log_totals, cosine, sine, segment), axis=1
    )
    into_shard = links.scatter_rows(contract_rows(normed_one_all, into_back))
    query_shard = into_shard[:, :query_cols]
    key_shard = into_shard[:, query_cols : query_cols + key_cols]
    value_shard = into_shard[:, query_cols + key_cols :]
    normed_other = contract_cols(rows_of(into_back, 1 - core), into_all).astype(lowtype)
    normed_own = contract_cols(rows_of(into_back, core), into_all)
    grad_normed_one = normed_own + swap_cores(normed_other).astype(jnp.float32)
    input_back, gain_one_grad = norm_back(inputs, inverse_one, gain_one, grad_normed_one)
    input_grad = hidden_grad + input_back
    gains_shard = links.sum_gains(jnp.stack([gain_one_grad, gain_two_grad], axis=0))
    q_all = adam(query_weight, query_shard, query_moment, query_square, RATE_MAIN, DECAY_RATE)
    k_all = adam(key_weight, key_shard, key_moment, key_square, RATE_MAIN, DECAY_RATE)
    v_all = adam(value_weight, value_shard, value_moment, value_square, RATE_MAIN, DECAY_RATE)
    o_all = adam(out_weight, out_shard, out_moment, out_square, RATE_OUT, DECAY_RATE)
    g_all = adam(gate_weight, gate_shard, gate_moment, gate_square, RATE_MAIN, DECAY_RATE)
    u_all = adam(up_weight, up_shard, up_moment, up_square, RATE_MAIN, DECAY_RATE)
    d_all = adam(down_weight, down_shard, down_moment, down_square, RATE_DOWN, DECAY_RATE)
    n_all = adam(norm_gains, gains_shard, gains_moment, gains_square, RATE_GAINS, 0.0)
    return (
        activations,
        input_grad,
        q_all[0],
        q_all[1],
        q_all[2],
        q_all[3],
        k_all[0],
        k_all[1],
        k_all[2],
        k_all[3],
        v_all[0],
        v_all[1],
        v_all[2],
        v_all[3],
        o_all[0],
        o_all[1],
        o_all[2],
        o_all[3],
        g_all[0],
        g_all[1],
        g_all[2],
        g_all[3],
        u_all[0],
        u_all[1],
        u_all[2],
        u_all[3],
        d_all[0],
        d_all[1],
        d_all[2],
        d_all[3],
        n_all[0],
        n_all[1],
        n_all[2],
        n_all[3],
    )


def solution(mesh):
    in_specs = (
        P(("dp", "tensor"), None),
        P(("dp", "tensor"), None),
        P("dp", None),
        P("dp", "tensor"),
        P("dp", "tensor"),
        P("dp", "tensor"),
        P("dp", "tensor"),
        P("dp", "tensor"),
        P("dp", "tensor"),
        P("dp", "tensor"),
        P(None, "dp"),
        P("dp", "tensor"),
        P("dp", "tensor"),
        P("dp", "tensor"),
        P("dp", "tensor"),
        P("dp", "tensor"),
        P("dp", "tensor"),
        P("dp", "tensor"),
        P(None, "dp"),
        P("dp", "tensor"),
        P("dp", "tensor"),
        P("dp", "tensor"),
        P("dp", "tensor"),
        P("dp", "tensor"),
        P("dp", "tensor"),
        P("dp", "tensor"),
        P(None, "dp"),
    )
    out_specs = (
        P(("dp", "tensor"), None),
        P(("dp", "tensor"), None),
        P("dp", "tensor"),
        P("dp", "tensor"),
        P("dp", "tensor"),
        P("dp", "tensor"),
        P("dp", "tensor"),
        P("dp", "tensor"),
        P("dp", "tensor"),
        P("dp", "tensor"),
        P("dp", "tensor"),
        P("dp", "tensor"),
        P("dp", "tensor"),
        P("dp", "tensor"),
        P("dp", "tensor"),
        P("dp", "tensor"),
        P("dp", "tensor"),
        P("dp", "tensor"),
        P("dp", "tensor"),
        P("dp", "tensor"),
        P("dp", "tensor"),
        P("dp", "tensor"),
        P("dp", "tensor"),
        P("dp", "tensor"),
        P("dp", "tensor"),
        P("dp", "tensor"),
        P("dp", "tensor"),
        P("dp", "tensor"),
        P("dp", "tensor"),
        P("dp", "tensor"),
        P(None, "dp"),
        P(None, "dp"),
        P(None, "dp"),
        P(None, "dp"),
    )
    links = Links(mesh.shape["dp"])
    return jax.shard_map(functools.partial(shards, links), mesh=mesh, in_specs=in_specs, out_specs=out_specs, check_vma=False)
```

time: 3060 us -> 855 us (0.28)
  waiting for transfers between devices: 2430 us -> 298 us
  matrix products: 374 us -> 171 us
  blocking collectives: 133 us -> 0 us
  starting transfers between devices: 1.25 us -> 91.7 us
  local copies, waits for them, and re-layouts: 13.3 us -> 100 us
  Pallas kernels: 0 us -> 79.2 us
    reduce_scatter x11 -> x3, waiting for transfers between devices: 1910 us -> 0.02 us  [sum_units(): lax.psum_scatter(sums, 'dp', scatter_dimension=0, tiled=True, axis_index_...]
    all_gather x9 -> x3, waiting for transfers between devices: 453 us -> 0.01 us  [gather_units(): lax.all_gather(plane, 'dp', axis=0, tiled=True, axis_index_groups=self.co...]
    ppermute x0 -> x78, waiting for transfers between devices: none -> 298 us  [the longest x48 232 us: swap(): return lax.ppermute(block, 'dp', self.pairs[step])]
    dot_general x18 -> x4, matrix products: 246 us -> 49.6 us  [the longest x1 21.4 us: shards(): gate = jnp.dot(normed, gate_all, preferred_element_type=jnp.float32)]
    all_gather x3 -> x0, blocking collectives: 131 us -> none  [the longest x1 46.4 us: shards(): lax.all_gather(key_weight.astype(lowtype), 'dp', axis=0, tiled=True)]
    ppermute x0 -> x78, starting transfers between devices: none -> 90.6 us  [the longest x48 56.6 us: swap(): return lax.ppermute(block, 'dp', self.pairs[step])]
    pallas_call x0 -> x13, Pallas kernels: none -> 79.2 us  [the longest x1 37.7 us: attend_back(): pl.pallas_call(functools.partial(attend_back_kernel, pairs // 2), grid=(p...]
    unnamed x22 -> x6, waiting for transfers between devices: 70.8 us -> 0.1 us
  transfers between devices with their start and end apart: 21 -> 84, of which waited for: 17 -> 34; matrix products, arithmetic and copies ran while one was open for 7% -> 31% of each run, Pallas kernels for 0% -> 9%
where the time goes in v1:
time: 855 us; the launch traced here: 844 us
  waiting for transfers between devices  298 us (35%)
  matrix products  171 us (20%)
  local copies, waits for them, and re-layouts  100 us (12%)
  starting transfers between devices  91.7 us (11%)
  other arithmetic  87.6 us (10%)
  Pallas kernels  79.2 us (9%)
  between operations  16.3 us (2%)
    ppermute x48, waiting for transfers between devices, swap(): return lax.ppermute(block, 'dp', self.pairs[step])  232 us
    dot_general x7, matrix products, contract_cols(): lax.dot_general(left, right, (((1,), (1,)), ((), ())), preferred_element_...  64.1 us
    ppermute x15, waiting for transfers between devices, turn(): return lax.ppermute(block, 'dp', self.ring)  63 us
    ppermute x48, starting transfers between devices, swap(): return lax.ppermute(block, 'dp', self.pairs[step])  56.6 us
    unnamed x215, local copies, waits for them, and re-layouts  51.7 us
    dot_general x5, matrix products, contract_rows(): lax.dot_general(left, right, (((0,), (0,)), ((), ())), preferred_element_...  50.3 us
    pallas_call x1, Pallas kernels, attend_back(): pl.pallas_call(functools.partial(attend_back_kernel, pairs // 2), grid=(p...  37.7 us
    ppermute x15, starting transfers between devices, turn(): return lax.ppermute(block, 'dp', self.ring)  31.7 us
  transfers between devices with their start and end apart: 84, of which 34 were waited for; matrix products, arithmetic and copies ran while one was open for 31% of the time, Pallas kernels for 9%

profile of v1, /device:TPU:0, one launch (start us, length us, event | category | flops | bytes accessed | tf_op | source)
XLA Modules:
  0.0 843.6 jit_solution(14100693023954254944)
XLA Ops:
  18.8 11.4 %collective-permute-done.8.refs_1_ = bf16[1,64,4224]{2,1,0:T(8,128)(2,1)S(1)} collective-permute-done((bf16[1,64,4224]{2,1,0:T(8,128)(2,1)S(1)}, bf16[1,64,4224]{2,1,0:T(8,128)(2,1)S(1)}, u32[]{:S(2)}, u32[]{:S(2)}) %collective-permute-start.8) | collective-permute-done | bytes 540704 | tf_op jit(solution)/shard_map/ppermute | solution.py:423
  30.2 12.6 %collective-permute-done.9.refs_2_ = bf16[1,64,4224]{2,1,0:T(8,128)(2,1)S(1)} collective-permute-done((bf16[1,64,4224]{2,1,0:T(8,128)(2,1)S(1)}, bf16[1,64,4224]{2,1,0:T(8,128)(2,1)S(1)}, u32[]{:S(2)}, u32[]{:S(2)}) %collective-permute-start.9) | collective-permute-done | bytes 540704 | tf_op jit(solution)/shard_map/ppermute | solution.py:423
  52.4 14.9 %collective-permute-done.6 = bf16[128,2304]{1,0:T(8,128)(2,1)} collective-permute-done((bf16[128,2304]{1,0:T(8,128)(2,1)S(1)}, bf16[128,2304]{1,0:T(8,128)(2,1)}, u32[]{:S(2)}, u32[]{:S(2)}) %collective-permute-start.6) | collective-permute-done | bytes 589856 | tf_op jit(solution)/shard_map/ppermute | solution.py:426
  70.6 5.6 collective-permute-start.2
  82.9 21.4 %collective-permute-done.3 = bf16[4,2,128]{2,1,0:T(2,128)(2,1)S(1)} collective-permute-done((bf16[4,2,128]{2,1,0:T(2,128)(2,1)S(1)}, bf16[4,2,128]{2,1,0:T(2,128)(2,1)S(1)}, u32[]{:S(2)}, u32[]{:S(2)}) %collective-permute-start.3) | collective-permute-done | bytes 2080 | tf_op jit(solution)/shard_map/ppermute | solution.py:426
  104.3 15.6 %collective-permute-start.4 = (bf16[4,2,128]{2,1,0:T(2,128)(2,1)S(1)}, bf16[4,2,128]{2,1,0:T(2,128)(2,1)S(1)}, u32[]{:S(2)}, u32[]{:S(2)}) collective-permute-start(bf16[4,2,128]{2,1,0:T(2,128)(2,1)S(1)} %collective-permute-done.3), channel_id=1, source_target_pairs={{0,8},{2,10},{4,12},{6,14},{8,16},{10,18},{12,20},{14,22},{16,24},... | collective-permute-start | bytes 6152 | tf_op jit(solution)/shard_map/ppermute | solution.py:426
  138.9 3.7 collective-permute-done.13
  149.5 18.2 %collective-permute-done.17 = bf16[256,2304]{1,0:T(8,128)(2,1)} collective-permute-done((bf16[256,2304]{1,0:T(8,128)(2,1)S(1)}, bf16[256,2304]{1,0:T(8,128)(2,1)}, u32[]{:S(2)}, u32[]{:S(2)}) %collective-permute-start.17) | collective-permute-done | bytes 1179680 | tf_op jit(solution)/shard_map/ppermute | solution.py:423
  174.6 3.7 maximum_select_fusion.normed_ref
  190.4 7.7 shard_map.526.query_ref.key_ref.value_ref
  198.1 24.7 %shard_map.527 = (bf16[768,1024]{1,0:T(8,128)(2,1)S(1)}, f32[768,128]{1,0:T(8,128)S(1)}) custom-call(bf16[768,1280]{1,0:T(8,128)(2,1)S(1)} %shard_map.526.query_ref.key_ref.value_ref, bf16[768,1280]{1,0:T(8,128)(2,1)S(1)} %shard_map.526.query_ref.key_ref.value_ref, bf16[768,1280]{1,0:T(8,128)(2,1)S(1)} %shard_map.526.query_ref.key_ref.value_ref, ...), custom_call_target="tpu_custom_call" | custom-call | flops 4831838208 | bytes 4718592 | tf_op jit(solution)/shard_map/pallas_call | solution.py:203
  230.5 6.1 multiply_reduce_fusion.2
  241.1 24.6 %collective-permute-done.30 = bf16[384,2048]{1,0:T(8,128)(2,1)} collective-permute-done((bf16[384,2048]{1,0:T(8,128)(2,1)S(1)}, bf16[384,2048]{1,0:T(8,128)(2,1)}, u32[]{:S(2)}, u32[]{:S(2)}) %collective-permute-start.30) | collective-permute-done | bytes 1572896 | tf_op jit(solution)/shard_map/ppermute | solution.py:423
  278.0 37.0 %collective-permute-done.31 = bf16[192,2048]{1,0:T(8,128)(2,1)} collective-permute-done((bf16[192,2048]{1,0:T(8,128)(2,1)S(1)}, bf16[192,2048]{1,0:T(8,128)(2,1)}, u32[]{:S(2)}, u32[]{:S(2)}) %collective-permute-start.31) | collective-permute-done | bytes 786464 | tf_op jit(solution)/shard_map/ppermute | solution.py:423
  333.3 15.1 %fusion.87 = f32[1536,1408]{1,0:T(8,128)} fusion(bf16[1536,2048]{1,0:T(8,128)(2,1)} %constant_dynamic-update-slice_fusion.5, bf16[2048,1408]{1,0:T(8,128)(2,1)S(1)} %bitcast.210), kind=kOutput, calls=%fused_computation.275 | convolution fusion | flops 8858370048 | bytes 20709376 | tf_op jit(solution)/shard_map/dot_general | solution.py:685
  356.5 12.1 %fusion.85 = f32[1536,1408]{1,0:T(8,128)} fusion(bf16[1536,2048]{1,0:T(8,128)(2,1)S(1)} %constant_dynamic-update-slice_fusion, bf16[2048,1408]{1,0:T(8,128)(2,1)S(1)} %bitcast.216), kind=kOutput, calls=%fused_computation.273 | convolution fusion | flops 8858370048 | bytes 20709376 | tf_op jit(solution)/shard_map/dot_general | solution.py:684
  368.6 21.4 %multiply_convert_fusion.1 = (bf16[1536,1408]{1,0:T(8,128)(2,1)}, bf16[1536,1408]{1,0:T(8,128)(2,1)}, bf16[1536,1408]{1,0:T(8,128)(2,1)}) fusion(f32[1536,1408]{1,0:T(8,128)} %fusion.87, f32[1536,1408]{1,0:T(8,128)} %fusion.85, bf16[1536,2048]{1,0:T(8,128)(2,1)} %copy-done.64, bf16[2048,1408]{1,0:T(8,128)(2,1)S(1)} %bitcast.214), kind=kOutput, calls=%fused_computation.1 | convolution fusion | flops 8892973056 | bytes 42336256 | tf_op jit(solution)/shard_map/dot_general | solution.py:683
  390.0 16.5 %fusion.88 = f32[1536,2048]{1,0:T(8,128)} fusion(bf16[1536,1408]{1,0:T(8,128)(2,1)} %get-tuple-element.97, bf16[2048,1408]{1,0:T(8,128)(2,1)} %bitcast.217), kind=kOutput, calls=%fused_computation.276 | convolution fusion | flops 8858370048 | bytes 22675456 | tf_op jit(solution)/shard_map/dot_general | solution.py:58
  406.5 10.2 %fusion.90 = f32[2048,1408]{1,0:T(8,128)S(1)} fusion(bf16[1536,2048]{1,0:T(8,128)(2,1)S(1)} %copy-done.65, bf16[1536,1408]{1,0:T(8,128)(2,1)S(1)} %copy-done.93), kind=kOutput, calls=%fused_computation.278 | convolution fusion | flops 8858370048 | bytes 22151168 | tf_op jit(solution)/shard_map/dot_general | solution.py:52
  416.6 4.3 copy-done.40
  423.0 19.0 %fusion.84 = (bf16[1536,2048]{1,0:T(8,128)(2,1)}, f32[1536,2048]{1,0:T(8,128)}) fusion(f32[1536,2048]{1,0:T(8,128)} %fusion.88, bf16[1536,1408]{1,0:T(8,128)(2,1)} %get-tuple-element.95, bf16[2048,1408]{1,0:T(8,128)(2,1)} %bitcast.215), kind=kOutput, calls=%fused_computation.272 | convolution fusion | flops 8864661504 | bytes 41549824 | tf_op jit(solution)/shard_map/dot_general | solution.py:58
  446.1 5.8 fusion.2
  452.0 13.4 %fusion.91 = f32[2048,1408]{1,0:T(8,128)S(1)} fusion(bf16[1536,2048]{1,0:T(8,128)(2,1)} %copy-done.64, bf16[1536,1408]{1,0:T(8,128)(2,1)} %get-tuple-element.97), kind=kOutput, calls=%fused_computation.279 | convolution fusion | flops 8858370048 | bytes 22151168 | tf_op jit(solution)/shard_map/dot_general | solution.py:52
  465.5 4.3 copy-done.39
  479.9 11.9 %fusion.86.refs_0_ = f32[1536,2048]{1,0:T(8,128)S(1)} fusion(bf16[1536,1408]{1,0:T(8,128)(2,1)} %get-tuple-element.96, bf16[2048,1408]{1,0:T(8,128)(2,1)S(1)} %bitcast.213), kind=kOutput, calls=%fused_computation.274 | convolution fusion | flops 8858370048 | bytes 22675456 | tf_op jit(solution)/shard_map/dot_general | solution.py:58
  491.8 20.8 %collective-permute-done.36 = bf16[384,2048]{1,0:T(8,128)(2,1)} collective-permute-done((bf16[384,2048]{1,0:T(8,128)(2,1)S(1)}, bf16[384,2048]{1,0:T(8,128)(2,1)}, u32[]{:S(2)}, u32[]{:S(2)}) %collective-permute-start.36) | collective-permute-done | bytes 1572896 | tf_op jit(solution)/shard_map/ppermute | solution.py:423
  515.0 4.6 multiply_reduce_fusion
  519.6 4.5 copy-done
  524.1 8.2 convert.48
  538.0 5.9 fusion.1
  544.1 11.0 %collective-permute-done.37 = bf16[192,2048]{1,0:T(8,128)(2,1)} collective-permute-done((bf16[192,2048]{1,0:T(8,128)(2,1)}, bf16[192,2048]{1,0:T(8,128)(2,1)}, u32[]{:S(2)}, u32[]{:S(2)}) %collective-permute-start.37) | collective-permute-done | bytes 786464 | tf_op jit(solution)/shard_map/ppermute | solution.py:423
  561.9 13.7 %fusion.92 = f32[2048,1408]{1,0:T(8,128)S(1)} fusion(bf16[1536,2048]{1,0:T(8,128)(2,1)} %constant_dynamic-update-slice_fusion.5, bf16[1536,1408]{1,0:T(8,128)(2,1)} %get-tuple-element.96), kind=kOutput, calls=%fused_computation.280 | convolution fusion | flops 8858370048 | bytes 22151168 | tf_op jit(solution)/shard_map/dot_general | solution.py:52
  577.8 15.6 %collective-permute-done.40 = bf16[384,2048]{1,0:T(8,128)(2,1)S(1)} collective-permute-done((bf16[384,2048]{1,0:T(8,128)(2,1)S(1)}, bf16[384,2048]{1,0:T(8,128)(2,1)S(1)}, u32[]{:S(2)}, u32[]{:S(2)}) %collective-permute-start.40) | collective-permute-done | bytes 1572896 | tf_op jit(solution)/shard_map/ppermute | solution.py:423
  594.5 6.0 fusion.74
  600.5 5.9 fusion
  606.5 6.7 convolution_convert_fusion.2.upstream_ref
  613.3 37.7 %shard_map.533 = (bf16[768,1024]{1,0:T(8,128)(2,1)S(1)}, bf16[768,256]{1,0:T(8,128)(2,1)S(1)}) custom-call(bf16[768,1280]{1,0:T(8,128)(2,1)} %copy-done.27, bf16[768,1280]{1,0:T(8,128)(2,1)} %copy-done.27, bf16[768,1280]{1,0:T(8,128)(2,1)} %copy-done.27, bf16[768,1024]{1,0:T(8,128)(2,1)S(1)} %convolution_convert_fusion.2.upstream_ref, ...), custom_call_target="tpu_custom_call" | custom-call | flops 12079595520 | bytes 6291456 | tf_op jit(solution)/shard_map/pallas_call | solution.py:322
  654.7 7.2 fusion.89
  667.7 5.8 fusion.38.refs_0_
  681.2 8.5 %collective-permute-done.52 = bf16[256,1024]{1,0:T(8,128)(2,1)S(1)} collective-permute-done((bf16[256,1024]{1,0:T(8,128)(2,1)S(1)}, bf16[256,1024]{1,0:T(8,128)(2,1)S(1)}, u32[]{:S(2)}, u32[]{:S(2)}) %collective-permute-start.52) | collective-permute-done | bytes 524320 | tf_op jit(solution)/shard_map/ppermute | solution.py:423
  691.2 14.8 %collective-permute-done.50 = bf16[256,1024]{1,0:T(8,128)(2,1)S(1)} collective-permute-done((bf16[256,1024]{1,0:T(8,128)(2,1)S(1)}, bf16[256,1024]{1,0:T(8,128)(2,1)S(1)}, u32[]{:S(2)}, u32[]{:S(2)}) %collective-permute-start.50) | collective-permute-done | bytes 524320 | tf_op jit(solution)/shard_map/ppermute | solution.py:423
  709.7 4.1 fusion.11
  716.2 12.2 %collective-permute-done.53 = bf16[512,1024]{1,0:T(8,128)(2,1)S(1)} collective-permute-done((bf16[512,1024]{1,0:T(8,128)(2,1)S(1)}, bf16[512,1024]{1,0:T(8,128)(2,1)S(1)}, u32[]{:S(2)}, u32[]{:S(2)}) %collective-permute-start.53) | collective-permute-done | bytes 1048608 | tf_op jit(solution)/shard_map/ppermute | solution.py:423
  728.4 3.9 collective-permute-done.51
  733.0 24.0 %collective-permute-done.73 = f32[2,2048]{1,0:T(2,128)S(1)} collective-permute-done((f32[2,2048]{1,0:T(2,128)S(1)}, f32[2,2048]{1,0:T(2,128)S(1)}, u32[]{:S(2)}, u32[]{:S(2)}) %collective-permute-start.73) | collective-permute-done | bytes 16416 | tf_op jit(solution)/shard_map/ppermute | solution.py:423
  762.3 4.1 collective-permute-done.75
  778.3 3.9 collective-permute-done.55
  783.0 6.3 collective-permute-done.47
  (510 shorter events, 250.8 us)
Async XLA Ops:
  7.2 223.2 %all-gather.8.cloned.1.call-start = ((), (), s32[]{:S(2)}) async-start(), calls=%async_computation.5 | async-start | bytes 3604480 | tf_op jit(solution)/shard_map/all_gather | solution.py:548
  17.2 25.6 %collective-permute-start.9 = (bf16[1,64,4224]{2,1,0:T(8,128)(2,1)S(1)}, bf16[1,64,4224]{2,1,0:T(8,128)(2,1)S(1)}, u32[]{:S(2)}, u32[]{:S(2)}) collective-permute-start(bf16[1,64,4224]{2,1,0:T(8,128)(2,1)S(1)} %get-tuple-element.121), channel_id=1, source_target_pairs={{0,4},{2,6},{4,0},{6,2},{8,12},{10,14},{12,8},{14,10},{16,20},{18,... | collective-permute-start | bytes 1622024 | tf_op jit(solution)/shard_map/ppermute | solution.py:423
  18.7 24.1 %collective-permute-start.10 = (bf16[1,64,4224]{2,1,0:T(8,128)(2,1)S(1)}, bf16[1,64,4224]{2,1,0:T(8,128)(2,1)S(1)}, u32[]{:S(2)}, u32[]{:S(2)}) collective-permute-start(bf16[1,64,4224]{2,1,0:T(8,128)(2,1)S(1)} %get-tuple-element.120), channel_id=1, source_target_pairs={{0,6},{2,4},{4,2},{6,0},{8,14},{10,12},{12,10},{14,8},{16,22},{18,... | collective-permute-start | bytes 1622024 | tf_op jit(solution)/shard_map/ppermute | solution.py:423
  45.4 232.6 %all-gather.6.cloned.1.call-start = ((), (), s32[]{:S(2)}) async-start(), calls=%async_computation.4 | async-start | bytes 3604480 | tf_op jit(solution)/shard_map/all_gather | solution.py:548
  45.7 21.7 %collective-permute-start.6 = (bf16[128,2304]{1,0:T(8,128)(2,1)S(1)}, bf16[128,2304]{1,0:T(8,128)(2,1)}, u32[]{:S(2)}, u32[]{:S(2)}) collective-permute-start(bf16[128,2304]{1,0:T(8,128)(2,1)S(1)} %pad_maximum_fusion.14), channel_id=1, source_target_pairs={{0,8},{2,10},{4,12},{6,14},{8,16},{10,18},{12,20},{14,22},{16,24},... | collective-permute-start | bytes 1769480 | tf_op jit(solution)/shard_map/ppermute | solution.py:426
  50.9 19.7 %collective-permute-start.1 = (bf16[2,2,128]{2,1,0:T(2,128)(2,1)S(1)}, bf16[2,2,128]{2,1,0:T(2,128)(2,1)S(1)}, u32[]{:S(2)}, u32[]{:S(2)}) collective-permute-start(bf16[2,2,128]{2,1,0:T(2,128)(2,1)S(1)} %pad_maximum_fusion.19), channel_id=1, source_target_pairs={{0,4},{2,6},{4,0},{6,2},{8,12},{10,14},{12,8},{14,10},{16,20},{18,... | collective-permute-start | bytes 3080 | tf_op jit(solution)/shard_map/ppermute | solution.py:423
  68.6 59.2 %collective-permute-start.11 = (bf16[256,2304]{1,0:T(8,128)(2,1)S(1)}, bf16[256,2304]{1,0:T(8,128)(2,1)S(1)}, u32[]{:S(2)}, u32[]{:S(2)}) collective-permute-start(bf16[256,2304]{1,0:T(8,128)(2,1)S(1)} %shard_map.523), channel_id=1, source_target_pairs={{0,2},{2,0},{4,6},{6,4},{8,10},{10,8},{12,14},{14,12},{16,18},{18,... | collective-permute-start | bytes 3538952 | tf_op jit(solution)/shard_map/ppermute | solution.py:423
  69.9 60.4 %collective-permute-start.12 = (bf16[256,2304]{1,0:T(8,128)(2,1)S(1)}, bf16[256,2304]{1,0:T(8,128)(2,1)S(1)}, u32[]{:S(2)}, u32[]{:S(2)}) collective-permute-start(bf16[256,2304]{1,0:T(8,128)(2,1)S(1)} %shard_map.523), channel_id=1, source_target_pairs={{0,4},{2,6},{4,0},{6,2},{8,12},{10,14},{12,8},{14,10},{16,20},{18,... | collective-permute-start | bytes 3538952 | tf_op jit(solution)/shard_map/ppermute | solution.py:423
  76.1 49.1 %collective-permute-start.15 = (bf16[128,2304]{1,0:T(8,128)(2,1)}, bf16[128,2304]{1,0:T(8,128)(2,1)}, u32[]{:S(2)}, u32[]{:S(2)}) collective-permute-start(bf16[128,2304]{1,0:T(8,128)(2,1)} %collective-permute-done.6), channel_id=1, source_target_pairs={{0,8},{2,10},{4,12},{6,14},{8,16},{10,18},{12,20},{14,22},{16,24},... | collective-permute-start | bytes 1769480 | tf_op jit(solution)/shard_map/ppermute | solution.py:426
  82.3 22.1 %collective-permute-start.3 = (bf16[4,2,128]{2,1,0:T(2,128)(2,1)S(1)}, bf16[4,2,128]{2,1,0:T(2,128)(2,1)S(1)}, u32[]{:S(2)}, u32[]{:S(2)}) collective-permute-start(bf16[4,2,128]{2,1,0:T(2,128)(2,1)S(1)} %collective-permute-done.2), channel_id=1, source_target_pairs={{0,8},{2,10},{4,12},{6,14},{8,16},{10,18},{12,20},{14,22},{16,24},... | collective-permute-start | bytes 6152 | tf_op jit(solution)/shard_map/ppermute | solution.py:426
  133.6 41.0 %collective-permute-start.5 = (bf16[384,2048]{1,0:T(8,128)(2,1)}, bf16[384,2048]{1,0:T(8,128)(2,1)}, u32[]{:S(2)}, u32[]{:S(2)}) collective-permute-start(bf16[384,2048]{1,0:T(8,128)(2,1)} %fusion.5), channel_id=1, source_target_pairs={{0,1},{1,0},{2,3},{3,2},{4,5},{5,4},{6,7},{7,6},{8,9},{9,8},{10,11... | collective-permute-start | bytes 4718600 | tf_op jit(solution)/shard_map/ppermute | solution.py:82
  133.6 183.4 %all-gather.4.cloned.1.call-start = ((), (), s32[]{:S(2)}) async-start(), calls=%async_computation.3 | async-start | bytes 3604480 | tf_op jit(solution)/shard_map/all_gather | solution.py:548
  143.9 23.8 %collective-permute-start.17 = (bf16[256,2304]{1,0:T(8,128)(2,1)S(1)}, bf16[256,2304]{1,0:T(8,128)(2,1)}, u32[]{:S(2)}, u32[]{:S(2)}) collective-permute-start(bf16[256,2304]{1,0:T(8,128)(2,1)S(1)} %shard_map.524), channel_id=1, source_target_pairs={{0,2},{2,0},{4,6},{6,4},{8,10},{10,8},{12,14},{14,12},{16,18},{18,... | collective-permute-start | bytes 3538952 | tf_op jit(solution)/shard_map/ppermute | solution.py:423
  144.3 24.6 %collective-permute-start.18 = (bf16[256,2304]{1,0:T(8,128)(2,1)S(1)}, bf16[256,2304]{1,0:T(8,128)(2,1)}, u32[]{:S(2)}, u32[]{:S(2)}) collective-permute-start(bf16[256,2304]{1,0:T(8,128)(2,1)S(1)} %shard_map.524), channel_id=1, source_target_pairs={{0,4},{2,6},{4,0},{6,2},{8,12},{10,14},{12,8},{14,10},{16,20},{18,... | collective-permute-start | bytes 3538952 | tf_op jit(solution)/shard_map/ppermute | solution.py:423
  225.8 564.4 %reduce-scatter.4.cloned.1.call-start = ((), (), s32[]{:S(2)}) async-start(), calls=%async_computation.6 | async-start | bytes 3604480 | tf_op jit(solution)/shard_map/reduce_scatter | solution.py:569
  227.6 40.6 %collective-permute-start.29 = (bf16[384,2048]{1,0:T(8,128)(2,1)S(1)}, bf16[384,2048]{1,0:T(8,128)(2,1)}, u32[]{:S(2)}, u32[]{:S(2)}) collective-permute-start(bf16[384,2048]{1,0:T(8,128)(2,1)S(1)} %shard_map.531), channel_id=1, source_target_pairs={{0,2},{2,0},{4,6},{6,4},{8,10},{10,8},{12,14},{14,12},{16,18},{18,... | collective-permute-start | bytes 4718600 | tf_op jit(solution)/shard_map/ppermute | solution.py:423
  228.0 37.7 %collective-permute-start.30 = (bf16[384,2048]{1,0:T(8,128)(2,1)S(1)}, bf16[384,2048]{1,0:T(8,128)(2,1)}, u32[]{:S(2)}, u32[]{:S(2)}) collective-permute-start(bf16[384,2048]{1,0:T(8,128)(2,1)S(1)} %shard_map.531), channel_id=1, source_target_pairs={{0,4},{2,6},{4,0},{6,2},{8,12},{10,14},{12,8},{14,10},{16,20},{18,... | collective-permute-start | bytes 4718600 | tf_op jit(solution)/shard_map/ppermute | solution.py:423
  230.5 100.3 %collective-permute-start.28 = (bf16[16,64,1408]{2,1,0:T(8,128)(2,1)}, bf16[16,64,1408]{2,1,0:T(8,128)(2,1)}, u32[]{:S(2)}, u32[]{:S(2)}) collective-permute-start(bf16[16,64,1408]{2,1,0:T(8,128)(2,1)} %all-gather.8.cloned.1.call-done.refs_0_), channel_id=1, source_target_pairs={{0,1},{1,0},{2,3},{3,2},{4,5},{5,4},{6,7},{7,6},{8,9},{9,8},{10,11... | collective-permute-start | bytes 8650760 | tf_op jit(solution)/shard_map/ppermute | solution.py:82
  239.4 80.3 %collective-permute-start.23 = (bf16[384,2048]{1,0:T(8,128)(2,1)}, bf16[384,2048]{1,0:T(8,128)(2,1)}, u32[]{:S(2)}, u32[]{:S(2)}) collective-permute-start(bf16[384,2048]{1,0:T(8,128)(2,1)} %get-tuple-element.94), channel_id=1, source_target_pairs={{0,4},{2,6},{4,0},{6,2},{8,12},{10,14},{12,8},{14,10},{16,20},{18,... | collective-permute-start | bytes 4718600 | tf_op jit(solution)/shard_map/ppermute | solution.py:423
  239.4 82.0 %collective-permute-start.22 = (bf16[384,2048]{1,0:T(8,128)(2,1)}, bf16[384,2048]{1,0:T(8,128)(2,1)}, u32[]{:S(2)}, u32[]{:S(2)}) collective-permute-start(bf16[384,2048]{1,0:T(8,128)(2,1)} %get-tuple-element.94), channel_id=1, source_target_pairs={{0,2},{2,0},{4,6},{6,4},{8,10},{10,8},{12,14},{14,12},{16,18},{18,... | collective-permute-start | bytes 4718600 | tf_op jit(solution)/shard_map/ppermute | solution.py:423
  267.0 48.0 %collective-permute-start.31 = (bf16[192,2048]{1,0:T(8,128)(2,1)S(1)}, bf16[192,2048]{1,0:T(8,128)(2,1)}, u32[]{:S(2)}, u32[]{:S(2)}) collective-permute-start(bf16[192,2048]{1,0:T(8,128)(2,1)S(1)} %slice.284), channel_id=1, source_target_pairs={{0,2},{2,0},{4,6},{6,4},{8,10},{10,8},{12,14},{14,12},{16,18},{18,... | collective-permute-start | bytes 2359304 | tf_op jit(solution)/shard_map/ppermute | solution.py:423
  270.3 46.8 %collective-permute-start.32 = (bf16[192,2048]{1,0:T(8,128)(2,1)}, bf16[192,2048]{1,0:T(8,128)(2,1)}, u32[]{:S(2)}, u32[]{:S(2)}) collective-permute-start(bf16[192,2048]{1,0:T(8,128)(2,1)} %slice.285), channel_id=1, source_target_pairs={{0,4},{2,6},{4,0},{6,2},{8,12},{10,14},{12,8},{14,10},{16,20},{18,... | collective-permute-start | bytes 2359304 | tf_op jit(solution)/shard_map/ppermute | solution.py:423
  315.0 33.5 %collective-permute-start.27 = (bf16[16,64,1408]{2,1,0:T(8,128)(2,1)}, bf16[16,64,1408]{2,1,0:T(8,128)(2,1)S(1)}, u32[]{:S(2)}, u32[]{:S(2)}) collective-permute-start(bf16[16,64,1408]{2,1,0:T(8,128)(2,1)} %all-gather.6.cloned.1.call-done.refs_0_), channel_id=1, source_target_pairs={{0,1},{1,0},{2,3},{3,2},{4,5},{5,4},{6,7},{7,6},{8,9},{9,8},{10,11... | collective-permute-start | bytes 8650760 | tf_op jit(solution)/shard_map/ppermute | solution.py:82
  317.1 32.4 %collective-permute-start.26 = (bf16[16,64,1408]{2,1,0:T(8,128)(2,1)}, bf16[16,64,1408]{2,1,0:T(8,128)(2,1)S(1)}, u32[]{:S(2)}, u32[]{:S(2)}) collective-permute-start(bf16[16,64,1408]{2,1,0:T(8,128)(2,1)} %all-gather.4.cloned.1.call-done.refs_0_), channel_id=1, source_target_pairs={{0,1},{1,0},{2,3},{3,2},{4,5},{5,4},{6,7},{7,6},{8,9},{9,8},{10,11... | collective-permute-start | bytes 8650760 | tf_op jit(solution)/shard_map/ppermute | solution.py:82
  320.9 30.4 %collective-permute-start.24 = (bf16[192,2048]{1,0:T(8,128)(2,1)S(1)}, bf16[192,2048]{1,0:T(8,128)(2,1)S(1)}, u32[]{:S(2)}, u32[]{:S(2)}) collective-permute-start(bf16[192,2048]{1,0:T(8,128)(2,1)S(1)} %slice.282), channel_id=1, source_target_pairs={{0,2},{2,0},{4,6},{6,4},{8,10},{10,8},{12,14},{14,12},{16,18},{18,... | collective-permute-start | bytes 2359304 | tf_op jit(solution)/shard_map/ppermute | solution.py:423
  322.6 33.8 %collective-permute-start.25 = (bf16[192,2048]{1,0:T(8,128)(2,1)S(1)}, bf16[192,2048]{1,0:T(8,128)(2,1)S(1)}, u32[]{:S(2)}, u32[]{:S(2)}) collective-permute-start(bf16[192,2048]{1,0:T(8,128)(2,1)S(1)} %slice.283), channel_id=1, source_target_pairs={{0,4},{2,6},{4,0},{6,2},{8,12},{10,14},{12,8},{14,10},{16,20},{18,... | collective-permute-start | bytes 2359304 | tf_op jit(solution)/shard_map/ppermute | solution.py:423
  423.0 23.2 %collective-permute-start.57 = (bf16[16,64,1408]{2,1,0:T(8,128)(2,1)}, bf16[16,64,1408]{2,1,0:T(8,128)(2,1)}, u32[]{:S(2)}, u32[]{:S(2)}) collective-permute-start(bf16[16,64,1408]{2,1,0:T(8,128)(2,1)} %fusion.14), channel_id=1, source_target_pairs={{0,1},{1,0},{2,3},{3,2},{4,5},{5,4},{6,7},{7,6},{8,9},{9,8},{10,11... | collective-permute-start | bytes 8650760 | tf_op jit(solution)/shard_map/ppermute | solution.py:82
  445.0 26.8 %collective-permute-start.33 = (bf16[192,2048]{1,0:T(8,128)(2,1)}, bf16[192,2048]{1,0:T(8,128)(2,1)S(1)}, u32[]{:S(2)}, u32[]{:S(2)}) collective-permute-start(bf16[192,2048]{1,0:T(8,128)(2,1)} %get-tuple-element.117), channel_id=1, source_target_pairs={{0,4},{2,6},{4,0},{6,2},{8,12},{10,14},{12,8},{14,10},{16,20},{18,... | collective-permute-start | bytes 2359304 | tf_op jit(solution)/shard_map/ppermute | solution.py:423
  445.0 26.7 %collective-permute-start.35 = (bf16[192,2048]{1,0:T(8,128)(2,1)S(1)}, bf16[192,2048]{1,0:T(8,128)(2,1)}, u32[]{:S(2)}, u32[]{:S(2)}) collective-permute-start(bf16[192,2048]{1,0:T(8,128)(2,1)S(1)} %get-tuple-element.116), channel_id=1, source_target_pairs={{0,2},{2,0},{4,6},{6,4},{8,10},{10,8},{12,14},{14,12},{16,18},{18,... | collective-permute-start | bytes 2359304 | tf_op jit(solution)/shard_map/ppermute | solution.py:423
  451.9 343.9 %reduce-scatter.6.cloned.1.call-start = ((), (), s32[]{:S(2)}) async-start(), calls=%async_computation.7 | async-start | bytes 3604480 | tf_op jit(solution)/shard_map/reduce_scatter | solution.py:569
  471.7 66.2 %collective-permute-start.62 = (bf16[16,64,1408]{2,1,0:T(8,128)(2,1)}, bf16[16,64,1408]{2,1,0:T(8,128)(2,1)}, u32[]{:S(2)}, u32[]{:S(2)}) collective-permute-start(bf16[16,64,1408]{2,1,0:T(8,128)(2,1)} %fusion.15), channel_id=1, source_target_pairs={{0,1},{1,0},{2,3},{3,2},{4,5},{5,4},{6,7},{7,6},{8,9},{9,8},{10,11... | collective-permute-start | bytes 8650760 | tf_op jit(solution)/shard_map/ppermute | solution.py:82
  475.6 37.0 %collective-permute-start.36 = (bf16[384,2048]{1,0:T(8,128)(2,1)S(1)}, bf16[384,2048]{1,0:T(8,128)(2,1)}, u32[]{:S(2)}, u32[]{:S(2)}) collective-permute-start(bf16[384,2048]{1,0:T(8,128)(2,1)S(1)} %pad_maximum_fusion.1), channel_id=1, source_target_pairs={{0,4},{2,6},{4,0},{6,2},{8,12},{10,14},{12,8},{14,10},{16,20},{18,... | collective-permute-start | bytes 4718600 | tf_op jit(solution)/shard_map/ppermute | solution.py:423
  478.1 36.9 %collective-permute-start.34 = (bf16[384,2048]{1,0:T(8,128)(2,1)}, bf16[384,2048]{1,0:T(8,128)(2,1)}, u32[]{:S(2)}, u32[]{:S(2)}) collective-permute-start(bf16[384,2048]{1,0:T(8,128)(2,1)} %pad_maximum_fusion), channel_id=1, source_target_pairs={{0,2},{2,0},{4,6},{6,4},{8,10},{10,8},{12,14},{14,12},{16,18},{18,... | collective-permute-start | bytes 4718600 | tf_op jit(solution)/shard_map/ppermute | solution.py:423
  535.9 19.2 %collective-permute-start.37 = (bf16[192,2048]{1,0:T(8,128)(2,1)}, bf16[192,2048]{1,0:T(8,128)(2,1)}, u32[]{:S(2)}, u32[]{:S(2)}) collective-permute-start(bf16[192,2048]{1,0:T(8,128)(2,1)} %get-tuple-element.113), channel_id=1, source_target_pairs={{0,4},{2,6},{4,0},{6,2},{8,12},{10,14},{12,8},{14,10},{16,20},{18,... | collective-permute-start | bytes 2359304 | tf_op jit(solution)/shard_map/ppermute | solution.py:423
  543.9 255.0 %reduce-scatter.8.cloned.1.call-start = ((), (), s32[]{:S(2)}) async-start(), calls=%async_computation.8 | async-start | bytes 3604480 | tf_op jit(solution)/shard_map/reduce_scatter | solution.py:569
  558.7 34.6 %collective-permute-start.40 = (bf16[384,2048]{1,0:T(8,128)(2,1)S(1)}, bf16[384,2048]{1,0:T(8,128)(2,1)S(1)}, u32[]{:S(2)}, u32[]{:S(2)}) collective-permute-start(bf16[384,2048]{1,0:T(8,128)(2,1)S(1)} %pad_maximum_fusion.3), channel_id=1, source_target_pairs={{0,4},{2,6},{4,0},{6,2},{8,12},{10,14},{12,8},{14,10},{16,20},{18,... | collective-permute-start | bytes 4718600 | tf_op jit(solution)/shard_map/ppermute | solution.py:423
  560.1 34.3 %collective-permute-start.38 = (bf16[384,2048]{1,0:T(8,128)(2,1)S(1)}, bf16[384,2048]{1,0:T(8,128)(2,1)S(1)}, u32[]{:S(2)}, u32[]{:S(2)}) collective-permute-start(bf16[384,2048]{1,0:T(8,128)(2,1)S(1)} %pad_maximum_fusion.2), channel_id=1, source_target_pairs={{0,2},{2,0},{4,6},{6,4},{8,10},{10,8},{12,14},{14,12},{16,18},{18,... | collective-permute-start | bytes 4718600 | tf_op jit(solution)/shard_map/ppermute | solution.py:423
  577.8 22.7 %collective-permute-start.67 = (bf16[16,64,1408]{2,1,0:T(8,128)(2,1)}, bf16[16,64,1408]{2,1,0:T(8,128)(2,1)}, u32[]{:S(2)}, u32[]{:S(2)}) collective-permute-start(bf16[16,64,1408]{2,1,0:T(8,128)(2,1)} %fusion.16), channel_id=1, source_target_pairs={{0,1},{1,0},{2,3},{3,2},{4,5},{5,4},{6,7},{7,6},{8,9},{9,8},{10,11... | collective-permute-start | bytes 8650760 | tf_op jit(solution)/shard_map/ppermute | solution.py:82
  674.2 35.4 %collective-permute-start.42 = (bf16[384,2048]{1,0:T(8,128)(2,1)}, bf16[384,2048]{1,0:T(8,128)(2,1)}, u32[]{:S(2)}, u32[]{:S(2)}) collective-permute-start(bf16[384,2048]{1,0:T(8,128)(2,1)} %convolution_convert_fusion), channel_id=1, source_target_pairs={{0,1},{1,0},{2,3},{3,2},{4,5},{5,4},{6,7},{7,6},{8,9},{9,8},{10,11... | collective-permute-start | bytes 4718600 | tf_op jit(solution)/shard_map/ppermute | solution.py:82
  676.7 31.3 %collective-permute-start.45 = (bf16[256,1280]{1,0:T(8,128)(2,1)S(1)}, bf16[256,1280]{1,0:T(8,128)(2,1)S(1)}, u32[]{:S(2)}, u32[]{:S(2)}) collective-permute-start(bf16[256,1280]{1,0:T(8,128)(2,1)S(1)} %bitcast.246), channel_id=1, source_target_pairs={{0,2},{2,0},{4,6},{6,4},{8,10},{10,8},{12,14},{14,12},{16,18},{18,... | collective-permute-start | bytes 1966088 | tf_op jit(solution)/shard_map/ppermute | solution.py:423
  677.1 32.4 %collective-permute-start.43 = (bf16[256,1280]{1,0:T(8,128)(2,1)S(1)}, bf16[256,1280]{1,0:T(8,128)(2,1)S(1)}, u32[]{:S(2)}, u32[]{:S(2)}) collective-permute-start(bf16[256,1280]{1,0:T(8,128)(2,1)S(1)} %bitcast.245), channel_id=1, source_target_pairs={{0,4},{2,6},{4,0},{6,2},{8,12},{10,14},{12,8},{14,10},{16,20},{18,... | collective-permute-start | bytes 1966088 | tf_op jit(solution)/shard_map/ppermute | solution.py:423
  678.3 27.7 %collective-permute-start.50 = (bf16[256,1024]{1,0:T(8,128)(2,1)S(1)}, bf16[256,1024]{1,0:T(8,128)(2,1)S(1)}, u32[]{:S(2)}, u32[]{:S(2)}) collective-permute-start(bf16[256,1024]{1,0:T(8,128)(2,1)S(1)} %bitcast.247), channel_id=1, source_target_pairs={{0,4},{2,6},{4,0},{6,2},{8,12},{10,14},{12,8},{14,10},{16,20},{18,... | collective-permute-start | bytes 1572872 | tf_op jit(solution)/shard_map/ppermute | solution.py:423
  689.9 38.5 %collective-permute-start.53 = (bf16[512,1024]{1,0:T(8,128)(2,1)S(1)}, bf16[512,1024]{1,0:T(8,128)(2,1)S(1)}, u32[]{:S(2)}, u32[]{:S(2)}) collective-permute-start(bf16[512,1024]{1,0:T(8,128)(2,1)S(1)} %pad_maximum_fusion.13), channel_id=1, source_target_pairs={{0,4},{2,6},{4,0},{6,2},{8,12},{10,14},{12,8},{14,10},{16,20},{18,... | collective-permute-start | bytes 3145736 | tf_op jit(solution)/shard_map/ppermute | solution.py:423
  706.2 26.2 %collective-permute-start.51 = (bf16[512,1024]{1,0:T(8,128)(2,1)S(1)}, bf16[512,1024]{1,0:T(8,128)(2,1)S(1)}, u32[]{:S(2)}, u32[]{:S(2)}) collective-permute-start(bf16[512,1024]{1,0:T(8,128)(2,1)S(1)} %pad_maximum_fusion.12), channel_id=1, source_target_pairs={{0,2},{2,0},{4,6},{6,4},{8,10},{10,8},{12,14},{14,12},{16,18},{18,... | collective-permute-start | bytes 3145736 | tf_op jit(solution)/shard_map/ppermute | solution.py:423
  708.3 64.1 %collective-permute-start.46 = (bf16[512,1280]{1,0:T(8,128)(2,1)S(1)}, bf16[512,1280]{1,0:T(8,128)(2,1)S(1)}, u32[]{:S(2)}, u32[]{:S(2)}) collective-permute-start(bf16[512,1280]{1,0:T(8,128)(2,1)S(1)} %pad_maximum_fusion.5), channel_id=1, source_target_pairs={{0,4},{2,6},{4,0},{6,2},{8,12},{10,14},{12,8},{14,10},{16,20},{18,... | collective-permute-start | bytes 3932168 | tf_op jit(solution)/shard_map/ppermute | solution.py:423
  714.0 58.3 %collective-permute-start.44 = (bf16[512,1280]{1,0:T(8,128)(2,1)S(1)}, bf16[512,1280]{1,0:T(8,128)(2,1)S(1)}, u32[]{:S(2)}, u32[]{:S(2)}) collective-permute-start(bf16[512,1280]{1,0:T(8,128)(2,1)S(1)} %pad_maximum_fusion.4), channel_id=1, source_target_pairs={{0,2},{2,0},{4,6},{6,4},{8,10},{10,8},{12,14},{14,12},{16,18},{18,... | collective-permute-start | bytes 3932168 | tf_op jit(solution)/shard_map/ppermute | solution.py:423
  715.2 41.8 %collective-permute-start.73 = (f32[2,2048]{1,0:T(2,128)S(1)}, f32[2,2048]{1,0:T(2,128)S(1)}, u32[]{:S(2)}, u32[]{:S(2)}) collective-permute-start(f32[2,2048]{1,0:T(2,128)S(1)} %fusion.64), channel_id=1, source_target_pairs={{0,2},{2,0},{4,6},{6,4},{8,10},{10,8},{12,14},{14,12},{16,18},{18,... | collective-permute-start | bytes 49160 | tf_op jit(solution)/shard_map/ppermute | solution.py:423
  790.0 28.7 %collective-permute-start.48 = (bf16[128,1280]{1,0:T(8,128)(2,1)}, bf16[128,1280]{1,0:T(8,128)(2,1)}, u32[]{:S(2)}, u32[]{:S(2)}) collective-permute-start(bf16[128,1280]{1,0:T(8,128)(2,1)} %add_convert_fusion.2), channel_id=1, source_target_pairs={{0,8},{2,10},{4,12},{6,14},{8,16},{10,18},{12,20},{14,22},{16,24},... | collective-permute-start | bytes 983048 | tf_op jit(solution)/shard_map/ppermute | solution.py:426
  (136 other events, 1445.1 us)
Sparse Core Ops, SparseCore 0:
  45.5 76.3 all-gather.7
  133.7 57.2 all-gather.5
  226.0 58.3 all-gather.3
  452.1 55.1 reduce-scatter.3
  544.0 54.5 reduce-scatter.5
  606.6 55.0 reduce-scatter.7

commit v2 on v1

v2 whole, which is shorter than its diff:
```python
import functools
import math

import jax
import jax.numpy as jnp
from jax import lax
from jax.experimental import pallas as pl
from jax.experimental.pallas import tpu as pltpu
from jax.sharding import PartitionSpec as P

HEAD = 64
STEP = 10


NORM_EPS = 1e-05
NEG_LARGE = -1000000000.0
BETA_FIRST = 0.9
BETA_SECOND = 0.95
ADAM_EPS = 1e-08
DECAY_RATE = 0.1
RATE_MAIN = 0.02
RATE_OUT = 0.15
RATE_DOWN = 0.015
RATE_GAINS = 0.6


def rope_tables(segment):
    length = segment.shape[0]
    order = jnp.arange(length, dtype=jnp.int32)
    before = jnp.sum((segment[None, :] < segment[:, None]).astype(jnp.int32), axis=1)
    place = (order - before).astype(jnp.float32)
    half = HEAD // 2
    freq = jnp.exp(jnp.arange(half, dtype=jnp.float32) * (-2.0 * math.log(10000.0) / HEAD))
    angle = place[:, None] * freq[None, :]
    cosine, sine = jnp.cos(angle), jnp.sin(angle)
    return (
        jnp.concatenate([cosine] * 4, axis=1),
        jnp.concatenate([-sine, sine, -sine, sine], axis=1),
    )


def contract_rows(left, right):
    return lax.dot_general(
        left, right, (((0,), (0,)), ((), ())), preferred_element_type=jnp.float32
    )


def contract_cols(left, right):
    return lax.dot_general(
        left, right, (((1,), (1,)), ((), ())), preferred_element_type=jnp.float32
    )


def adam(weight, grad, moment, square, rate, decay):
    moment_new = BETA_FIRST * moment + (1.0 - BETA_FIRST) * grad
    square_new = BETA_SECOND * square + (1.0 - BETA_SECOND) * grad * grad
    direction = (
        moment_new
        / (1.0 - BETA_FIRST**STEP)
        / (jnp.sqrt(square_new / (1.0 - BETA_SECOND**STEP)) + ADAM_EPS)
    )
    return (grad, moment_new, square_new, weight - rate * (direction + decay * weight))


LOW = jnp.bfloat16
PLANE = 4
LANES = 128
TILE = 256
VMEM_LIMIT = 48 * 1024 * 1024
SMALL_COST = pl.CostEstimate(flops=1024, bytes_accessed=1024, transcendentals=0)
LARGE_COST = pl.CostEstimate(flops=1 << 35, bytes_accessed=1 << 20, transcendentals=0)


def swap_cores(block):
    return lax.ppermute(block, "tensor", [(0, 1), (1, 0)])


def late(kernel, count, *refs):
    ins, rest = refs[: count[0]], refs[count[0] + count[1] :]
    kernel(*ins, *rest)


def call(kernel, waits, operands, *, in_specs, cost=LARGE_COST, **options):
    place = pl.BlockSpec(memory_space=pltpu.HBM)
    return pl.pallas_call(
        functools.partial(late, kernel, (len(operands), len(waits))),
        in_specs=list(in_specs) + [place] * len(waits),
        compiler_params=pltpu.CompilerParams(vmem_limit_bytes=VMEM_LIMIT),
        cost_estimate=cost,
        **options,
    )(*operands, *waits)


def lane_of(shape):
    return lax.broadcasted_iota(jnp.int32, shape, len(shape) - 1)


def turn_heads(values, cosine, sine):
    first = lane_of(values.shape) % HEAD < HEAD // 2
    ahead = pltpu.roll(values, LANES - HEAD // 2, 1)
    behind = pltpu.roll(values, HEAD // 2, 1)
    return values * cosine + jnp.where(first, ahead, behind) * sine


def project_kernel(heads, normed_ref, weight_ref, cosine_ref, sine_ref, out_ref):
    part = jnp.dot(normed_ref[...], weight_ref[...], preferred_element_type=jnp.float32)
    cosine, sine = cosine_ref[...], sine_ref[...]
    step = pl.program_id(0)
    for at in range(0, part.shape[1], LANES):
        piece = part[:, at : at + LANES]
        turned = turn_heads(piece, cosine, sine)
        keep = step * part.shape[1] + at >= heads
        out_ref[:, at : at + LANES] = jnp.where(keep, piece, turned).astype(LOW)


def project(normed, weight, cosine, sine, turned, waits=()):
    rows, depth = normed.shape
    columns = weight.shape[1]
    block = 2 * LANES
    return call(
        functools.partial(project_kernel, turned),
        waits,
        (normed, weight, cosine, sine),
        cost=SMALL_COST,
        grid=(columns // block,),
        in_specs=[
            pl.BlockSpec((rows, depth), lambda i: (0, 0)),
            pl.BlockSpec((depth, block), lambda i: (0, i)),
            pl.BlockSpec((rows, LANES), lambda i: (0, 0)),
            pl.BlockSpec((rows, LANES), lambda i: (0, 0)),
        ],
        out_specs=pl.BlockSpec((rows, block), lambda i: (0, i)),
        out_shape=jax.ShapeDtypeStruct((rows, columns), LOW),
    )


def double(values, group):
    low_half = lane_of(values.shape) < HEAD
    other = pltpu.roll(values.astype(jnp.float32), HEAD, 1).astype(values.dtype)
    return jnp.where(low_half == (group == 0), values, other)


def set_bias(across_ref, down_ref, bias):
    rows = bias.shape[0]
    row = lax.broadcasted_iota(jnp.int32, (rows, rows), 0)
    column = lax.broadcasted_iota(jnp.int32, (rows, rows), 1)
    allowed = (down_ref[...] == across_ref[...]) & (column <= row)
    bias[...] = jnp.where(allowed, 0.0, NEG_LARGE)


def halves_of(block):
    low_half = lane_of(block.shape) < HEAD
    zero = jnp.zeros_like(block)
    return jnp.where(low_half, block, zero), jnp.where(low_half, zero, block)


def dot_last(left, right):
    return lax.dot_general(
        left, right, (((1,), (1,)), ((), ())), preferred_element_type=jnp.float32
    )


def dot_first(left, right):
    return lax.dot_general(
        left, right, (((0,), (0,)), ((), ())), preferred_element_type=jnp.float32
    )


def attend_kernel(
    group, query_ref, key_ref, value_ref, across_ref, down_ref, out_ref, total_ref, bias, keys, values
):
    step = pl.program_id(0)
    rows = query_ref.shape[0]

    @pl.when(step == 0)
    def _():
        set_bias(across_ref, down_ref, bias)
        total_ref[...] = jnp.zeros_like(total_ref)
        keys[...] = double(key_ref[...], group)
        values[...] = double(value_ref[...], group)

    for start in range(0, rows, TILE):
        stop = start + TILE
        query = query_ref[start:stop, :] * jnp.asarray(HEAD**-0.5, LOW)
        key, value = keys[:stop, :], values[:stop, :]
        shade = bias[start:stop, :stop]
        outs = []
        lane = lane_of((TILE, LANES))
        totals = total_ref[start:stop, :]
        for side, part in enumerate(halves_of(query)):
            score = dot_last(part, key) + shade
            largest = jnp.max(score, axis=1, keepdims=True)
            expo = jnp.exp(score - largest)
            total = jnp.sum(expo, axis=1, keepdims=True)
            probs = (expo * (1.0 / total)).astype(LOW)
            outs.append(jnp.dot(probs, value, preferred_element_type=jnp.float32))
            totals = jnp.where(lane == 2 * step + side, largest + jnp.log(total), totals)
        total_ref[start:stop, :] = totals
        out_ref[start:stop, :] = jnp.where(lane < HEAD, outs[0], outs[1]).astype(LOW)


def attend(into, segment, query_cols, group, waits=()):
    rows = into.shape[0]
    pairs = query_cols // LANES
    here = pairs // 2
    return call(
        functools.partial(attend_kernel, group),
        waits,
        (into, into, into, segment[None, :], segment[:, None]),
        cost=SMALL_COST,
        grid=(here,),
        in_specs=[
            pl.BlockSpec((rows, LANES), lambda i: (0, group * here + i)),
            pl.BlockSpec((rows, LANES), lambda i: (0, pairs)),
            pl.BlockSpec((rows, LANES), lambda i: (0, pairs + 1)),
            pl.BlockSpec((1, rows), lambda i: (0, 0)),
            pl.BlockSpec((rows, 1), lambda i: (0, 0)),
        ],
        out_specs=[
            pl.BlockSpec((rows, LANES), lambda i: (0, i)),
            pl.BlockSpec((rows, LANES), lambda i: (0, 0)),
        ],
        out_shape=[
            jax.ShapeDtypeStruct((rows, query_cols // 2), LOW),
            jax.ShapeDtypeStruct((rows, LANES), jnp.float32),
        ],
        scratch_shapes=[
            pltpu.VMEM((rows, rows), jnp.float32),
            pltpu.VMEM((rows, LANES), LOW),
            pltpu.VMEM((rows, LANES), LOW),
        ],
    )


def attend_back_kernel(
    group,
    query_ref,
    key_ref,
    value_ref,
    upstream_ref,
    total_ref,
    cosine_ref,
    sine_ref,
    across_ref,
    down_ref,
    before_ref,
    query_back_ref,
    rest_ref,
    bias,
    keys,
    values,
    key_sum,
    value_sum,
):
    step = pl.program_id(0)
    rows = query_ref.shape[0]

    @pl.when(step == 0)
    def _():
        set_bias(across_ref, down_ref, bias)
        keys[...] = double(key_ref[...], group)
        values[...] = double(value_ref[...], group)
        key_sum[...] = jnp.zeros_like(key_sum)
        value_sum[...] = jnp.zeros_like(value_sum)

    scale = jnp.asarray(HEAD**-0.5, LOW)
    for start in range(0, rows, TILE):
        stop = start + TILE
        query = query_ref[start:stop, :] * scale
        upstream = upstream_ref[start:stop, :]
        key, value = keys[:stop, :], values[:stop, :]
        shade = bias[start:stop, :stop]
        lane = lane_of((TILE, LANES))
        backs = []
        key_part = value_part = None
        for side, (part, grad) in enumerate(zip(halves_of(query), halves_of(upstream))):
            log_total = jnp.sum(
                jnp.where(lane == 2 * step + side, total_ref[start:stop, :], 0.0),
                axis=1,
                keepdims=True,
            )
            probs = jnp.exp(dot_last(part, key) + shade - log_total)
            value_here = dot_first(probs.astype(LOW), grad)
            probs_grad = dot_last(grad, value)
            delta = jnp.sum(probs * probs_grad, axis=1, keepdims=True)
            score_grad = (probs * (probs_grad - delta)).astype(LOW)
            backs.append(jnp.dot(score_grad, key, preferred_element_type=jnp.float32))
            key_here = dot_first(score_grad, part)
            key_part = key_here if key_part is None else key_part + key_here
            value_part = value_here if value_part is None else value_part + value_here
        key_sum[:stop, :] += key_part
        value_sum[:stop, :] += value_part
        back = jnp.where(lane < HEAD, backs[0], backs[1]) * HEAD**-0.5
        back = turn_heads(back, cosine_ref[start:stop, :], -sine_ref[start:stop, :])
        query_back_ref[start:stop, :] = back.astype(LOW)

    @pl.when(step == pl.num_programs(0) - 1)
    def _():
        key_back = key_sum[...] + pltpu.roll(key_sum[...], HEAD, 1)
        key_back = turn_heads(key_back, cosine_ref[...], -sine_ref[...]).astype(LOW)
        value_back = (value_sum[...] + pltpu.roll(value_sum[...], HEAD, 1)).astype(LOW)
        first = (lane_of(key_back.shape) < HEAD) & (group > 0)
        rest_ref[:, :LANES] = jnp.where(first, before_ref[:, :LANES], key_back)
        rest_ref[:, LANES:] = jnp.where(first, before_ref[:, LANES:], value_back)


def attend_back(into, upstream, log_totals, cosine, sine, segment, before, group, waits=()):
    rows, query_cols = upstream.shape
    pairs = query_cols // LANES
    here = pairs // 2
    whole = lambda width: pl.BlockSpec((rows, width), lambda i: (0, 0))
    return call(
        functools.partial(attend_back_kernel, group),
        waits,
        (into, into, into, upstream, log_totals, cosine, sine, segment[None, :], segment[:, None], before),
        grid=(here,),
        in_specs=[
            pl.BlockSpec((rows, LANES), lambda i: (0, group * here + i)),
            pl.BlockSpec((rows, LANES), lambda i: (0, pairs)),
            pl.BlockSpec((rows, LANES), lambda i: (0, pairs + 1)),
            pl.BlockSpec((rows, LANES), lambda i: (0, group * here + i)),
            whole(LANES),
            whole(LANES),
            whole(LANES),
            pl.BlockSpec((1, rows), lambda i: (0, 0)),
            whole(1),
            whole(2 * LANES),
        ],
        out_specs=[pl.BlockSpec((rows, LANES), lambda i: (0, i)), whole(2 * LANES)],
        out_shape=[
            jax.ShapeDtypeStruct((rows, query_cols // 2), LOW),
            jax.ShapeDtypeStruct((rows, 2 * LANES), LOW),
        ],
        scratch_shapes=[
            pltpu.VMEM((rows, rows), jnp.float32),
            pltpu.VMEM((rows, LANES), LOW),
            pltpu.VMEM((rows, LANES), LOW),
            pltpu.VMEM((rows, LANES), jnp.float32),
            pltpu.VMEM((rows, LANES), jnp.float32),
        ],
    )


def across_kernel(cuts, left_ref, right_ref, *out_refs):
    part = dot_last(left_ref[...], right_ref[...]).astype(LOW)
    start = 0
    for rows, out_ref in zip(cuts, out_refs):
        out_ref[...] = part[start : start + rows]
        start += rows


def across(left, right, first, cuts, waits=()):
    depth, columns = right.shape[1], right.shape[0]
    rows = sum(cuts)
    block = min(columns, 4 * LANES)
    assert first % rows == 0
    return call(
        functools.partial(across_kernel, cuts),
        waits,
        (left, right),
        grid=(columns // block,),
        in_specs=[
            pl.BlockSpec((rows, depth), lambda i: (first // rows, 0)),
            pl.BlockSpec((block, depth), lambda i: (i, 0)),
        ],
        out_specs=[pl.BlockSpec((cut, block), lambda i: (0, i)) for cut in cuts],
        out_shape=[jax.ShapeDtypeStruct((cut, columns), LOW) for cut in cuts],
    )


def plain_kernel(left_ref, right_ref, out_ref):
    out_ref[...] = jnp.dot(
        left_ref[...], right_ref[...], preferred_element_type=jnp.float32
    ).astype(LOW)


def plain(left, right, waits=()):
    rows, depth = left.shape
    columns = right.shape[1]
    block = 2 * LANES
    return call(
        plain_kernel,
        waits,
        (left, right),
        grid=(columns // block,),
        in_specs=[
            pl.BlockSpec((rows, depth), lambda i: (0, 0)),
            pl.BlockSpec((depth, block), lambda i: (0, i)),
        ],
        out_specs=pl.BlockSpec((rows, block), lambda i: (0, i)),
        out_shape=jax.ShapeDtypeStruct((rows, columns), LOW),
    )


def join_kernel(first_ref, second_ref, far_one_ref, far_two_ref, one_ref, two_ref):
    half = far_one_ref.shape[0]
    one_ref[:half] = first_ref[:half]
    one_ref[half:] = low(wide(first_ref[half:]) + wide(far_two_ref[...]))
    two_ref[:half] = low(wide(second_ref[:half]) + wide(far_one_ref[...]))
    two_ref[half:] = second_ref[half:]


def join_sends(first, second, far_one, far_two, waits=()):
    rows, columns = first.shape
    block = min(columns, 4 * LANES) if columns % (4 * LANES) == 0 else 2 * LANES
    full = pl.BlockSpec((rows, block), lambda i: (0, i))
    part = pl.BlockSpec((rows // 2, block), lambda i: (0, i))
    shape = jax.ShapeDtypeStruct((rows, columns), LOW)
    return call(
        join_kernel,
        waits,
        (first, second, far_one, far_two),
        cost=SMALL_COST,
        grid=(columns // block,),
        in_specs=[full, full, part, part],
        out_specs=[full, full],
        out_shape=[shape, shape],
    )


def norm_back_kernel(count, *refs):
    grads = refs[:count]
    values_ref, gain_ref, plus_ref, sum_ref, low_ref, gain_grad_ref = refs[count:]
    grad = sum(wide(ref[...]) for ref in grads)
    values = wide(values_ref[...])
    mean = jnp.mean(values * values, axis=1, keepdims=True)
    inverse = lax.rsqrt(mean + NORM_EPS)
    weighted = gain_ref[...] * grad
    across_mean = jnp.mean(weighted * values, axis=1, keepdims=True)
    back = inverse * weighted - values * (inverse * inverse * inverse) * across_mean
    total = wide(plus_ref[...]) + back
    sum_ref[...] = total
    low_ref[...] = low(total)

    @pl.when(pl.program_id(0) == 0)
    def _():
        gain_grad_ref[...] = jnp.zeros_like(gain_grad_ref)

    gain_grad_ref[...] += jnp.sum(grad * values * inverse, axis=0, keepdims=True)


def norm_back(grads, values, gain, plus, waits=()):
    rows, columns = values.shape
    block = LANES
    row = by_rows(block, columns)
    line = pl.BlockSpec((1, columns), lambda i: (0, 0))
    return call(
        functools.partial(norm_back_kernel, len(grads)),
        waits,
        (*grads, values, gain[None, :], plus),
        cost=SMALL_COST,
        grid=(rows // block,),
        in_specs=[row] * len(grads) + [row, line, row],
        out_specs=[row, row, line],
        out_shape=[
            jax.ShapeDtypeStruct((rows, columns), jnp.float32),
            jax.ShapeDtypeStruct((rows, columns), LOW),
            jax.ShapeDtypeStruct((1, columns), jnp.float32),
        ],
    )


def gate_up_kernel(normed_ref, weight_ref, out_ref):
    out_ref[...] = jnp.dot(normed_ref[...], weight_ref[...], preferred_element_type=jnp.float32)


def hidden_kernel(upstream_ref, down_ref, gate_up_ref, inner_ref, grads_ref):
    width = down_ref.shape[1]
    grad = jnp.dot(upstream_ref[...], down_ref[...], preferred_element_type=jnp.float32)
    gate = gate_up_ref[:, :width]
    upper = gate_up_ref[:, width:]
    sigma = 1.0 / (1.0 + jnp.exp(-gate))
    active = gate * sigma
    inner_ref[...] = (active * upper).astype(LOW)
    slope = sigma * (1.0 + gate * (1.0 - sigma))
    grads_ref[:, :width] = (grad * upper * slope).astype(LOW)
    grads_ref[:, width:] = (grad * active).astype(LOW)


def held(array):
    return pl.BlockSpec(array.shape, lambda i: (0, 0), pipeline_mode=pl.Buffered(1))


def by_rows(block, width):
    return pl.BlockSpec((block, width), lambda i: (i, 0))


def gate_and_up(normed, weight, waits=()):
    rows, depth = normed.shape
    columns = weight.shape[1]
    return call(
        gate_up_kernel,
        waits,
        (normed, weight),
        grid=(rows // TILE,),
        in_specs=[by_rows(TILE, depth), held(weight)],
        out_specs=by_rows(TILE, columns),
        out_shape=jax.ShapeDtypeStruct((rows, columns), jnp.float32),
    )


def hidden(upstream, down, gate_up, waits=()):
    rows, depth = upstream.shape
    width = down.shape[1]
    return call(
        hidden_kernel,
        waits,
        (upstream, down, gate_up),
        grid=(rows // TILE,),
        in_specs=[by_rows(TILE, depth), held(down), by_rows(TILE, 2 * width)],
        out_specs=[by_rows(TILE, width), by_rows(TILE, 2 * width)],
        out_shape=[
            jax.ShapeDtypeStruct((rows, width), LOW),
            jax.ShapeDtypeStruct((rows, 2 * width), LOW),
        ],
    )


def inner_kernel(left_ref, right_ref, out_ref):
    out_ref[...] = dot_first(left_ref[...], right_ref[...]).astype(LOW)


def inner_rows(left, right, waits=()):
    depth, rows = left.shape
    columns = right.shape[1]
    block = 2 * LANES
    return call(
        inner_kernel,
        waits,
        (left, right),
        grid=(rows // block,),
        in_specs=[pl.BlockSpec((depth, block), lambda i: (0, i)), held(right)],
        out_specs=pl.BlockSpec((block, columns), lambda i: (i, 0)),
        out_shape=jax.ShapeDtypeStruct((rows, columns), LOW),
    )


def put_halves(core_ref, part, keep_ref, give_ref):
    rows = keep_ref.shape[1]
    first = core_ref[0] == 0
    for at in range(keep_ref.shape[0]):
        start = 2 * rows * at
        top, bottom = part[start : start + rows], part[start + rows : start + 2 * rows]
        keep_ref[at] = jnp.where(first, top, bottom)
        give_ref[at] = jnp.where(first, bottom, top)


def unit_grads_kernel(
    blocks,
    core_ref,
    upstream_ref,
    inner_ref,
    normed_ref,
    grads_ref,
    down_keep_ref,
    down_give_ref,
    keep_ref,
    give_ref,
):
    step = pl.program_id(0)

    @pl.when(step < blocks)
    def _():
        part = dot_first(upstream_ref[...], inner_ref[...]).astype(LOW)
        put_halves(core_ref, part, down_keep_ref, down_give_ref)

    @pl.when(step >= blocks)
    def _():
        part = dot_first(normed_ref[...], grads_ref[...]).astype(LOW)
        put_halves(core_ref, part, keep_ref, give_ref)


def unit_grads(upstream, inner, normed, grads, rows, waits=()):
    depth, total = upstream.shape
    block = 2 * LANES
    blocks, lots = total // block, block // rows // 2
    core = lax.axis_index("tensor").astype(jnp.int32).reshape(1)
    early = lambda i: jnp.minimum(i, blocks - 1)
    late_on = lambda i: jnp.maximum(i - blocks, 0)
    out = lambda width, when: pl.BlockSpec((lots, rows, width), lambda i: (when(i), 0, 0))
    shape = lambda width: jax.ShapeDtypeStruct((total // rows // 2, rows, width), LOW)
    widths = inner.shape[1], grads.shape[1]
    return call(
        functools.partial(unit_grads_kernel, blocks),
        waits,
        (core, upstream, inner, normed, grads),
        grid=(2 * blocks,),
        in_specs=[
            pl.BlockSpec(memory_space=pltpu.SMEM),
            pl.BlockSpec((depth, block), lambda i: (0, early(i))),
            held(inner),
            pl.BlockSpec((depth, block), lambda i: (0, late_on(i))),
            held(grads),
        ],
        out_specs=[out(widths[0], early)] * 2 + [out(widths[1], late_on)] * 2,
        out_shape=[shape(widths[0])] * 2 + [shape(widths[1])] * 2,
    )


def hold_kernel(*refs):
    half = len(refs) // 2
    for source, target in zip(refs[:half], refs[half:]):
        target[...] = source[...]


def hold(values, waits=()):
    specs = [pl.BlockSpec(value.shape, lambda *_, rank=value.ndim: (0,) * rank) for value in values]
    return list(
        call(
            hold_kernel,
            waits,
            values,
            cost=SMALL_COST,
            grid=(1,),
            in_specs=specs,
            out_specs=specs,
            out_shape=[jax.ShapeDtypeStruct(value.shape, value.dtype) for value in values],
        )
    )


def nothing_kernel(*refs):
    del refs


def fence(values, waits=()):
    place = pl.BlockSpec(memory_space=pltpu.HBM)
    return list(
        pl.pallas_call(
            nothing_kernel,
            in_specs=[place] * (len(values) + len(waits)),
            out_specs=[place] * len(values),
            out_shape=[jax.ShapeDtypeStruct(value.shape, value.dtype) for value in values],
            input_output_aliases={at: at for at in range(len(values))},
            compiler_params=pltpu.CompilerParams(vmem_limit_bytes=1024 * 1024),
            cost_estimate=SMALL_COST,
        )(*values, *waits)
    )


def move_kernel(counts, cuts, extra, spots_ref, *refs):
    *blocks, sems = refs
    sources, targets = blocks[: len(counts)], blocks[len(counts) + extra :]
    copies, step = [], 0
    for count, source in zip(counts, sources):
        for at in range(count):
            for (left, right), target in zip(cuts, targets):
                part = source.at[at] if len(cuts) == 1 else source.at[at, :, left:right]
                copies.append(
                    pltpu.make_async_copy(part, target.at[spots_ref[step]], sems.at[len(copies)])
                )
            step += 1
    for copy in copies:
        copy.start()
    for copy in copies:
        copy.wait()


def move(blocks, spots, cuts=None, waits=()):
    counts = [block.shape[0] for block in blocks]
    rows, columns = blocks[0].shape[1:]
    ends = [0, *(cuts or []), columns]
    lots = list(zip(ends[:-1], ends[1:]))
    place = pl.BlockSpec(memory_space=pltpu.HBM)
    return pl.pallas_call(
        functools.partial(move_kernel, counts, lots, len(waits)),
        in_specs=[pl.BlockSpec(memory_space=pltpu.SMEM)] + [place] * (len(blocks) + len(waits)),
        out_specs=[place] * len(lots),
        out_shape=[
            jax.ShapeDtypeStruct((sum(counts), rows, right - left), LOW) for left, right in lots
        ],
        scratch_shapes=[pltpu.SemaphoreType.DMA((sum(counts) * len(lots),))],
        compiler_params=pltpu.CompilerParams(vmem_limit_bytes=1024 * 1024),
        cost_estimate=SMALL_COST,
    )(spots, *blocks, *waits)


def split_kernel(left_columns, whole_ref, left_ref, right_ref):
    left_ref[...] = whole_ref[:, :, :left_columns]
    right_ref[...] = whole_ref[:, :, left_columns:]


def split_columns(whole, left, waits=()):
    lots, rows, columns = whole.shape
    block = max(1, lots // 4)
    spec = lambda width: pl.BlockSpec((block, rows, width), lambda i: (i, 0, 0))
    shape = lambda width: jax.ShapeDtypeStruct((lots, rows, width), LOW)
    return call(
        functools.partial(split_kernel, left),
        waits,
        (whole,),
        cost=SMALL_COST,
        grid=(lots // block,),
        in_specs=[spec(columns)],
        out_specs=[spec(left), spec(columns - left)],
        out_shape=[shape(left), shape(columns - left)],
    )


def spread_kernel(cuts, extra, spots_ref, own_ref, other_ref, *refs):
    *targets, sems = refs[extra:]
    copies = []
    for at, source in enumerate((own_ref, other_ref)):
        for (left, right), target in zip(cuts, targets):
            copies.append(
                pltpu.make_async_copy(
                    source.at[:, :, left:right], target.at[:, spots_ref[at]], sems.at[len(copies)]
                )
            )
    for copy in copies:
        copy.start()
    for copy in copies:
        copy.wait()


def spread_halves(own, other, spots, cuts):
    count, rows, columns = own.shape
    ends = [0, *cuts, columns]
    lots = list(zip(ends[:-1], ends[1:]))
    place = pl.BlockSpec(memory_space=pltpu.HBM)
    return pl.pallas_call(
        functools.partial(spread_kernel, lots, 0),
        in_specs=[pl.BlockSpec(memory_space=pltpu.SMEM), place, place],
        out_specs=[place] * len(lots),
        out_shape=[
            jax.ShapeDtypeStruct((count, 2, rows, right - left), LOW) for left, right in lots
        ],
        scratch_shapes=[pltpu.SemaphoreType.DMA((2 * len(lots),))],
        compiler_params=pltpu.CompilerParams(vmem_limit_bytes=1024 * 1024),
        cost_estimate=SMALL_COST,
    )(spots, own, other)


def pick_kernel(count, spots_ref, *refs):
    del spots_ref
    for source, target in zip(refs[:count], refs[len(refs) - count :]):
        target[...] = source[0]


def pick(parts, spots, waits=()):
    lots, _, rows, columns = parts.shape
    count = spots.shape[0]
    place = pl.BlockSpec(memory_space=pltpu.HBM)
    return pl.pallas_call(
        functools.partial(pick_kernel, count),
        grid_spec=pltpu.PrefetchScalarGridSpec(
            num_scalar_prefetch=1,
            grid=(lots,),
            in_specs=[
                pl.BlockSpec(
                    (1, 1, rows, columns), lambda i, spots_ref, at=at: (i, spots_ref[at], 0, 0)
                )
                for at in range(count)
            ]
            + [place] * len(waits),
            out_specs=[
                pl.BlockSpec((1, rows, columns), lambda i, spots_ref: (i, 0, 0))
                for at in range(count)
            ],
        ),
        out_shape=[jax.ShapeDtypeStruct((lots, rows, columns), LOW)] * count,
        compiler_params=pltpu.CompilerParams(vmem_limit_bytes=VMEM_LIMIT),
        cost_estimate=SMALL_COST,
    )(spots, *[parts] * count, *waits)


def add_kernel(*refs):
    out_ref = refs[-1]
    start = 0
    for one_ref, two_ref in zip(refs[:-1:2], refs[1:-1:2]):
        stop = start + one_ref.shape[2]
        out_ref[:, :, start:stop] = low(wide(one_ref[...]) + wide(two_ref[...]))
        start = stop


def add_low(pairs, waits=()):
    lots, rows, _ = pairs[0][0].shape
    block = max(1, lots // 4)
    spec = lambda width: pl.BlockSpec((block, rows, width), lambda i: (i, 0, 0))
    arrays = [array for pair in pairs for array in pair]
    total = sum(one.shape[2] for one, _ in pairs)
    return call(
        add_kernel,
        waits,
        arrays,
        cost=SMALL_COST,
        grid=(lots // block,),
        in_specs=[spec(array.shape[2]) for array in arrays],
        out_specs=spec(total),
        out_shape=jax.ShapeDtypeStruct((lots, rows, total), LOW),
    )


def norm_kernel(values_ref, gain_ref, out_ref):
    values = wide(values_ref[...])
    mean = jnp.mean(values * values, axis=1, keepdims=True)
    out_ref[...] = low(values * lax.rsqrt(mean + NORM_EPS) * gain_ref[...])


def norm(values, gain, waits=()):
    rows, columns = values.shape
    row = by_rows(LANES, columns)
    return call(
        norm_kernel,
        waits,
        (values, gain[None, :]),
        cost=SMALL_COST,
        grid=(rows // LANES,),
        in_specs=[row, pl.BlockSpec((1, columns), lambda i: (0, 0))],
        out_specs=row,
        out_shape=jax.ShapeDtypeStruct((rows, columns), LOW),
    )


def order_rows(own, other):
    core = lax.axis_index("tensor").astype(jnp.int32)
    (whole,) = move([own[None], other[None]], jnp.stack([core, 1 - core]))
    return whole.reshape(-1, own.shape[1])


def pick_halves_kernel(count, half, spots_ref, *refs):
    del spots_ref
    targets = refs[count:]
    step = pl.program_id(0)
    targets[0][...] = refs[0][0]

    @pl.when(step < half)
    def _():
        for at in range(1, count):
            targets[2 * at - 1][...] = refs[at][0]

    @pl.when(step >= half)
    def _():
        for at in range(1, count):
            targets[2 * at][...] = refs[at][0]


def pick_halves(parts, spots):
    lots, _, rows, columns = parts.shape
    count, half = spots.shape[0], lots // 2
    spec = lambda where: pl.BlockSpec((1, rows, columns), where)
    shape = lambda size: jax.ShapeDtypeStruct((size, rows, columns), LOW)
    early = spec(lambda i, spots_ref: (jnp.minimum(i, half - 1), 0, 0))
    late_on = spec(lambda i, spots_ref: (jnp.maximum(i - half, 0), 0, 0))
    found = pl.pallas_call(
        functools.partial(pick_halves_kernel, count, half),
        grid_spec=pltpu.PrefetchScalarGridSpec(
            num_scalar_prefetch=1,
            grid=(lots,),
            in_specs=[
                pl.BlockSpec(
                    (1, 1, rows, columns), lambda i, spots_ref, at=at: (i, spots_ref[at], 0, 0)
                )
                for at in range(count)
            ],
            out_specs=[spec(lambda i, spots_ref: (i, 0, 0))] + [early, late_on] * (count - 1),
        ),
        out_shape=[shape(lots)] + [shape(half), shape(lots - half)] * (count - 1),
        compiler_params=pltpu.CompilerParams(vmem_limit_bytes=VMEM_LIMIT),
        cost_estimate=SMALL_COST,
    )(spots, *[parts] * count)
    return [block.reshape(-1, columns) for block in found]


def add_pairs_kernel(*refs):
    third = len(refs) // 3
    for one_ref, two_ref, out_ref in zip(refs[:third], refs[third : 2 * third], refs[2 * third :]):
        out_ref[...] = low(wide(one_ref[...]) + wide(two_ref[...]))


def add_pairs(ones, twos, waits=()):
    rows, columns = ones[0].shape
    block = columns // 2
    spec = pl.BlockSpec((rows, block), lambda i: (0, i))
    return call(
        add_pairs_kernel,
        waits,
        (*ones, *twos),
        cost=SMALL_COST,
        grid=(2,),
        in_specs=[spec] * (2 * len(ones)),
        out_specs=[spec] * len(ones),
        out_shape=[jax.ShapeDtypeStruct((rows, columns), LOW)] * len(ones),
    )


def part_rows(whole, waits=()):
    core = lax.axis_index("tensor").astype(jnp.int32)
    rows, columns = whole.shape[0] // 2, whole.shape[1]
    own, other = pick(whole.reshape(1, 2, rows, columns), jnp.stack([core, 1 - core]), waits)
    return own[0], other[0]


def wide(block):
    return block.astype(jnp.float32)


def low(block):
    return block.astype(LOW)


def order_cores(own, other, axis=0):
    return jnp.where(
        lax.axis_index("tensor") == 0,
        jnp.concatenate([own, other], axis=axis),
        jnp.concatenate([other, own], axis=axis),
    )


class Links:
    def __init__(self, devices):
        self.devices = devices
        self.planes = devices // PLANE
        self.pairs = {
            step: [(index, index ^ step) for index in range(devices)] for step in (1, 2, 3)
        }
        self.columns = [list(range(corner, devices, PLANE)) for corner in range(PLANE)]
        self.ring = [(index, (index + PLANE) % devices) for index in range(devices)]

    def swap(self, block, step):
        return lax.ppermute(block, "dp", self.pairs[step])

    def turn(self, block):
        return lax.ppermute(block, "dp", self.ring)

    def place(self):
        index = lax.axis_index("dp").astype(jnp.int32)
        return index // PLANE, index % PLANE

    def corner_spots(self):
        _, corner = self.place()
        return jnp.stack([corner ^ other for other in range(PLANE)])

    def shift(self, block, step):
        pairs = [(at, (at + PLANE * step) % self.devices) for at in range(self.devices)]
        return lax.ppermute(block, "dp", pairs)

    def gather_near(self, block):
        return [self.swap(block, 1), self.swap(block, 2)]

    def gather_far(self, first, second):
        half = first.shape[0] // 2
        return [self.swap(second[:half], 1), self.swap(first[half:], 2)]

    def sum_far(self, far_top, far_bottom):
        return [self.swap(far_top, 1), self.swap(far_bottom, 2)]

    def ring_start(self, sums, rows):
        level, _ = self.place()
        return lax.dynamic_slice_in_dim(sums, (level - 1) % self.planes * rows, rows, 0)

    def ring_step(self, total, sums, rows, step):
        level, _ = self.place()
        spot = (level - 1 - step) % self.planes * rows
        return wide(self.turn(low(total))) + lax.dynamic_slice_in_dim(sums, spot, rows, 0)

    def corners(self, part):
        rows, columns = part.shape[0] // self.devices, part.shape[1]
        parts = part.reshape(self.planes, PLANE, rows, columns)
        return pick_halves(parts, self.corner_spots())

    def sum_top(self, one_top, two_low):
        return [self.swap(one_top, 1), self.swap(two_low, 2)]

    def sum_low(self, one_low, two_top, far_one, far_two, waits=()):
        one, two = add_pairs([one_low, two_top], [far_two, far_one], waits)
        return [self.swap(one, 1), self.swap(two, 2)]

    def place_rows(self, rows, columns, bundles):
        level, corner = self.place()
        blocks, spots = [], []
        for start, parts in bundles:
            for other, lists in enumerate(parts):
                step = start
                for block in lists:
                    here = block.shape[0] // rows
                    for _ in range(here):
                        spots.append(((level - step) % self.planes) * PLANE + (corner ^ other))
                        step += 1
                    blocks.append(block.reshape(here, rows, columns))
        (whole,) = move(blocks, jnp.stack(spots))
        return whole.reshape(-1, columns)

    def cut_units(self, weights):
        core = lax.axis_index("tensor")
        rows, columns = weights[0].shape
        wanted = columns // 2
        pieces = jnp.stack(
            [
                jnp.concatenate(
                    [low(weight[:, half * wanted : (half + 1) * wanted]) for weight in weights],
                    axis=1,
                )
                for half in range(2)
            ],
            axis=0,
        ).reshape(2, 2, rows // 2, wanted * len(weights))
        keep = lax.dynamic_index_in_dim(pieces, core, 1, False)
        give = lax.dynamic_index_in_dim(pieces, 1 - core, 1, False)
        return keep, give

    def spread_units(self, keep, given):
        _, corner = self.place()
        quarters = order_cores(keep, given)
        arrived = []
        for other in range(PLANE):
            piece = lax.dynamic_slice_in_dim(quarters, corner ^ other, 1, 0)
            arrived.append(self.swap(piece, other) if other else piece)
        return arrived

    def place_plane(self, arrived, waits=()):
        return move(arrived, self.corner_spots(), None, waits)

    def gather_planes(self, plane):
        return lax.all_gather(plane, "dp", axis=0, tiled=True, axis_index_groups=self.columns)

    def place_units(self, own, other, cuts):
        core = lax.axis_index("tensor").astype(jnp.int32)
        parts = spread_halves(own, other, jnp.stack([core, 1 - core]), cuts)
        return [part.reshape(-1, part.shape[3]) for part in parts]

    def sum_planes(self, sums):
        return lax.psum_scatter(
            sums, "dp", scatter_dimension=0, tiled=True, axis_index_groups=self.columns
        )

    def return_units(self, total, waits=()):
        pieces = pick(total[None], self.corner_spots(), waits)
        arrived = [pieces[0]] + [self.swap(pieces[other], other) for other in (1, 2, 3)]
        return self.place_plane(arrived)[0]

    def join_units(self, quarters, count):
        core = lax.axis_index("tensor")
        keep = lax.dynamic_slice_in_dim(quarters, 2 * core, 2, 0)
        give = lax.dynamic_slice_in_dim(quarters, 2 - 2 * core, 2, 0)
        halves = order_cores(keep, swap_cores(give), axis=1)
        width = quarters.shape[2] // count
        return [
            wide(
                jnp.concatenate(
                    [halves[half][:, at * width : (at + 1) * width] for half in range(2)], axis=1
                )
            )
            for at in range(count)
        ]

    def gather_gains(self, corners, shape):
        level, corner = self.place()
        count, width = shape
        found = jnp.stack(corners, axis=0).reshape(self.devices, count * width)
        origin = jnp.arange(self.devices, dtype=jnp.int32)
        spot = ((origin % PLANE) ^ corner) * self.planes + (level - origin // PLANE) % self.planes
        choose = (spot[:, None] == origin[None, :]).astype(LOW)
        whole = jnp.dot(choose, found, preferred_element_type=jnp.float32)
        return jnp.swapaxes(whole.reshape(self.devices, count, width), 0, 1).reshape(count, -1)

    def own_gains(self, whole):
        width = whole.shape[1] // self.devices
        return lax.dynamic_slice(whole, (0, lax.axis_index("dp") * width), (whole.shape[0], width))


def shards(
    links,
    tokens,
    cotangent,
    segments,
    query_weight,
    key_weight,
    value_weight,
    out_weight,
    gate_weight,
    up_weight,
    down_weight,
    norm_gains,
    query_moment,
    key_moment,
    value_moment,
    out_moment,
    gate_moment,
    up_moment,
    down_moment,
    gains_moment,
    query_square,
    key_square,
    value_square,
    out_square,
    gate_square,
    up_square,
    down_square,
    gains_square,
):
    core = lax.axis_index("tensor")
    rows = tokens.shape[0]
    weight_rows, query_cols = query_weight.shape
    key_cols = key_weight.shape[1]
    into_cols = query_cols + 2 * key_cols
    units = gate_weight.shape[1]
    steps = links.planes

    def rows_of(values, which):
        return lax.dynamic_slice_in_dim(values, which * rows, rows, 0)

    def place_tokens(own, first, second, far_one, far_two):
        half, columns = rows // 2, own.shape[1]
        blocks = [block.reshape(-1, half, columns) for block in (own, first, second, far_one, far_two)]
        (whole,) = move(blocks, jnp.arange(2 * PLANE, dtype=jnp.int32))
        return whole.reshape(-1, columns)

    gains_low = low(norm_gains)
    into_weight = jnp.concatenate([low(query_weight), low(key_weight), low(value_weight)], axis=1)
    units_keep, units_give = links.cut_units([down_weight, gate_weight, up_weight])
    gain_slots = [gains_low] + [links.shift(gains_low, step) for step in range(1, steps)]
    slots = [into_weight, links.turn(into_weight)]
    units_given = swap_cores(units_give)
    gains_level = jnp.stack(gain_slots, axis=0)
    gains_level, units_given, slots[1] = fence([gains_level, units_given, slots[1]])

    gain_corners = [gains_level] + [links.swap(gains_level, other) for other in (1, 2, 3)]
    spread = links.spread_units(units_keep, units_given)
    for _ in range(2, steps):
        slots.append(links.turn(slots[-1]))
    values = fence([*spread[1:], slots[-1]])
    spread[1:], slots[-1] = values[:3], values[3]

    (units_plane,) = links.place_plane(spread)
    units_own = links.gather_planes(units_plane)
    out_slots = [low(out_weight)]
    for _ in range(1, steps):
        out_slots.append(links.turn(out_slots[-1]))

    group = max(1, steps // 2)
    into_one = jnp.concatenate(slots[:group], axis=0)
    into_two = jnp.concatenate(slots[group:], axis=0)
    near_one = links.gather_near(into_one)
    gain_all = links.gather_gains(gain_corners, norm_gains.shape)
    gain_one = gain_all[0]
    gain_two = gain_all[1]
    normed_one = norm(tokens, gain_one)
    normed_one_all = order_rows(normed_one, swap_cores(normed_one))
    segment = segments[0]
    cosine, sine = rope_tables(segment)
    near_one = fence(near_one, [normed_one_all, cosine, sine])
    far_one = links.gather_far(*near_one)
    near_two = links.gather_near(into_two)
    *far_one, near_a, near_b = fence([*far_one, *near_two])
    near_two = [near_a, near_b]
    far_two = fence(links.gather_far(*near_two))
    into_all = links.place_rows(
        weight_rows,
        into_cols,
        [
            (0, [[into_one], [near_one[0]], [near_one[1]], far_one]),
            (group, [[into_two], [near_two[0]], [near_two[1]], far_two]),
        ],
    )

    (out_bundle,) = fence([jnp.concatenate(out_slots, axis=0)], far_two)
    out_near = links.gather_near(out_bundle)
    into = project(normed_one_all, into_all, cosine, sine, query_cols + key_cols)
    attended_one, totals_one = attend(into, segment, query_cols, 0)
    out_near = fence(out_near, [attended_one])
    out_far = links.gather_far(*out_near)
    attended_two, totals_two = attend(into, segment, query_cols, 1, out_near)
    *out_far, cotangent_late = fence([*out_far, *hold([cotangent])], [attended_two])
    upstream_near = links.gather_near(cotangent_late)
    out_all = links.place_rows(
        weight_rows, query_cols, [(0, [[out_bundle], [out_near[0]], [out_near[1]], out_far])]
    )
    attended = jnp.concatenate([attended_one, attended_two], axis=1)
    attn_other = low(contract_cols(rows_of(attended, 1 - core), out_all))
    attn_own = contract_cols(rows_of(attended, core), out_all)
    hidden_state = wide(tokens) + (attn_own + wide(swap_cores(attn_other)))
    normed_two = norm(hidden_state, gain_two)

    normed_near = links.gather_near(normed_two)
    upstream_near = fence(upstream_near, [normed_two])
    (units_own,) = fence([units_own], upstream_near)
    units_other = swap_cores(units_own)
    *normed_near, units_other = fence([*normed_near, units_other])
    normed_far = links.gather_far(*normed_near)
    down_all, gate_up_all = links.place_units(units_own, units_other, [units // 2])
    normed_far = fence(normed_far, [down_all, gate_up_all])
    normed = place_tokens(normed_two, *normed_near, *normed_far)

    upstream_near = fence(upstream_near, normed_far)
    upstream_far = links.gather_far(*upstream_near)
    gate_up = gate_and_up(normed, gate_up_all)
    upstream = place_tokens(cotangent_late, *upstream_near, *upstream_far)
    inner, grads = hidden(upstream, down_all, gate_up)
    half = rows // 2
    back_far = across(grads, gate_up_all, 3 * rows, (half, half))
    back_far_sent = links.sum_far(*back_far)
    back_own, back_one, back_two = across(
        grads, gate_up_all, 0, (rows, rows, rows), [back_far[0]]
    )
    one_send, two_send = join_sends(back_one, back_two, *back_far_sent, [back_own])
    back_sent = [links.swap(one_send, 1), links.swap(two_send, 2)]
    down_keep, down_give, gate_up_keep, gate_up_give = unit_grads(
        upstream, inner, normed, grads, weight_rows // 2, [one_send, two_send]
    )
    hidden_grad, attn_grad_low, gain_two_grad = norm_back(
        [back_own, *back_sent], hidden_state, gain_two, cotangent, [down_keep]
    )
    attn_grad_other = swap_cores(attn_grad_low)
    down_other = swap_cores(down_give)
    gate_up_other = swap_cores(gate_up_give)
    ffn_own, one_top, one_low, two_top, two_low, *ffn_far = across(
        inner, down_all, 0, (rows, *[half] * 6), [attn_grad_low]
    )
    ffn_far_sent = links.sum_far(*ffn_far)
    ffn_near = [links.swap(one_top, 1), links.swap(two_low, 2)]
    unit_sums = add_low([(down_keep, down_other), (gate_up_keep, gate_up_other)], [ffn_own])
    units_sum = links.sum_planes(unit_sums)

    attn_grad_all = order_rows(attn_grad_low, attn_grad_other)
    attended_grad = plain(attn_grad_all, out_all, [ffn_own])
    out_own, one_top, one_low_out, two_top_out, two_low_out, *out_far = links.corners(
        inner_rows(attn_grad_all, attended, [attended_grad, unit_sums])
    )
    out_far_sent = links.sum_far(*out_far)
    out_top = links.sum_top(one_top, two_low_out)
    nothing = jnp.zeros((2 * rows, 2 * LANES), LOW)
    query_back_one, rest_back = attend_back(
        into,
        attended_grad,
        totals_one,
        cosine,
        sine,
        segment,
        nothing,
        0,
        [*ffn_far_sent, *ffn_near, *out_far],
    )
    out_low = links.sum_low(one_low_out, two_top_out, *out_far_sent, [rest_back])
    query_back_two, rest_back = attend_back(
        into, attended_grad, totals_two, cosine, sine, segment, rest_back, 1, out_top
    )
    into_back = jnp.concatenate([query_back_one, query_back_two, rest_back], axis=1)
    into_own, into_one_top, into_one_low, into_two_top, into_two_low, *into_far = links.corners(
        inner_rows(normed_one_all, into_back, out_low)
    )
    into_far_sent = links.sum_far(*into_far)
    into_top = links.sum_top(into_one_top, into_two_low)
    out_sent = [
        jnp.concatenate([out_top[0], out_low[0]], axis=0),
        jnp.concatenate([out_low[1], out_top[1]], axis=0),
    ]
    (normed_part,) = across(into_back, into_all, 0, (2 * rows,), into_far)
    out_sums = wide(out_own) + wide(out_sent[0]) + wide(out_sent[1])
    out_shard = links.ring_start(out_sums, weight_rows)
    out_shard = links.ring_step(out_shard, out_sums, weight_rows, 1)
    into_low = links.sum_low(
        into_one_low, into_two_top, *into_far_sent, [normed_part, *into_top]
    )
    normed_own, normed_other = part_rows(normed_part, into_far_sent)
    input_grad, _, gain_one_grad = norm_back(
        [normed_own, swap_cores(normed_other)], tokens, gain_one, hidden_grad
    )
    gains_part = jnp.concatenate([gain_one_grad, gain_two_grad], axis=0)
    gains_part = gains_part + swap_cores(gains_part)
    for step in range(2, steps):
        out_shard = links.ring_step(out_shard, out_sums, weight_rows, step)
    into_low = hold(into_low, [gains_part])
    into_sent = [
        jnp.concatenate([into_top[0], into_low[0]], axis=0),
        jnp.concatenate([into_low[1], into_top[1]], axis=0),
    ]
    into_sums = wide(into_own) + wide(into_sent[0]) + wide(into_sent[1])
    into_shard = links.ring_start(into_sums, weight_rows)
    into_shard = links.ring_step(into_shard, into_sums, weight_rows, 1)
    (gains_part,) = hold([gains_part], into_low)
    gains_level = gains_part
    for block in [links.shift(gains_part, step) for step in range(1, steps)]:
        gains_level = gains_level + block
    one_send, two_send = hold(
        [low(wide(one_low) + wide(ffn_far_sent[1])), low(wide(two_top) + wide(ffn_far_sent[0]))],
        into_low,
    )
    ffn_low = [links.swap(one_send, 1), links.swap(two_send, 2)]
    units_back = links.return_units(units_sum, ffn_low)
    for step in range(2, steps):
        if step == steps - 1:
            (into_shard,) = hold([into_shard], [gains_level, *ffn_low])
        into_shard = links.ring_step(into_shard, into_sums, weight_rows, step)
    gains_others = [links.swap(gains_level, other) for other in (1, 2, 3)]
    gains_shard = links.own_gains(gains_level + gains_others[0] + gains_others[1] + gains_others[2])
    down_shard, gate_shard, up_shard = links.join_units(units_back, 3)
    ffn_sum = jnp.concatenate(
        [
            wide(ffn_near[0]) + wide(ffn_low[1]),
            wide(ffn_low[0]) + wide(ffn_near[1]),
        ],
        axis=0,
    )
    activations = low(hidden_state + (wide(ffn_own) + ffn_sum))
    query_shard = into_shard[:, :query_cols]
    key_shard = into_shard[:, query_cols : query_cols + key_cols]
    value_shard = into_shard[:, query_cols + key_cols :]
    q_all = adam(query_weight, query_shard, query_moment, query_square, RATE_MAIN, DECAY_RATE)
    k_all = adam(key_weight, key_shard, key_moment, key_square, RATE_MAIN, DECAY_RATE)
    v_all = adam(value_weight, value_shard, value_moment, value_square, RATE_MAIN, DECAY_RATE)
    o_all = adam(out_weight, out_shard, out_moment, out_square, RATE_OUT, DECAY_RATE)
    g_all = adam(gate_weight, gate_shard, gate_moment, gate_square, RATE_MAIN, DECAY_RATE)
    u_all = adam(up_weight, up_shard, up_moment, up_square, RATE_MAIN, DECAY_RATE)
    d_all = adam(down_weight, down_shard, down_moment, down_square, RATE_DOWN, DECAY_RATE)
    n_all = adam(norm_gains, gains_shard, gains_moment, gains_square, RATE_GAINS, 0.0)
    return (
        activations,
        input_grad,
        q_all[0],
        q_all[1],
        q_all[2],
        q_all[3],
        k_all[0],
        k_all[1],
        k_all[2],
        k_all[3],
        v_all[0],
        v_all[1],
        v_all[2],
        v_all[3],
        o_all[0],
        o_all[1],
        o_all[2],
        o_all[3],
        g_all[0],
        g_all[1],
        g_all[2],
        g_all[3],
        u_all[0],
        u_all[1],
        u_all[2],
        u_all[3],
        d_all[0],
        d_all[1],
        d_all[2],
        d_all[3],
        n_all[0],
        n_all[1],
        n_all[2],
        n_all[3],
    )


def solution(mesh):
    in_specs = (
        P(("dp", "tensor"), None),
        P(("dp", "tensor"), None),
        P("dp", None),
        P("dp", "tensor"),
        P("dp", "tensor"),
        P("dp", "tensor"),
        P("dp", "tensor"),
        P("dp", "tensor"),
        P("dp", "tensor"),
        P("dp", "tensor"),
        P(None, "dp"),
        P("dp", "tensor"),
        P("dp", "tensor"),
        P("dp", "tensor"),
        P("dp", "tensor"),
        P("dp", "tensor"),
        P("dp", "tensor"),
        P("dp", "tensor"),
        P(None, "dp"),
        P("dp", "tensor"),
        P("dp", "tensor"),
        P("dp", "tensor"),
        P("dp", "tensor"),
        P("dp", "tensor"),
        P("dp", "tensor"),
        P("dp", "tensor"),
        P(None, "dp"),
    )
    out_specs = (
        P(("dp", "tensor"), None),
        P(("dp", "tensor"), None),
        P("dp", "tensor"),
        P("dp", "tensor"),
        P("dp", "tensor"),
        P("dp", "tensor"),
        P("dp", "tensor"),
        P("dp", "tensor"),
        P("dp", "tensor"),
        P("dp", "tensor"),
        P("dp", "tensor"),
        P("dp", "tensor"),
        P("dp", "tensor"),
        P("dp", "tensor"),
        P("dp", "tensor"),
        P("dp", "tensor"),
        P("dp", "tensor"),
        P("dp", "tensor"),
        P("dp", "tensor"),
        P("dp", "tensor"),
        P("dp", "tensor"),
        P("dp", "tensor"),
        P("dp", "tensor"),
        P("dp", "tensor"),
        P("dp", "tensor"),
        P("dp", "tensor"),
        P("dp", "tensor"),
        P("dp", "tensor"),
        P("dp", "tensor"),
        P("dp", "tensor"),
        P(None, "dp"),
        P(None, "dp"),
        P(None, "dp"),
        P(None, "dp"),
    )
    links = Links(mesh.shape["dp"])
    return jax.shard_map(functools.partial(shards, links), mesh=mesh, in_specs=in_specs, out_specs=out_specs, check_vma=False)
```

time: 855 us -> 739 us (0.86)
  Pallas kernels: 79.2 us -> 282 us
  matrix products: 171 us -> 8.43 us
  waiting for transfers between devices: 298 us -> 203 us
  other arithmetic: 87.6 us -> 33.5 us
  local copies, waits for them, and re-layouts: 100 us -> 78 us
  starting transfers between devices: 91.7 us -> 109 us
    pallas_call x13 -> x54, Pallas kernels: 79.2 us -> 282 us  [the longest x28 255 us: call(): pl.pallas_call(functools.partial(late, kernel, (len(operands), len(waits)...]
    dot_general x9 -> x0, matrix products: 106 us -> none  [the longest x5 50.3 us: contract_rows(): lax.dot_general(left, right, (((0,), (0,)), ((), ())), preferred_element_...]
    ppermute x48 -> x54, waiting for transfers between devices: 232 us -> 139 us  [swap(): return lax.ppermute(block, 'dp', self.pairs[step])]
    dot_general x7 -> x2, matrix products: 64.1 us -> 8.24 us  [contract_cols(): lax.dot_general(left, right, (((1,), (1,)), ((), ())), preferred_element_...]
    convert_element_type x17 -> x12, other arithmetic: 26.6 us -> 4.57 us  [low(): return block.astype(LOW)]
    unnamed x215 -> x264, local copies, waits for them, and re-layouts: 51.7 us -> 69.8 us
    ppermute x0 -> x6, starting transfers between devices: none -> 15.7 us  [shift(): return lax.ppermute(block, 'dp', pairs)]
    slice x17 -> x16, local copies, waits for them, and re-layouts: 18.9 us -> 7.1 us  [the longest x10 6.76 us: gather_far(): return [self.swap(second[:half], 1), self.swap(first[half:], 2)]]
  transfers between devices with their start and end apart: 84 -> 84, of which waited for: 34 -> 33; matrix products, arithmetic and copies ran while one was open for 31% -> 5% of each run, Pallas kernels for 9% -> 34%
where the time goes in v2:
time: 739 us; the launch traced here: 731 us
  Pallas kernels  282 us (38%)
  waiting for transfers between devices  203 us (27%)
  starting transfers between devices  109 us (15%)
  local copies, waits for them, and re-layouts  78 us (11%)
  other arithmetic  33.5 us (5%)
  between operations  16.3 us (2%)
  matrix products  8.43 us (1%)
    pallas_call x28, Pallas kernels, call(): pl.pallas_call(functools.partial(late, kernel, (len(operands), len(waits)...  255 us
    ppermute x54, waiting for transfers between devices, swap(): return lax.ppermute(block, 'dp', self.pairs[step])  139 us
    unnamed x264, local copies, waits for them, and re-layouts  69.8 us
    ppermute x54, starting transfers between devices, swap(): return lax.ppermute(block, 'dp', self.pairs[step])  62.7 us
    ppermute x12, waiting for transfers between devices, turn(): return lax.ppermute(block, 'dp', self.ring)  52.7 us
    ppermute x12, starting transfers between devices, turn(): return lax.ppermute(block, 'dp', self.ring)  29.7 us
    ppermute x6, starting transfers between devices, shift(): return lax.ppermute(block, 'dp', pairs)  15.7 us
  transfers between devices with their start and end apart: 84, of which 33 were waited for; matrix products, arithmetic and copies ran while one was open for 5% of the time, Pallas kernels for 34%

profile of v2, /device:TPU:0, one launch (start us, length us, event | category | flops | bytes accessed | tf_op | source)
XLA Modules:
  0.0 731.0 jit_solution(9441943678389974346)
XLA Ops:
  21.2 9.7 %collective-permute-done.4.refs_2_ = bf16[128,1280]{1,0:T(8,128)(2,1)S(1)} collective-permute-done((bf16[128,1280]{1,0:T(8,128)(2,1)S(1)}, bf16[128,1280]{1,0:T(8,128)(2,1)S(1)}, u32[]{:S(2)}, u32[]{:S(2)}) %collective-permute-start.4) | collective-permute-done | bytes 327712 | tf_op jit(solution)/shard_map/ppermute | solution.py:924
  35.0 6.0 collective-permute-done.13
  41.1 5.6 collective-permute-done.14.refs_0_
  46.7 10.5 %collective-permute-done.15.refs_1_ = bf16[1,64,4224]{2,1,0:T(8,128)(2,1)S(1)} collective-permute-done((bf16[1,64,4224]{2,1,0:T(8,128)(2,1)S(1)}, bf16[1,64,4224]{2,1,0:T(8,128)(2,1)S(1)}, u32[]{:S(2)}, u32[]{:S(2)}) %collective-permute-start.15) | collective-permute-done | bytes 540704 | tf_op jit(solution)/shard_map/ppermute | solution.py:921
  76.8 9.8 %collective-permute-done.10.refs_1_ = bf16[256,1280]{1,0:T(8,128)(2,1)S(1)} collective-permute-done((bf16[256,1280]{1,0:T(8,128)(2,1)S(1)}, bf16[256,1280]{1,0:T(8,128)(2,1)S(1)}, u32[]{:S(2)}, u32[]{:S(2)}) %collective-permute-start.10) | collective-permute-done | bytes 655392 | tf_op jit(solution)/shard_map/ppermute | solution.py:921
  91.8 6.2 collective-permute-start.24
  98.0 3.9 collective-permute-done.18.refs_2_
  101.9 6.3 collective-permute-done.11.refs_0_
  115.0 3.9 collective-permute-done.20.refs_0_
  135.6 7.7 %shard_map.530.refs_0_.refs_1_.refs_2_ = bf16[768,1280]{1,0:T(8,128)(2,1)S(1)} custom-call(bf16[768,2048]{1,0:T(8,128)(2,1)S(1)} %bitcast.137, bf16[2048,1280]{1,0:T(8,128)(2,1)} %bitcast.139, f32[768,128]{1,0:T(8,128)S(1)} %copy-done.38, f32[768,128]{1,0:T(8,128)S(1)} %copy-done.41), custom_call_target="tpu_custom_call" | custom-call | flops 1024 | bytes 1024 | tf_op jit(solution)/shard_map/pallas_call | solution.py:85
  143.3 12.3 %shard_map.531 = (bf16[768,512]{1,0:T(8,128)(2,1)S(1)}, f32[768,128]{1,0:T(8,128)S(1)}) custom-call(bf16[768,1280]{1,0:T(8,128)(2,1)S(1)} %shard_map.530.refs_0_.refs_1_.refs_2_, bf16[768,1280]{1,0:T(8,128)(2,1)S(1)} %shard_map.530.refs_0_.refs_1_.refs_2_, bf16[768,1280]{1,0:T(8,128)(2,1)S(1)} %shard_map.530.refs_0_.refs_1_.refs_2_, ...), custom_call_target="tpu_custom_call" | custom-call | flops 1024 | bytes 1024 | tf_op jit(solution)/shard_map/pallas_call | solution.py:85
  164.8 12.4 %shard_map.534 = (bf16[768,512]{1,0:T(8,128)(2,1)S(1)}, f32[768,128]{1,0:T(8,128)S(1)}) custom-call(bf16[768,1280]{1,0:T(8,128)(2,1)S(1)} %shard_map.530.refs_0_.refs_1_.refs_2_, bf16[768,1280]{1,0:T(8,128)(2,1)S(1)} %shard_map.530.refs_0_.refs_1_.refs_2_, bf16[768,1280]{1,0:T(8,128)(2,1)S(1)} %shard_map.530.refs_0_.refs_1_.refs_2_, ...), custom_call_target="tpu_custom_call" | custom-call | flops 1024 | bytes 1024 | tf_op jit(solution)/shard_map/pallas_call | solution.py:85
  187.3 5.2 add_add_fusion.refs_0_.refs_3_
  194.2 26.3 %collective-permute-done.30.refs_0_ = bf16[384,2048]{1,0:T(8,128)(2,1)S(1)} collective-permute-done((bf16[384,2048]{1,0:T(8,128)(2,1)}, bf16[384,2048]{1,0:T(8,128)(2,1)S(1)}, u32[]{:S(2)}, u32[]{:S(2)}) %collective-permute-start.30) | collective-permute-done | bytes 1572896 | tf_op jit(solution)/shard_map/ppermute | solution.py:921
  224.7 3.5 copy-done.2
  234.5 33.8 %collective-permute-done.32.refs_0_ = bf16[384,2048]{1,0:T(8,128)(2,1)S(1)} collective-permute-done((bf16[384,2048]{1,0:T(8,128)(2,1)S(1)}, bf16[384,2048]{1,0:T(8,128)(2,1)S(1)}, u32[]{:S(2)}, u32[]{:S(2)}) %collective-permute-start.32) | collective-permute-done | bytes 1572896 | tf_op jit(solution)/shard_map/ppermute | solution.py:921
  276.8 3.5 copy-done.4
  280.3 3.5 copy-done.6
  286.0 7.0 collective-permute-done.35.refs_0_
  304.1 25.1 %shard_map.548.refs_2_ = f32[1536,2816]{1,0:T(8,128)} custom-call(bf16[1536,2048]{1,0:T(8,128)(2,1)} %bitcast.149, bf16[2048,2816]{1,0:T(8,128)(2,1)} %bitcast.144), custom_call_target="tpu_custom_call" | custom-call | flops 34359738368 | bytes 1048576 | tf_op jit(solution)/shard_map/pallas_call | solution.py:85
  333.9 19.0 %shard_map.549 = (bf16[1536,1408]{1,0:T(8,128)(2,1)S(1)}, bf16[1536,2816]{1,0:T(8,128)(2,1)}) custom-call(bf16[1536,2048]{1,0:T(8,128)(2,1)} %bitcast.151, bf16[2048,1408]{1,0:T(8,128)(2,1)} %bitcast.155, f32[1536,2816]{1,0:T(8,128)} %shard_map.548.refs_2_), custom_call_target="tpu_custom_call" | custom-call | flops 34359738368 | bytes 1048576 | tf_op jit(solution)/shard_map/pallas_call | solution.py:85
  352.8 10.0 %shard_map.550 = (bf16[192,2048]{1,0:T(8,128)(2,1)S(1)}, bf16[192,2048]{1,0:T(8,128)(2,1)S(1)}) custom-call(bf16[1536,2816]{1,0:T(8,128)(2,1)} %get-tuple-element.160.refs_0_.refs_4_, bf16[2048,2816]{1,0:T(8,128)(2,1)} %bitcast.145), custom_call_target="tpu_custom_call" | custom-call | flops 34359738368 | bytes 1048576 | tf_op jit(solution)/shard_map/pallas_call | solution.py:85
  364.1 18.3 %shard_map.551 = (bf16[384,2048]{1,0:T(8,128)(2,1)S(1)}, bf16[384,2048]{1,0:T(8,128)(2,1)S(1)}, bf16[384,2048]{1,0:T(8,128)(2,1)S(1)}) custom-call(bf16[1536,2816]{1,0:T(8,128)(2,1)} %get-tuple-element.160.refs_0_.refs_4_, bf16[2048,2816]{1,0:T(8,128)(2,1)} %bitcast.146, bf16[192,2048]{1,0:T(8,128)(2,1)S(1)} %get-tuple-element.161.refs_2_), custom_call_target="tpu_custom_call" | custom-call | flops 34359738368 | bytes 1048576 | tf_op jit(solution)/shard_map/pallas_call | solution.py:85
  391.8 38.4 %shard_map.553 = (bf16[16,64,1408]{2,1,0:T(8,128)(2,1)S(1)}, bf16[16,64,1408]{2,1,0:T(8,128)(2,1)}, bf16[16,64,2816]{2,1,0:T(8,128)(2,1)}, bf16[16,64,2816]{2,1,0:T(8,128)(2,1)}) custom-call(s32[1]{0:T(128)} %bitcast.refs_0_, bf16[1536,2048]{1,0:T(8,128)(2,1)} %bitcast.152, bf16[1536,1408]{1,0:T(8,128)(2,1)} %copy-done.88, bf16[1536,2048]{1,0:T(8,128)(2,1)} %bitcast.150, ...), custom_call_target="tpu_custom_call" | custom-call | flops 34359738368 | bytes 1048576 | tf_op jit(solution)/shard_map/pallas_call | solution.py:85
  433.4 6.2 shard_map.554
  440.8 14.7 %shard_map.555 = (bf16[384,2048]{1,0:T(8,128)(2,1)}, bf16[192,2048]{1,0:T(8,128)(2,1)}, bf16[192,2048]{1,0:T(8,128)(2,1)S(1)}, bf16[192,2048]{1,0:T(8,128)(2,1)S...) custom-call(bf16[1536,1408]{1,0:T(8,128)(2,1)} %copy-done.88, ...), custom_call_target="tpu_custom_call" | custom-call | flops 34359738368 | bytes 1048576 | tf_op jit(solution)/shard_map/pallas_call | solution.py:85
  462.9 6.7 shard_map.557.refs_2_.refs_3_
  472.2 9.0 %shard_map.558.refs_3_ = bf16[16,64,4224]{2,1,0:T(8,128)(2,1)} custom-call(bf16[16,64,1408]{2,1,0:T(8,128)(2,1)S(1)} %copy-done.18, bf16[16,64,1408]{2,1,0:T(8,128)(2,1)} %collective-permute-done.48.refs_1_, bf16[16,64,2816]{2,1,0:T(8,128)(2,1)} %get-tuple-element.179.refs_2_, bf16[16,64,2816]{2,1,0:T(8,128)(2,1)} %collective-permute-done.49.refs_3_, ...), custom_call_target="tpu_custom_call" | custom-call | flops 1024 | bytes 1024 | tf_op jit(solution)/shard_map/pallas_call | solution.py:85
  484.0 8.7 %shard_map.559 = bf16[2048,1024]{1,0:T(8,128)(2,1)} custom-call(bf16[768,2048]{1,0:T(8,128)(2,1)} %bitcast.165, bf16[768,1024]{1,0:T(8,128)(2,1)S(1)} %copy-done.78, bf16[768,1024]{1,0:T(8,128)(2,1)S(1)} %copy-done.90, bf16[16,64,4224]{2,1,0:T(8,128)(2,1)} %shard_map.558.refs_3_), custom_call_target="tpu_custom_call" | custom-call | flops 34359738368 | bytes 1048576 | tf_op jit(solution)/shard_map/pallas_call | solution.py:85
  492.7 3.5 shard_map.560
  500.5 19.0 %shard_map.561 = (bf16[768,512]{1,0:T(8,128)(2,1)S(1)}, bf16[768,256]{1,0:T(8,128)(2,1)S(1)}) custom-call(bf16[768,1280]{1,0:T(8,128)(2,1)} %copy-done, bf16[768,1280]{1,0:T(8,128)(2,1)} %copy-done, bf16[768,1280]{1,0:T(8,128)(2,1)} %copy-done, bf16[768,1024]{1,0:T(8,128)(2,1)} %copy-done.89, f32[768,128]{1,0:T(8,128)S(1)} %copy-done.85, ...), custom_call_target="tpu_custom_call" | custom-call | flops 34359738368 | bytes 1048576 | tf_op jit(solution)/shard_map/pallas_call | solution.py:85
  523.1 19.4 %shard_map.562 = (bf16[768,512]{1,0:T(8,128)(2,1)S(1)}, bf16[768,256]{1,0:T(8,128)(2,1)S(1)}) custom-call(bf16[768,1280]{1,0:T(8,128)(2,1)} %copy-done, bf16[768,1280]{1,0:T(8,128)(2,1)} %copy-done, bf16[768,1280]{1,0:T(8,128)(2,1)} %copy-done, bf16[768,1024]{1,0:T(8,128)(2,1)S(1)} %copy-done.91, f32[768,128]{1,0:T(8,128)S(1)} %copy-done.87, ...), custom_call_target="tpu_custom_call" | custom-call | flops 34359738368 | bytes 1048576 | tf_op jit(solution)/shard_map/pallas_call | solution.py:85
  542.7 7.3 %shard_map.564 = bf16[2048,1280]{1,0:T(8,128)(2,1)} custom-call(bf16[768,2048]{1,0:T(8,128)(2,1)S(1)} %bitcast.138, bf16[768,1280]{1,0:T(8,128)(2,1)S(1)} %constant_dynamic-update-slice_fusion.4.refs_1_.refs_0_, bf16[256,1024]{1,0:T(8,128)(2,1)S(1)} %collective-permute-done.54.refs_2_, bf16[256,1024]{1,0:T(8,128)(2,1)S(1)} %collective-permute-done.55.refs_3_), custom_call_target="tpu_custom_call" | custom-call | flops 34359738368 | bytes 1048576 | tf_op jit(solution)/shard_map/pallas_call | solution.py:85
  550.1 3.9 shard_map.565
  557.7 7.7 %shard_map.566.refs_4_ = bf16[768,2048]{1,0:T(8,128)(2,1)} custom-call(bf16[768,1280]{1,0:T(8,128)(2,1)S(1)} %constant_dynamic-update-slice_fusion.4.refs_1_.refs_0_, bf16[2048,1280]{1,0:T(8,128)(2,1)} %bitcast.140, bf16[256,1280]{1,0:T(8,128)(2,1)S(1)} %bitcast.192, bf16[256,1280]{1,0:T(8,128)(2,1)S(1)} %bitcast.194), custom_call_target="tpu_custom_call" | custom-call | flops 34359738368 | bytes 1048576 | tf_op jit(solution)/shard_map/pallas_call | solution.py:85
  565.4 3.5 collective-permute-done.56.refs_2_.refs_3_
  576.5 13.6 %collective-permute-done.72 = bf16[128,1024]{1,0:T(8,128)(2,1)S(1)} collective-permute-done((bf16[128,1024]{1,0:T(8,128)(2,1)S(1)}, bf16[128,1024]{1,0:T(8,128)(2,1)S(1)}, u32[]{:S(2)}, u32[]{:S(2)}) %collective-permute-start.72) | collective-permute-done | bytes 262176 | tf_op jit(solution)/shard_map/ppermute | solution.py:924
  590.2 7.0 collective-permute-start.73
  601.4 6.1 shard_map.569
  607.7 4.2 collective-permute-done.73
  613.0 3.8 collective-permute-start.74
  616.9 5.6 collective-permute-start.68
  628.6 6.9 collective-permute-done.68
  637.7 8.6 %collective-permute-start.66 = (bf16[128,1280]{1,0:T(8,128)(2,1)S(1)}, bf16[128,1280]{1,0:T(8,128)(2,1)S(1)}, u32[]{:S(2)}, u32[]{:S(2)}) collective-permute-start(bf16[128,1280]{1,0:T(8,128)(2,1)S(1)} %dynamic-slice_convert_fusion), channel_id=1, source_target_pairs={{0,8},{2,10},{4,12},{6,14},{8,16},{10,18},{12,20},{14,22},{16,24},... | collective-permute-start | bytes 983048 | tf_op jit(solution)/shard_map/ppermute | solution.py:924
  647.0 10.8 %collective-permute-done.66 = bf16[128,1280]{1,0:T(8,128)(2,1)S(1)} collective-permute-done((bf16[128,1280]{1,0:T(8,128)(2,1)S(1)}, bf16[128,1280]{1,0:T(8,128)(2,1)S(1)}, u32[]{:S(2)}, u32[]{:S(2)}) %collective-permute-start.66) | collective-permute-done | bytes 327712 | tf_op jit(solution)/shard_map/ppermute | solution.py:924
  667.0 6.1 collective-permute-done.67
  682.0 8.9 %collective-permute-done.75.refs_1_ = bf16[1,64,4224]{2,1,0:T(8,128)(2,1)S(1)} collective-permute-done((bf16[1,64,4224]{2,1,0:T(8,128)(2,1)S(1)}, bf16[1,64,4224]{2,1,0:T(8,128)(2,1)S(1)}, u32[]{:S(2)}, u32[]{:S(2)}) %collective-permute-start.75) | collective-permute-done | bytes 540704 | tf_op jit(solution)/shard_map/ppermute | solution.py:921
  690.9 10.1 %collective-permute-done.76.refs_2_ = bf16[1,64,4224]{2,1,0:T(8,128)(2,1)S(1)} collective-permute-done((bf16[1,64,4224]{2,1,0:T(8,128)(2,1)S(1)}, bf16[1,64,4224]{2,1,0:T(8,128)(2,1)S(1)}, u32[]{:S(2)}, u32[]{:S(2)}) %collective-permute-start.76) | collective-permute-done | bytes 540704 | tf_op jit(solution)/shard_map/ppermute | solution.py:921
  (523 shorter events, 225.5 us)
Async XLA Ops:
  7.2 217.5 %all-gather.2.cloned.1.call-start = ((), (), s32[]{:S(2)}) async-start(), calls=%async_computation.1 | async-start | bytes 10813440 | tf_op jit(solution)/shard_map/all_gather | solution.py:1015
  12.0 18.9 %collective-permute-start.3 = (bf16[2,64,4224]{2,1,0:T(8,128)(2,1)}, bf16[2,64,4224]{2,1,0:T(8,128)(2,1)S(1)}, u32[]{:S(2)}, u32[]{:S(2)}) collective-permute-start(bf16[2,64,4224]{2,1,0:T(8,128)(2,1)} %get-tuple-element.259), channel_id=1, source_target_pairs={{0,1},{1,0},{2,3},{3,2},{4,5},{5,4},{6,7},{7,6},{8,9},{9,8},{10,11... | collective-permute-start | bytes 3244040 | tf_op jit(solution)/shard_map/ppermute | solution.py:75
  33.0 24.2 %collective-permute-start.15 = (bf16[1,64,4224]{2,1,0:T(8,128)(2,1)S(1)}, bf16[1,64,4224]{2,1,0:T(8,128)(2,1)S(1)}, u32[]{:S(2)}, u32[]{:S(2)}) collective-permute-start(bf16[1,64,4224]{2,1,0:T(8,128)(2,1)S(1)} %get-tuple-element.256), channel_id=1, source_target_pairs={{0,4},{2,6},{4,0},{6,2},{8,12},{10,14},{12,8},{14,10},{16,20},{18,... | collective-permute-start | bytes 1622024 | tf_op jit(solution)/shard_map/ppermute | solution.py:921
  34.5 22.7 %collective-permute-start.16 = (bf16[1,64,4224]{2,1,0:T(8,128)(2,1)S(1)}, bf16[1,64,4224]{2,1,0:T(8,128)(2,1)S(1)}, u32[]{:S(2)}, u32[]{:S(2)}) collective-permute-start(bf16[1,64,4224]{2,1,0:T(8,128)(2,1)S(1)} %get-tuple-element.255), channel_id=1, source_target_pairs={{0,6},{2,4},{4,2},{6,0},{8,14},{10,12},{12,10},{14,8},{16,22},{18,... | collective-permute-start | bytes 1622024 | tf_op jit(solution)/shard_map/ppermute | solution.py:921
  59.2 614.1 %reduce-scatter.2.cloned.1.call-start = ((), (), s32[]{:S(2)}) async-start(), calls=%async_computation.2 | async-start | bytes 10813440 | tf_op jit(solution)/shard_map/reduce_scatter | solution.py:1023
  71.1 30.8 %collective-permute-start.18 = (bf16[256,1280]{1,0:T(8,128)(2,1)S(1)}, bf16[256,1280]{1,0:T(8,128)(2,1)S(1)}, u32[]{:S(2)}, u32[]{:S(2)}) collective-permute-start(bf16[256,1280]{1,0:T(8,128)(2,1)S(1)} %constant_dynamic-update-slice_fusion), channel_id=1, source_target_pairs={{0,2},{2,0},{4,6},{6,4},{8,10},{10,8},{12,14},{14,12},{16,18},{18,... | collective-permute-start | bytes 1966088 | tf_op jit(solution)/shard_map/ppermute | solution.py:921
  72.4 29.4 %collective-permute-start.19 = (bf16[256,1280]{1,0:T(8,128)(2,1)S(1)}, bf16[256,1280]{1,0:T(8,128)(2,1)S(1)}, u32[]{:S(2)}, u32[]{:S(2)}) collective-permute-start(bf16[256,1280]{1,0:T(8,128)(2,1)S(1)} %constant_dynamic-update-slice_fusion), channel_id=1, source_target_pairs={{0,4},{2,6},{4,0},{6,2},{8,12},{10,14},{12,8},{14,10},{16,20},{18,... | collective-permute-start | bytes 1966088 | tf_op jit(solution)/shard_map/ppermute | solution.py:921
  87.9 20.3 %collective-permute-start.11 = (bf16[128,1280]{1,0:T(8,128)(2,1)S(1)}, bf16[128,1280]{1,0:T(8,128)(2,1)S(1)}, u32[]{:S(2)}, u32[]{:S(2)}) collective-permute-start(bf16[128,1280]{1,0:T(8,128)(2,1)S(1)} %slice.111), channel_id=1, source_target_pairs={{0,2},{2,0},{4,6},{6,4},{8,10},{10,8},{12,14},{14,12},{16,18},{18,... | collective-permute-start | bytes 983048 | tf_op jit(solution)/shard_map/ppermute | solution.py:921
  88.8 19.4 %collective-permute-start.12 = (bf16[128,1280]{1,0:T(8,128)(2,1)S(1)}, bf16[128,1280]{1,0:T(8,128)(2,1)S(1)}, u32[]{:S(2)}, u32[]{:S(2)}) collective-permute-start(bf16[128,1280]{1,0:T(8,128)(2,1)S(1)} %slice.112), channel_id=1, source_target_pairs={{0,4},{2,6},{4,0},{6,2},{8,12},{10,14},{12,8},{14,10},{16,20},{18,... | collective-permute-start | bytes 983048 | tf_op jit(solution)/shard_map/ppermute | solution.py:921
  91.8 21.1 %collective-permute-start.24 = (bf16[128,1024]{1,0:T(8,128)(2,1)S(1)}, bf16[128,1024]{1,0:T(8,128)(2,1)S(1)}, u32[]{:S(2)}, u32[]{:S(2)}) collective-permute-start(bf16[128,1024]{1,0:T(8,128)(2,1)S(1)} %collective-permute-done.23), channel_id=1, source_target_pairs={{0,8},{2,10},{4,12},{6,14},{8,16},{10,18},{12,20},{14,22},{16,24},... | collective-permute-start | bytes 786440 | tf_op jit(solution)/shard_map/ppermute | solution.py:924
  121.0 35.4 %collective-permute-start.25 = (bf16[512,1024]{1,0:T(8,128)(2,1)}, bf16[512,1024]{1,0:T(8,128)(2,1)S(1)}, u32[]{:S(2)}, u32[]{:S(2)}) collective-permute-start(bf16[512,1024]{1,0:T(8,128)(2,1)} %shard_map.532), channel_id=1, source_target_pairs={{0,2},{2,0},{4,6},{6,4},{8,10},{10,8},{12,14},{14,12},{16,18},{18,... | collective-permute-start | bytes 3145736 | tf_op jit(solution)/shard_map/ppermute | solution.py:921
  122.1 34.2 %collective-permute-start.26 = (bf16[512,1024]{1,0:T(8,128)(2,1)}, bf16[512,1024]{1,0:T(8,128)(2,1)}, u32[]{:S(2)}, u32[]{:S(2)}) collective-permute-start(bf16[512,1024]{1,0:T(8,128)(2,1)} %shard_map.532), channel_id=1, source_target_pairs={{0,4},{2,6},{4,0},{6,2},{8,12},{10,14},{12,8},{14,10},{16,20},{18,... | collective-permute-start | bytes 3145736 | tf_op jit(solution)/shard_map/ppermute | solution.py:921
  183.5 37.0 %collective-permute-start.30 = (bf16[384,2048]{1,0:T(8,128)(2,1)}, bf16[384,2048]{1,0:T(8,128)(2,1)S(1)}, u32[]{:S(2)}, u32[]{:S(2)}) collective-permute-start(bf16[384,2048]{1,0:T(8,128)(2,1)} %get-tuple-element.144), channel_id=1, source_target_pairs={{0,2},{2,0},{4,6},{6,4},{8,10},{10,8},{12,14},{14,12},{16,18},{18,... | collective-permute-start | bytes 4718600 | tf_op jit(solution)/shard_map/ppermute | solution.py:921
  184.6 36.7 %collective-permute-start.31 = (bf16[384,2048]{1,0:T(8,128)(2,1)}, bf16[384,2048]{1,0:T(8,128)(2,1)S(1)}, u32[]{:S(2)}, u32[]{:S(2)}) collective-permute-start(bf16[384,2048]{1,0:T(8,128)(2,1)} %get-tuple-element.144), channel_id=1, source_target_pairs={{0,4},{2,6},{4,0},{6,2},{8,12},{10,14},{12,8},{14,10},{16,20},{18,... | collective-permute-start | bytes 4718600 | tf_op jit(solution)/shard_map/ppermute | solution.py:921
  228.2 41.3 %collective-permute-start.34 = (bf16[16,64,4224]{2,1,0:T(8,128)(2,1)S(1)}, bf16[16,64,4224]{2,1,0:T(8,128)(2,1)S(1)}, u32[]{:S(2)}, u32[]{:S(2)}) collective-permute-start(bf16[16,64,4224]{2,1,0:T(8,128)(2,1)S(1)} %shard_map.541.own_ref), channel_id=1, source_target_pairs={{0,1},{1,0},{2,3},{3,2},{4,5},{5,4},{6,7},{7,6},{8,9},{9,8},{10,11... | collective-permute-start | bytes 25952264 | tf_op jit(solution)/shard_map/ppermute | solution.py:75
  231.6 36.7 %collective-permute-start.32 = (bf16[384,2048]{1,0:T(8,128)(2,1)S(1)}, bf16[384,2048]{1,0:T(8,128)(2,1)S(1)}, u32[]{:S(2)}, u32[]{:S(2)}) collective-permute-start(bf16[384,2048]{1,0:T(8,128)(2,1)S(1)} %copy-done.14), channel_id=1, source_target_pairs={{0,2},{2,0},{4,6},{6,4},{8,10},{10,8},{12,14},{14,12},{16,18},{18,... | collective-permute-start | bytes 4718600 | tf_op jit(solution)/shard_map/ppermute | solution.py:921
  233.1 36.5 %collective-permute-start.33 = (bf16[384,2048]{1,0:T(8,128)(2,1)S(1)}, bf16[384,2048]{1,0:T(8,128)(2,1)S(1)}, u32[]{:S(2)}, u32[]{:S(2)}) collective-permute-start(bf16[384,2048]{1,0:T(8,128)(2,1)S(1)} %copy-done.14), channel_id=1, source_target_pairs={{0,4},{2,6},{4,0},{6,2},{8,12},{10,14},{12,8},{14,10},{16,20},{18,... | collective-permute-start | bytes 4718600 | tf_op jit(solution)/shard_map/ppermute | solution.py:921
  273.9 19.1 %collective-permute-start.35 = (bf16[192,2048]{1,0:T(8,128)(2,1)}, bf16[192,2048]{1,0:T(8,128)(2,1)}, u32[]{:S(2)}, u32[]{:S(2)}) collective-permute-start(bf16[192,2048]{1,0:T(8,128)(2,1)} %slice.119), channel_id=1, source_target_pairs={{0,2},{2,0},{4,6},{6,4},{8,10},{10,8},{12,14},{14,12},{16,18},{18,... | collective-permute-start | bytes 2359304 | tf_op jit(solution)/shard_map/ppermute | solution.py:921
  295.2 34.0 %collective-permute-start.37 = (bf16[192,2048]{1,0:T(8,128)(2,1)}, bf16[192,2048]{1,0:T(8,128)(2,1)S(1)}, u32[]{:S(2)}, u32[]{:S(2)}) collective-permute-start(bf16[192,2048]{1,0:T(8,128)(2,1)} %slice.121), channel_id=1, source_target_pairs={{0,2},{2,0},{4,6},{6,4},{8,10},{10,8},{12,14},{14,12},{16,18},{18,... | collective-permute-start | bytes 2359304 | tf_op jit(solution)/shard_map/ppermute | solution.py:921
  297.6 31.6 %collective-permute-start.38 = (bf16[192,2048]{1,0:T(8,128)(2,1)}, bf16[192,2048]{1,0:T(8,128)(2,1)S(1)}, u32[]{:S(2)}, u32[]{:S(2)}) collective-permute-start(bf16[192,2048]{1,0:T(8,128)(2,1)} %slice.122), channel_id=1, source_target_pairs={{0,4},{2,6},{4,0},{6,2},{8,12},{10,14},{12,8},{14,10},{16,20},{18,... | collective-permute-start | bytes 2359304 | tf_op jit(solution)/shard_map/ppermute | solution.py:921
  362.8 23.1 %collective-permute-start.39 = (bf16[192,2048]{1,0:T(8,128)(2,1)S(1)}, bf16[192,2048]{1,0:T(8,128)(2,1)S(1)}, u32[]{:S(2)}, u32[]{:S(2)}) collective-permute-start(bf16[192,2048]{1,0:T(8,128)(2,1)S(1)} %get-tuple-element.161.refs_2_), channel_id=1, source_target_pairs={{0,2},{2,0},{4,6},{6,4},{8,10},{10,8},{12,14},{14,12},{16,18},{18,... | collective-permute-start | bytes 2359304 | tf_op jit(solution)/shard_map/ppermute | solution.py:921
  363.5 22.5 %collective-permute-start.40 = (bf16[192,2048]{1,0:T(8,128)(2,1)S(1)}, bf16[192,2048]{1,0:T(8,128)(2,1)S(1)}, u32[]{:S(2)}, u32[]{:S(2)}) collective-permute-start(bf16[192,2048]{1,0:T(8,128)(2,1)S(1)} %get-tuple-element.165), channel_id=1, source_target_pairs={{0,4},{2,6},{4,0},{6,2},{8,12},{10,14},{12,8},{14,10},{16,20},{18,... | collective-permute-start | bytes 2359304 | tf_op jit(solution)/shard_map/ppermute | solution.py:921
  388.9 43.4 %collective-permute-start.41 = (bf16[384,2048]{1,0:T(8,128)(2,1)S(1)}, bf16[384,2048]{1,0:T(8,128)(2,1)S(1)}, u32[]{:S(2)}, u32[]{:S(2)}) collective-permute-start(bf16[384,2048]{1,0:T(8,128)(2,1)S(1)} %get-tuple-element.166.refs_5_), channel_id=1, source_target_pairs={{0,2},{2,0},{4,6},{6,4},{8,10},{10,8},{12,14},{14,12},{16,18},{18,... | collective-permute-start | bytes 4718600 | tf_op jit(solution)/shard_map/ppermute | solution.py:921
  390.4 41.9 %collective-permute-start.42 = (bf16[384,2048]{1,0:T(8,128)(2,1)S(1)}, bf16[384,2048]{1,0:T(8,128)(2,1)S(1)}, u32[]{:S(2)}, u32[]{:S(2)}) collective-permute-start(bf16[384,2048]{1,0:T(8,128)(2,1)S(1)} %get-tuple-element.167.refs_6_), channel_id=1, source_target_pairs={{0,4},{2,6},{4,0},{6,2},{8,12},{10,14},{12,8},{14,10},{16,20},{18,... | collective-permute-start | bytes 4718600 | tf_op jit(solution)/shard_map/ppermute | solution.py:921
  431.8 40.4 %collective-permute-start.49 = (bf16[16,64,2816]{2,1,0:T(8,128)(2,1)}, bf16[16,64,2816]{2,1,0:T(8,128)(2,1)}, u32[]{:S(2)}, u32[]{:S(2)}) collective-permute-start(bf16[16,64,2816]{2,1,0:T(8,128)(2,1)} %get-tuple-element.180), channel_id=1, source_target_pairs={{0,1},{1,0},{2,3},{3,2},{4,5},{5,4},{6,7},{7,6},{8,9},{9,8},{10,11... | collective-permute-start | bytes 17301512 | tf_op jit(solution)/shard_map/ppermute | solution.py:75
  431.8 39.0 %collective-permute-start.48 = (bf16[16,64,1408]{2,1,0:T(8,128)(2,1)}, bf16[16,64,1408]{2,1,0:T(8,128)(2,1)}, u32[]{:S(2)}, u32[]{:S(2)}) collective-permute-start(bf16[16,64,1408]{2,1,0:T(8,128)(2,1)} %get-tuple-element.178), channel_id=1, source_target_pairs={{0,1},{1,0},{2,3},{3,2},{4,5},{5,4},{6,7},{7,6},{8,9},{9,8},{10,11... | collective-permute-start | bytes 8650760 | tf_op jit(solution)/shard_map/ppermute | solution.py:75
  456.4 40.6 %collective-permute-start.43 = (bf16[192,2048]{1,0:T(8,128)(2,1)}, bf16[192,2048]{1,0:T(8,128)(2,1)}, u32[]{:S(2)}, u32[]{:S(2)}) collective-permute-start(bf16[192,2048]{1,0:T(8,128)(2,1)} %get-tuple-element.171), channel_id=1, source_target_pairs={{0,2},{2,0},{4,6},{6,4},{8,10},{10,8},{12,14},{14,12},{16,18},{18,... | collective-permute-start | bytes 2359304 | tf_op jit(solution)/shard_map/ppermute | solution.py:921
  457.0 40.5 %collective-permute-start.44 = (bf16[192,2048]{1,0:T(8,128)(2,1)}, bf16[192,2048]{1,0:T(8,128)(2,1)S(1)}, u32[]{:S(2)}, u32[]{:S(2)}) collective-permute-start(bf16[192,2048]{1,0:T(8,128)(2,1)} %get-tuple-element.173), channel_id=1, source_target_pairs={{0,4},{2,6},{4,0},{6,2},{8,12},{10,14},{12,8},{14,10},{16,20},{18,... | collective-permute-start | bytes 2359304 | tf_op jit(solution)/shard_map/ppermute | solution.py:921
  457.6 41.4 %collective-permute-start.45 = (bf16[192,2048]{1,0:T(8,128)(2,1)}, bf16[192,2048]{1,0:T(8,128)(2,1)S(1)}, u32[]{:S(2)}, u32[]{:S(2)}) collective-permute-start(bf16[192,2048]{1,0:T(8,128)(2,1)} %get-tuple-element.175), channel_id=1, source_target_pairs={{0,2},{2,0},{4,6},{6,4},{8,10},{10,8},{12,14},{14,12},{16,18},{18,... | collective-permute-start | bytes 2359304 | tf_op jit(solution)/shard_map/ppermute | solution.py:921
  470.7 29.7 %collective-permute-start.47 = (bf16[192,2048]{1,0:T(8,128)(2,1)}, bf16[192,2048]{1,0:T(8,128)(2,1)}, u32[]{:S(2)}, u32[]{:S(2)}) collective-permute-start(bf16[192,2048]{1,0:T(8,128)(2,1)} %get-tuple-element.177), channel_id=1, source_target_pairs={{0,4},{2,6},{4,0},{6,2},{8,12},{10,14},{12,8},{14,10},{16,20},{18,... | collective-permute-start | bytes 2359304 | tf_op jit(solution)/shard_map/ppermute | solution.py:921
  496.3 23.3 %collective-permute-start.52 = (bf16[256,1024]{1,0:T(8,128)(2,1)S(1)}, bf16[256,1024]{1,0:T(8,128)(2,1)S(1)}, u32[]{:S(2)}, u32[]{:S(2)}) collective-permute-start(bf16[256,1024]{1,0:T(8,128)(2,1)S(1)} %bitcast.199), channel_id=1, source_target_pairs={{0,4},{2,6},{4,0},{6,2},{8,12},{10,14},{12,8},{14,10},{16,20},{18,... | collective-permute-start | bytes 1572872 | tf_op jit(solution)/shard_map/ppermute | solution.py:921
  496.9 22.7 %collective-permute-start.53 = (bf16[256,1024]{1,0:T(8,128)(2,1)S(1)}, bf16[256,1024]{1,0:T(8,128)(2,1)S(1)}, u32[]{:S(2)}, u32[]{:S(2)}) collective-permute-start(bf16[256,1024]{1,0:T(8,128)(2,1)S(1)} %bitcast.197), channel_id=1, source_target_pairs={{0,2},{2,0},{4,6},{6,4},{8,10},{10,8},{12,14},{14,12},{16,18},{18,... | collective-permute-start | bytes 1572872 | tf_op jit(solution)/shard_map/ppermute | solution.py:921
  497.5 23.9 %collective-permute-start.50 = (bf16[256,1024]{1,0:T(8,128)(2,1)S(1)}, bf16[256,1024]{1,0:T(8,128)(2,1)S(1)}, u32[]{:S(2)}, u32[]{:S(2)}) collective-permute-start(bf16[256,1024]{1,0:T(8,128)(2,1)S(1)} %bitcast.196), channel_id=1, source_target_pairs={{0,2},{2,0},{4,6},{6,4},{8,10},{10,8},{12,14},{14,12},{16,18},{18,... | collective-permute-start | bytes 1572872 | tf_op jit(solution)/shard_map/ppermute | solution.py:921
  499.0 22.4 %collective-permute-start.51 = (bf16[256,1024]{1,0:T(8,128)(2,1)S(1)}, bf16[256,1024]{1,0:T(8,128)(2,1)S(1)}, u32[]{:S(2)}, u32[]{:S(2)}) collective-permute-start(bf16[256,1024]{1,0:T(8,128)(2,1)S(1)} %bitcast.195), channel_id=1, source_target_pairs={{0,4},{2,6},{4,0},{6,2},{8,12},{10,14},{12,8},{14,10},{16,20},{18,... | collective-permute-start | bytes 1572872 | tf_op jit(solution)/shard_map/ppermute | solution.py:921
  520.1 22.5 %collective-permute-start.54 = (bf16[256,1024]{1,0:T(8,128)(2,1)S(1)}, bf16[256,1024]{1,0:T(8,128)(2,1)S(1)}, u32[]{:S(2)}, u32[]{:S(2)}) collective-permute-start(bf16[256,1024]{1,0:T(8,128)(2,1)S(1)} %get-tuple-element.192), channel_id=1, source_target_pairs={{0,2},{2,0},{4,6},{6,4},{8,10},{10,8},{12,14},{14,12},{16,18},{18,... | collective-permute-start | bytes 1572872 | tf_op jit(solution)/shard_map/ppermute | solution.py:921
  520.8 21.9 %collective-permute-start.55 = (bf16[256,1024]{1,0:T(8,128)(2,1)S(1)}, bf16[256,1024]{1,0:T(8,128)(2,1)S(1)}, u32[]{:S(2)}, u32[]{:S(2)}) collective-permute-start(bf16[256,1024]{1,0:T(8,128)(2,1)S(1)} %get-tuple-element.193), channel_id=1, source_target_pairs={{0,4},{2,6},{4,0},{6,2},{8,12},{10,14},{12,8},{14,10},{16,20},{18,... | collective-permute-start | bytes 1572872 | tf_op jit(solution)/shard_map/ppermute | solution.py:921
  572.7 28.7 %collective-permute-start.62 = (bf16[384,2048]{1,0:T(8,128)(2,1)S(1)}, bf16[384,2048]{1,0:T(8,128)(2,1)S(1)}, u32[]{:S(2)}, u32[]{:S(2)}) collective-permute-start(bf16[384,2048]{1,0:T(8,128)(2,1)S(1)} %bitcast.188), channel_id=1, source_target_pairs={{0,1},{1,0},{2,3},{3,2},{4,5},{5,4},{6,7},{7,6},{8,9},{9,8},{10,11... | collective-permute-start | bytes 4718600 | tf_op jit(solution)/shard_map/ppermute | solution.py:75
  574.5 23.0 %collective-permute-start.58 = (bf16[256,1280]{1,0:T(8,128)(2,1)S(1)}, bf16[256,1280]{1,0:T(8,128)(2,1)S(1)}, u32[]{:S(2)}, u32[]{:S(2)}) collective-permute-start(bf16[256,1280]{1,0:T(8,128)(2,1)S(1)} %bitcast.190), channel_id=1, source_target_pairs={{0,2},{2,0},{4,6},{6,4},{8,10},{10,8},{12,14},{14,12},{16,18},{18,... | collective-permute-start | bytes 1966088 | tf_op jit(solution)/shard_map/ppermute | solution.py:921
  576.0 21.5 %collective-permute-start.59 = (bf16[256,1280]{1,0:T(8,128)(2,1)S(1)}, bf16[256,1280]{1,0:T(8,128)(2,1)S(1)}, u32[]{:S(2)}, u32[]{:S(2)}) collective-permute-start(bf16[256,1280]{1,0:T(8,128)(2,1)S(1)} %bitcast.189), channel_id=1, source_target_pairs={{0,4},{2,6},{4,0},{6,2},{8,12},{10,14},{12,8},{14,10},{16,20},{18,... | collective-permute-start | bytes 1966088 | tf_op jit(solution)/shard_map/ppermute | solution.py:921
  590.2 21.7 %collective-permute-start.73 = (bf16[128,1024]{1,0:T(8,128)(2,1)S(1)}, bf16[128,1024]{1,0:T(8,128)(2,1)S(1)}, u32[]{:S(2)}, u32[]{:S(2)}) collective-permute-start(bf16[128,1024]{1,0:T(8,128)(2,1)S(1)} %add_convert_fusion.4), channel_id=1, source_target_pairs={{0,8},{2,10},{4,12},{6,14},{8,16},{10,18},{12,20},{14,22},{16,24},... | collective-permute-start | bytes 786440 | tf_op jit(solution)/shard_map/ppermute | solution.py:924
  613.0 46.4 %collective-permute-start.74 = (bf16[128,1024]{1,0:T(8,128)(2,1)S(1)}, bf16[128,1024]{1,0:T(8,128)(2,1)S(1)}, u32[]{:S(2)}, u32[]{:S(2)}) collective-permute-start(bf16[128,1024]{1,0:T(8,128)(2,1)S(1)} %add_convert_fusion.3), channel_id=1, source_target_pairs={{0,8},{2,10},{4,12},{6,14},{8,16},{10,18},{12,20},{14,22},{16,24},... | collective-permute-start | bytes 786440 | tf_op jit(solution)/shard_map/ppermute | solution.py:924
  623.2 23.1 %collective-permute-start.70 = (f32[2,2048]{1,0:T(2,128)S(1)}, f32[2,2048]{1,0:T(2,128)S(1)}, u32[]{:S(2)}, u32[]{:S(2)}) collective-permute-start(f32[2,2048]{1,0:T(2,128)S(1)} %shard_map.572), channel_id=1, source_target_pairs={{0,24},{2,26},{4,28},{6,30},{8,0},{10,2},{12,4},{14,6},{16,8},{18,... | collective-permute-start | bytes 49160 | tf_op jit(solution)/shard_map/ppermute | solution.py:936
  626.2 46.9 %collective-permute-start.64 = (bf16[192,2048]{1,0:T(8,128)(2,1)S(1)}, bf16[192,2048]{1,0:T(8,128)(2,1)S(1)}, u32[]{:S(2)}, u32[]{:S(2)}) collective-permute-start(bf16[192,2048]{1,0:T(8,128)(2,1)S(1)} %get-tuple-element.209), channel_id=1, source_target_pairs={{0,4},{2,6},{4,0},{6,2},{8,12},{10,14},{12,8},{14,10},{16,20},{18,... | collective-permute-start | bytes 2359304 | tf_op jit(solution)/shard_map/ppermute | solution.py:921
  635.4 37.7 %collective-permute-start.65 = (bf16[192,2048]{1,0:T(8,128)(2,1)S(1)}, bf16[192,2048]{1,0:T(8,128)(2,1)S(1)}, u32[]{:S(2)}, u32[]{:S(2)}) collective-permute-start(bf16[192,2048]{1,0:T(8,128)(2,1)S(1)} %get-tuple-element.210), channel_id=1, source_target_pairs={{0,2},{2,0},{4,6},{6,4},{8,10},{10,8},{12,14},{14,12},{16,18},{18,... | collective-permute-start | bytes 2359304 | tf_op jit(solution)/shard_map/ppermute | solution.py:921
  637.7 20.1 %collective-permute-start.66 = (bf16[128,1280]{1,0:T(8,128)(2,1)S(1)}, bf16[128,1280]{1,0:T(8,128)(2,1)S(1)}, u32[]{:S(2)}, u32[]{:S(2)}) collective-permute-start(bf16[128,1280]{1,0:T(8,128)(2,1)S(1)} %dynamic-slice_convert_fusion), channel_id=1, source_target_pairs={{0,8},{2,10},{4,12},{6,14},{8,16},{10,18},{12,20},{14,22},{16,24},... | collective-permute-start | bytes 983048 | tf_op jit(solution)/shard_map/ppermute | solution.py:924
  673.2 32.5 %collective-permute-start.71 = (bf16[128,1280]{1,0:T(8,128)(2,1)S(1)}, bf16[128,1280]{1,0:T(8,128)(2,1)S(1)}, u32[]{:S(2)}, u32[]{:S(2)}) collective-permute-start(bf16[128,1280]{1,0:T(8,128)(2,1)S(1)} %convert_element_type.176), channel_id=1, source_target_pairs={{0,8},{2,10},{4,12},{6,14},{8,16},{10,18},{12,20},{14,22},{16,24},... | collective-permute-start | bytes 983048 | tf_op jit(solution)/shard_map/ppermute | solution.py:924
  677.4 23.6 %collective-permute-start.76 = (bf16[1,64,4224]{2,1,0:T(8,128)(2,1)S(1)}, bf16[1,64,4224]{2,1,0:T(8,128)(2,1)S(1)}, u32[]{:S(2)}, u32[]{:S(2)}) collective-permute-start(bf16[1,64,4224]{2,1,0:T(8,128)(2,1)S(1)} %get-tuple-element.216), channel_id=1, source_target_pairs={{0,4},{2,6},{4,0},{6,2},{8,12},{10,14},{12,8},{14,10},{16,20},{18,... | collective-permute-start | bytes 1622024 | tf_op jit(solution)/shard_map/ppermute | solution.py:921
  677.4 23.6 %collective-permute-start.77 = (bf16[1,64,4224]{2,1,0:T(8,128)(2,1)S(1)}, bf16[1,64,4224]{2,1,0:T(8,128)(2,1)S(1)}, u32[]{:S(2)}, u32[]{:S(2)}) collective-permute-start(bf16[1,64,4224]{2,1,0:T(8,128)(2,1)S(1)} %get-tuple-element.217), channel_id=1, source_target_pairs={{0,6},{2,4},{4,2},{6,0},{8,14},{10,12},{12,10},{14,8},{16,22},{18,... | collective-permute-start | bytes 1622024 | tf_op jit(solution)/shard_map/ppermute | solution.py:921
  (166 other events, 1306.6 us)
Sparse Core Ops, SparseCore 0:
  59.3 165.4 all-gather.1
  481.3 168.2 reduce-scatter.1

commit v3 on v2

--- a/solution.py
+++ b/solution.py
@@ -66,6 +66,7 @@
 PLANE = 4
 LANES = 128
 TILE = 256
+ROWS = 384
 VMEM_LIMIT = 48 * 1024 * 1024
 SMALL_COST = pl.CostEstimate(flops=1024, bytes_accessed=1024, transcendentals=0)
 LARGE_COST = pl.CostEstimate(flops=1 << 35, bytes_accessed=1 << 20, transcendentals=0)
@@ -492,9 +493,9 @@
         gate_up_kernel,
         waits,
         (normed, weight),
-        grid=(rows // TILE,),
-        in_specs=[by_rows(TILE, depth), held(weight)],
-        out_specs=by_rows(TILE, columns),
+        grid=(rows // ROWS,),
+        in_specs=[by_rows(ROWS, depth), held(weight)],
+        out_specs=by_rows(ROWS, columns),
         out_shape=jax.ShapeDtypeStruct((rows, columns), jnp.float32),
     )
 
@@ -506,9 +507,9 @@
         hidden_kernel,
         waits,
         (upstream, down, gate_up),
-        grid=(rows // TILE,),
-        in_specs=[by_rows(TILE, depth), held(down), by_rows(TILE, 2 * width)],
-        out_specs=[by_rows(TILE, width), by_rows(TILE, 2 * width)],
+        grid=(rows // ROWS,),
+        in_specs=[by_rows(ROWS, depth), held(down), by_rows(ROWS, 2 * width)],
+        out_specs=[by_rows(ROWS, width), by_rows(ROWS, 2 * width)],
         out_shape=[
             jax.ShapeDtypeStruct((rows, width), LOW),
             jax.ShapeDtypeStruct((rows, 2 * width), LOW),
@@ -545,33 +546,24 @@
         give_ref[at] = jnp.where(first, bottom, top)
 
 
-def unit_grads_kernel(
-    blocks,
-    core_ref,
-    upstream_ref,
-    inner_ref,
-    normed_ref,
-    grads_ref,
-    down_keep_ref,
-    down_give_ref,
-    keep_ref,
-    give_ref,
-):
+def unit_grads_kernel(blocks, count, core_ref, *refs):
+    upstream, inner, normed, grads = [refs[at * count : (at + 1) * count] for at in range(4)]
+    down_keep_ref, down_give_ref, keep_ref, give_ref = refs[4 * count :]
     step = pl.program_id(0)
 
     @pl.when(step < blocks)
     def _():
-        part = dot_first(upstream_ref[...], inner_ref[...]).astype(LOW)
-        put_halves(core_ref, part, down_keep_ref, down_give_ref)
+        part = sum(dot_first(one[...], two[...]) for one, two in zip(upstream, inner))
+        put_halves(core_ref, low(part), down_keep_ref, down_give_ref)
 
     @pl.when(step >= blocks)
     def _():
-        part = dot_first(normed_ref[...], grads_ref[...]).astype(LOW)
-        put_halves(core_ref, part, keep_ref, give_ref)
+        part = sum(dot_first(one[...], two[...]) for one, two in zip(normed, grads))
+        put_halves(core_ref, low(part), keep_ref, give_ref)
 
 
 def unit_grads(upstream, inner, normed, grads, rows, waits=()):
-    depth, total = upstream.shape
+    total = upstream[0].shape[1]
     block = 2 * LANES
     blocks, lots = total // block, block // rows // 2
     core = lax.axis_index("tensor").astype(jnp.int32).reshape(1)
@@ -579,18 +571,19 @@
     late_on = lambda i: jnp.maximum(i - blocks, 0)
     out = lambda width, when: pl.BlockSpec((lots, rows, width), lambda i: (when(i), 0, 0))
     shape = lambda width: jax.ShapeDtypeStruct((total // rows // 2, rows, width), LOW)
-    widths = inner.shape[1], grads.shape[1]
+    left = lambda array, when: pl.BlockSpec((array.shape[0], block), lambda i: (0, when(i)))
+    widths = inner[0].shape[1], grads[0].shape[1]
     return call(
-        functools.partial(unit_grads_kernel, blocks),
+        functools.partial(unit_grads_kernel, blocks, len(upstream)),
         waits,
-        (core, upstream, inner, normed, grads),
+        (core, *upstream, *inner, *normed, *grads),
         grid=(2 * blocks,),
         in_specs=[
             pl.BlockSpec(memory_space=pltpu.SMEM),
-            pl.BlockSpec((depth, block), lambda i: (0, early(i))),
-            held(inner),
-            pl.BlockSpec((depth, block), lambda i: (0, late_on(i))),
-            held(grads),
+            *[left(array, early) for array in upstream],
+            *[held(array) for array in inner],
+            *[left(array, late_on) for array in normed],
+            *[held(array) for array in grads],
         ],
         out_specs=[out(widths[0], early)] * 2 + [out(widths[1], late_on)] * 2,
         out_shape=[shape(widths[0])] * 2 + [shape(widths[1])] * 2,
@@ -1100,10 +1093,11 @@
     def rows_of(values, which):
         return lax.dynamic_slice_in_dim(values, which * rows, rows, 0)
 
-    def place_tokens(own, first, second, far_one, far_two):
-        half, columns = rows // 2, own.shape[1]
-        blocks = [block.reshape(-1, half, columns) for block in (own, first, second, far_one, far_two)]
-        (whole,) = move(blocks, jnp.arange(2 * PLANE, dtype=jnp.int32))
+    def place_tokens(*blocks):
+        half, columns = rows // 2, blocks[0].shape[1]
+        lots = [block.reshape(-1, half, columns) for block in blocks]
+        count = sum(lot.shape[0] for lot in lots)
+        (whole,) = move(lots, jnp.arange(count, dtype=jnp.int32))
         return whole.reshape(-1, columns)
 
     gains_low = low(norm_gains)
@@ -1179,24 +1173,34 @@
     *normed_near, units_other = fence([*normed_near, units_other])
     normed_far = links.gather_far(*normed_near)
     down_all, gate_up_all = links.place_units(units_own, units_other, [units // 2])
-    normed_far = fence(normed_far, [down_all, gate_up_all])
-    normed = place_tokens(normed_two, *normed_near, *normed_far)
+    normed_front = place_tokens(normed_two, *normed_near)
+    gate_up_front = gate_and_up(normed_front, gate_up_all)
+    normed_far = fence(normed_far, [gate_up_front[:16, :LANES]])
+    normed_back = place_tokens(*normed_far)
 
     upstream_near = fence(upstream_near, normed_far)
     upstream_far = links.gather_far(*upstream_near)
-    gate_up = gate_and_up(normed, gate_up_all)
-    upstream = place_tokens(cotangent_late, *upstream_near, *upstream_far)
-    inner, grads = hidden(upstream, down_all, gate_up)
+    gate_up_back = gate_and_up(normed_back, gate_up_all)
+    upstream_front = place_tokens(cotangent_late, *upstream_near)
+    inner_front, grads_front = hidden(upstream_front, down_all, gate_up_front)
+    upstream_far = fence(upstream_far, [inner_front[:16, :LANES]])
+    upstream_back = place_tokens(*upstream_far)
+    inner_back, grads_back = hidden(upstream_back, down_all, gate_up_back)
     half = rows // 2
-    back_far = across(grads, gate_up_all, 3 * rows, (half, half))
+    back_far = across(grads_back, gate_up_all, 0, (half, half))
     back_far_sent = links.sum_far(*back_far)
     back_own, back_one, back_two = across(
-        grads, gate_up_all, 0, (rows, rows, rows), [back_far[0]]
+        grads_front, gate_up_all, 0, (rows, rows, rows), [back_far[0]]
     )
     one_send, two_send = join_sends(back_one, back_two, *back_far_sent, [back_own])
     back_sent = [links.swap(one_send, 1), links.swap(two_send, 2)]
     down_keep, down_give, gate_up_keep, gate_up_give = unit_grads(
-        upstream, inner, normed, grads, weight_rows // 2, [one_send, two_send]
+        [upstream_front, upstream_back],
+        [inner_front, inner_back],
+        [normed_front, normed_back],
+        [grads_front, grads_back],
+        weight_rows // 2,
+        [one_send, two_send],
     )
     hidden_grad, attn_grad_low, gain_two_grad = norm_back(
         [back_own, *back_sent], hidden_state, gain_two, cotangent, [down_keep]
@@ -1204,8 +1208,9 @@
     attn_grad_other = swap_cores(attn_grad_low)
     down_other = swap_cores(down_give)
     gate_up_other = swap_cores(gate_up_give)
-    ffn_own, one_top, one_low, two_top, two_low, *ffn_far = across(
-        inner, down_all, 0, (rows, *[half] * 6), [attn_grad_low]
+    ffn_far = across(inner_back, down_all, 0, (half, half), [attn_grad_low])
+    ffn_own, one_top, one_low, two_top, two_low = across(
+        inner_front, down_all, 0, (rows, *[half] * 4), [attn_grad_low]
     )
     ffn_far_sent = links.sum_far(*ffn_far)
     ffn_near = [links.swap(one_top, 1), links.swap(two_low, 2)]

time: 739 us -> 738 us (level)
  Pallas kernels: 282 us -> 308 us
  local copies, waits for them, and re-layouts: 78 us -> 59.3 us
  starting transfers between devices: 109 us -> 97.8 us
    unnamed x264 -> x238, local copies, waits for them, and re-layouts: 69.8 us -> 50 us
    pallas_call x28 -> x31, Pallas kernels: 255 us -> 273 us  [call(): pl.pallas_call(functools.partial(late, kernel, (len(operands), len(waits)...]
    ppermute x54, waiting for transfers between devices: 139 us -> 128 us  [swap(): return lax.ppermute(block, 'dp', self.pairs[step])]
    ppermute x54, starting transfers between devices: 62.7 us -> 55 us  [swap(): return lax.ppermute(block, 'dp', self.pairs[step])]
    ppermute x12, waiting for transfers between devices: 52.7 us -> 60.3 us  [turn(): return lax.ppermute(block, 'dp', self.ring)]
    pallas_call x8 -> x10, Pallas kernels: 13.8 us -> 17.5 us  [move(): pl.pallas_call(functools.partial(move_kernel, counts, lots, len(waits)),...]
  transfers between devices with their start and end apart: 84 -> 84, of which waited for: 33 -> 36; matrix products, arithmetic and copies ran while one was open for 5% -> 5% of each run, Pallas kernels for 34% -> 38%
where the time goes in v3:
time: 738 us; the launch traced here: 730 us
  Pallas kernels  308 us (42%)
  waiting for transfers between devices  204 us (28%)
  starting transfers between devices  97.8 us (13%)
  local copies, waits for them, and re-layouts  59.3 us (8%)
  other arithmetic  35.7 us (5%)
  between operations  16.2 us (2%)
  matrix products  8.43 us (1%)
    pallas_call x31, Pallas kernels, call(): pl.pallas_call(functools.partial(late, kernel, (len(operands), len(waits)...  273 us
    ppermute x54, waiting for transfers between devices, swap(): return lax.ppermute(block, 'dp', self.pairs[step])  128 us
    ppermute x12, waiting for transfers between devices, turn(): return lax.ppermute(block, 'dp', self.ring)  60.3 us
    ppermute x54, starting transfers between devices, swap(): return lax.ppermute(block, 'dp', self.pairs[step])  55 us
    unnamed x238, local copies, waits for them, and re-layouts  50 us
    ppermute x12, starting transfers between devices, turn(): return lax.ppermute(block, 'dp', self.ring)  28.6 us
    pallas_call x10, Pallas kernels, move(): pl.pallas_call(functools.partial(move_kernel, counts, lots, len(waits)),...  17.5 us
  transfers between devices with their start and end apart: 84, of which 36 were waited for; matrix products, arithmetic and copies ran while one was open for 5% of the time, Pallas kernels for 38%

profile of v3, /device:TPU:0, one launch (start us, length us, event | category | flops | bytes accessed | tf_op | source)
XLA Modules:
  0.0 729.6 jit_solution(18212820413319786677)
XLA Ops:
  12.5 3.7 collective-permute-start.1
  21.5 10.4 %collective-permute-done.4.refs_2_ = bf16[128,1280]{1,0:T(8,128)(2,1)S(1)} collective-permute-done((bf16[128,1280]{1,0:T(8,128)(2,1)S(1)}, bf16[128,1280]{1,0:T(8,128)(2,1)S(1)}, u32[]{:S(2)}, u32[]{:S(2)}) %collective-permute-start.4) | collective-permute-done | bytes 327712 | tf_op jit(solution)/shard_map/ppermute | solution.py:917
  35.9 6.0 collective-permute-done.13
  42.0 6.6 collective-permute-done.16.refs_2_
  48.6 9.2 %collective-permute-done.15.refs_1_ = bf16[1,64,4224]{2,1,0:T(8,128)(2,1)S(1)} collective-permute-done((bf16[1,64,4224]{2,1,0:T(8,128)(2,1)S(1)}, bf16[1,64,4224]{2,1,0:T(8,128)(2,1)S(1)}, u32[]{:S(2)}, u32[]{:S(2)}) %collective-permute-start.15) | collective-permute-done | bytes 540704 | tf_op jit(solution)/shard_map/ppermute | solution.py:914
  77.5 9.8 %collective-permute-done.10.refs_1_ = bf16[256,1280]{1,0:T(8,128)(2,1)S(1)} collective-permute-done((bf16[256,1280]{1,0:T(8,128)(2,1)S(1)}, bf16[256,1280]{1,0:T(8,128)(2,1)S(1)}, u32[]{:S(2)}, u32[]{:S(2)}) %collective-permute-start.10) | collective-permute-done | bytes 655392 | tf_op jit(solution)/shard_map/ppermute | solution.py:914
  92.5 6.2 collective-permute-start.24
  102.1 6.3 collective-permute-done.11.refs_0_
  135.0 7.7 %shard_map.530.refs_0_.refs_1_.refs_2_ = bf16[768,1280]{1,0:T(8,128)(2,1)S(1)} custom-call(bf16[768,2048]{1,0:T(8,128)(2,1)S(1)} %bitcast.139, bf16[2048,1280]{1,0:T(8,128)(2,1)} %bitcast.141, f32[768,128]{1,0:T(8,128)S(1)} %copy-done.23, f32[768,128]{1,0:T(8,128)S(1)} %copy-done.26), custom_call_target="tpu_custom_call" | custom-call | flops 1024 | bytes 1024 | tf_op jit(solution)/shard_map/pallas_call | solution.py:86
  142.7 12.3 %shard_map.531 = (bf16[768,512]{1,0:T(8,128)(2,1)S(1)}, f32[768,128]{1,0:T(8,128)S(1)}) custom-call(bf16[768,1280]{1,0:T(8,128)(2,1)S(1)} %shard_map.530.refs_0_.refs_1_.refs_2_, bf16[768,1280]{1,0:T(8,128)(2,1)S(1)} %shard_map.530.refs_0_.refs_1_.refs_2_, bf16[768,1280]{1,0:T(8,128)(2,1)S(1)} %shard_map.530.refs_0_.refs_1_.refs_2_, ...), custom_call_target="tpu_custom_call" | custom-call | flops 1024 | bytes 1024 | tf_op jit(solution)/shard_map/pallas_call | solution.py:86
  164.1 12.4 %shard_map.534 = (bf16[768,512]{1,0:T(8,128)(2,1)S(1)}, f32[768,128]{1,0:T(8,128)S(1)}) custom-call(bf16[768,1280]{1,0:T(8,128)(2,1)S(1)} %shard_map.530.refs_0_.refs_1_.refs_2_, bf16[768,1280]{1,0:T(8,128)(2,1)S(1)} %shard_map.530.refs_0_.refs_1_.refs_2_, bf16[768,1280]{1,0:T(8,128)(2,1)S(1)} %shard_map.530.refs_0_.refs_1_.refs_2_, ...), custom_call_target="tpu_custom_call" | custom-call | flops 1024 | bytes 1024 | tf_op jit(solution)/shard_map/pallas_call | solution.py:86
  186.5 5.2 add_add_fusion.refs_0_.refs_3_
  194.0 25.8 %collective-permute-done.31.refs_1_ = bf16[384,2048]{1,0:T(8,128)(2,1)S(1)} collective-permute-done((bf16[384,2048]{1,0:T(8,128)(2,1)}, bf16[384,2048]{1,0:T(8,128)(2,1)S(1)}, u32[]{:S(2)}, u32[]{:S(2)}) %collective-permute-start.31) | collective-permute-done | bytes 1572896 | tf_op jit(solution)/shard_map/ppermute | solution.py:914
  220.1 5.5 all-gather.2.cloned.1.call-done.refs_0_
  228.6 34.1 %collective-permute-done.33.refs_1_ = bf16[384,2048]{1,0:T(8,128)(2,1)} collective-permute-done((bf16[384,2048]{1,0:T(8,128)(2,1)}, bf16[384,2048]{1,0:T(8,128)(2,1)}, u32[]{:S(2)}, u32[]{:S(2)}) %collective-permute-start.33) | collective-permute-done | bytes 1572896 | tf_op jit(solution)/shard_map/ppermute | solution.py:914
  263.9 6.6 shard_map.544
  270.5 4.3 copy-done.67
  284.7 21.8 %shard_map.545.refs_2_ = f32[1152,2816]{1,0:T(8,128)} custom-call(bf16[1152,2048]{1,0:T(8,128)(2,1)S(1)} %bitcast.147, bf16[2048,2816]{1,0:T(8,128)(2,1)} %bitcast.185), custom_call_target="tpu_custom_call" | custom-call | flops 34359738368 | bytes 1048576 | tf_op jit(solution)/shard_map/pallas_call | solution.py:86
  311.9 8.9 %shard_map.553.refs_2_ = f32[384,2816]{1,0:T(8,128)S(1)} custom-call(bf16[384,2048]{1,0:T(8,128)(2,1)S(1)} %bitcast.165, bf16[2048,2816]{1,0:T(8,128)(2,1)} %bitcast.186), custom_call_target="tpu_custom_call" | custom-call | flops 34359738368 | bytes 1048576 | tf_op jit(solution)/shard_map/pallas_call | solution.py:86
  327.0 15.9 %shard_map.549 = (bf16[1152,1408]{1,0:T(8,128)(2,1)S(1)}, bf16[1152,2816]{1,0:T(8,128)(2,1)}) custom-call(bf16[1152,2048]{1,0:T(8,128)(2,1)} %bitcast.149, bf16[2048,1408]{1,0:T(8,128)(2,1)} %bitcast.189, f32[1152,2816]{1,0:T(8,128)} %shard_map.545.refs_2_), custom_call_target="tpu_custom_call" | custom-call | flops 34359738368 | bytes 1048576 | tf_op jit(solution)/shard_map/pallas_call | solution.py:86
  344.6 7.0 shard_map.554
  351.6 8.5 %shard_map.555 = (bf16[192,2048]{1,0:T(8,128)(2,1)S(1)}, bf16[192,2048]{1,0:T(8,128)(2,1)S(1)}) custom-call(bf16[384,2816]{1,0:T(8,128)(2,1)S(1)} %get-tuple-element.167.refs_0_.refs_8_, bf16[2048,2816]{1,0:T(8,128)(2,1)} %bitcast.187), custom_call_target="tpu_custom_call" | custom-call | flops 34359738368 | bytes 1048576 | tf_op jit(solution)/shard_map/pallas_call | solution.py:86
  362.3 18.4 %shard_map.556 = (bf16[384,2048]{1,0:T(8,128)(2,1)S(1)}, bf16[384,2048]{1,0:T(8,128)(2,1)S(1)}, bf16[384,2048]{1,0:T(8,128)(2,1)S(1)}) custom-call(bf16[1152,2816]{1,0:T(8,128)(2,1)} %get-tuple-element.164.refs_0_.refs_7_, bf16[2048,2816]{1,0:T(8,128)(2,1)} %bitcast.188, bf16[192,2048]{1,0:T(8,128)(2,1)S(1)} %get-tuple-element.168.refs_2_), custom_call_target="tpu_custom_call" | custom-call | flops 34359738368 | bytes 1048576 | tf_op jit(solution)/shard_map/pallas_call | solution.py:86
  389.1 43.2 %shard_map.558 = (bf16[16,64,1408]{2,1,0:T(8,128)(2,1)}, bf16[16,64,1408]{2,1,0:T(8,128)(2,1)}, bf16[16,64,2816]{2,1,0:T(8,128)(2,1)}, bf16[16,64,2816]{2,1,0:T(8,128)(2,1)}) custom-call(s32[1]{0:T(128)} %bitcast.refs_0_, bf16[1152,2048]{1,0:T(8,128)(2,1)} %bitcast.150, bf16[384,2048]{1,0:T(8,128)(2,1)S(1)} %bitcast.169, bf16[1152,1408]{1,0:T(8,128)(2,1)} %copy-done.66, ...), custom_call_target="tpu_custom_call" | custom-call | flops 34359738368 | bytes 1048576 | tf_op jit(solution)/shard_map/pallas_call | solution.py:86
  434.0 6.7 shard_map.559
  440.7 6.1 shard_map.561
  446.8 11.5 %shard_map.560 = (bf16[384,2048]{1,0:T(8,128)(2,1)S(1)}, bf16[192,2048]{1,0:T(8,128)(2,1)}, bf16[192,2048]{1,0:T(8,128)(2,1)S(1)}, bf16[192,2048]{1,0:T(8,128)(2,1)S(1)}, bf16[192,2048]{1,0:T(8,128)(2,1)}) custom-call(bf16[1152,1408]{1,0:T(8,128)(2,1)} %copy-done.66, bf16[2048,1408]{1,0:T(8,128)(2,1)} %bitcast.192, bf16[384,2048]{1,0:T(8,128)(2,1)} %get-tuple-element.177.refs_2_), custom_call_target="tpu_custom_call" | custom-call | flops 34359738368 | bytes 1048576 | tf_op jit(solution)/shard_map/pallas_call | solution.py:86
  464.6 6.7 shard_map.563.refs_2_.refs_3_
  472.9 9.4 %shard_map.564.refs_3_ = bf16[16,64,4224]{2,1,0:T(8,128)(2,1)} custom-call(bf16[16,64,1408]{2,1,0:T(8,128)(2,1)S(1)} %copy-done.8, bf16[16,64,1408]{2,1,0:T(8,128)(2,1)} %collective-permute-done.48.refs_1_, bf16[16,64,2816]{2,1,0:T(8,128)(2,1)} %get-tuple-element.187.refs_2_, bf16[16,64,2816]{2,1,0:T(8,128)(2,1)} %collective-permute-done.49.refs_3_, ...), custom_call_target="tpu_custom_call" | custom-call | flops 1024 | bytes 1024 | tf_op jit(solution)/shard_map/pallas_call | solution.py:86
  485.1 8.7 %shard_map.565 = bf16[2048,1024]{1,0:T(8,128)(2,1)} custom-call(bf16[768,2048]{1,0:T(8,128)(2,1)} %bitcast.159, bf16[768,1024]{1,0:T(8,128)(2,1)S(1)} %copy-done.57, bf16[768,1024]{1,0:T(8,128)(2,1)S(1)} %copy-done.77, bf16[16,64,4224]{2,1,0:T(8,128)(2,1)} %shard_map.564.refs_3_), custom_call_target="tpu_custom_call" | custom-call | flops 34359738368 | bytes 1048576 | tf_op jit(solution)/shard_map/pallas_call | solution.py:86
  493.8 3.5 shard_map.566
  501.6 19.0 %shard_map.567 = (bf16[768,512]{1,0:T(8,128)(2,1)S(1)}, bf16[768,256]{1,0:T(8,128)(2,1)S(1)}) custom-call(bf16[768,1280]{1,0:T(8,128)(2,1)} %copy-done, bf16[768,1280]{1,0:T(8,128)(2,1)} %copy-done, bf16[768,1280]{1,0:T(8,128)(2,1)} %copy-done, bf16[768,1024]{1,0:T(8,128)(2,1)} %copy-done.76, f32[768,128]{1,0:T(8,128)S(1)} %copy-done.71, ...), custom_call_target="tpu_custom_call" | custom-call | flops 34359738368 | bytes 1048576 | tf_op jit(solution)/shard_map/pallas_call | solution.py:86
  525.2 19.2 %shard_map.568 = (bf16[768,512]{1,0:T(8,128)(2,1)S(1)}, bf16[768,256]{1,0:T(8,128)(2,1)S(1)}) custom-call(bf16[768,1280]{1,0:T(8,128)(2,1)} %copy-done, bf16[768,1280]{1,0:T(8,128)(2,1)} %copy-done, bf16[768,1280]{1,0:T(8,128)(2,1)} %copy-done, bf16[768,1024]{1,0:T(8,128)(2,1)S(1)} %copy-done.78, f32[768,128]{1,0:T(8,128)S(1)} %copy-done.73, ...), custom_call_target="tpu_custom_call" | custom-call | flops 34359738368 | bytes 1048576 | tf_op jit(solution)/shard_map/pallas_call | solution.py:86
  544.6 7.4 %shard_map.570 = bf16[2048,1280]{1,0:T(8,128)(2,1)} custom-call(bf16[768,2048]{1,0:T(8,128)(2,1)S(1)} %bitcast.140, bf16[768,1280]{1,0:T(8,128)(2,1)S(1)} %constant_dynamic-update-slice_fusion.4.refs_1_.refs_0_, bf16[256,1024]{1,0:T(8,128)(2,1)S(1)} %collective-permute-done.54.refs_2_, bf16[256,1024]{1,0:T(8,128)(2,1)S(1)} %collective-permute-done.55.refs_3_), custom_call_target="tpu_custom_call" | custom-call | flops 34359738368 | bytes 1048576 | tf_op jit(solution)/shard_map/pallas_call | solution.py:86
  551.9 4.1 shard_map.571
  560.2 7.6 %shard_map.572.refs_4_ = bf16[768,2048]{1,0:T(8,128)(2,1)} custom-call(bf16[768,1280]{1,0:T(8,128)(2,1)S(1)} %constant_dynamic-update-slice_fusion.4.refs_1_.refs_0_, bf16[2048,1280]{1,0:T(8,128)(2,1)} %bitcast.142, bf16[256,1280]{1,0:T(8,128)(2,1)S(1)} %bitcast.197, bf16[256,1280]{1,0:T(8,128)(2,1)S(1)} %bitcast.199), custom_call_target="tpu_custom_call" | custom-call | flops 34359738368 | bytes 1048576 | tf_op jit(solution)/shard_map/pallas_call | solution.py:86
  567.8 4.0 collective-permute-done.56.refs_2_.refs_3_
  580.2 13.0 %collective-permute-done.72 = bf16[128,1024]{1,0:T(8,128)(2,1)S(1)} collective-permute-done((bf16[128,1024]{1,0:T(8,128)(2,1)S(1)}, bf16[128,1024]{1,0:T(8,128)(2,1)S(1)}, u32[]{:S(2)}, u32[]{:S(2)}) %collective-permute-start.72) | collective-permute-done | bytes 262176 | tf_op jit(solution)/shard_map/ppermute | solution.py:917
  593.3 8.1 %collective-permute-start.73 = (bf16[128,1024]{1,0:T(8,128)(2,1)S(1)}, bf16[128,1024]{1,0:T(8,128)(2,1)S(1)}, u32[]{:S(2)}, u32[]{:S(2)}) collective-permute-start(bf16[128,1024]{1,0:T(8,128)(2,1)S(1)} %add_convert_fusion.4), channel_id=1, source_target_pairs={{0,8},{2,10},{4,12},{6,14},{8,16},{10,18},{12,20},{14,22},{16,24},... | collective-permute-start | bytes 786440 | tf_op jit(solution)/shard_map/ppermute | solution.py:917
  603.7 6.1 shard_map.575
  610.0 6.1 collective-permute-done.73
  617.2 7.6 %collective-permute-start.74 = (bf16[128,1024]{1,0:T(8,128)(2,1)S(1)}, bf16[128,1024]{1,0:T(8,128)(2,1)S(1)}, u32[]{:S(2)}, u32[]{:S(2)}) collective-permute-start(bf16[128,1024]{1,0:T(8,128)(2,1)S(1)} %add_convert_fusion.3), channel_id=1, source_target_pairs={{0,8},{2,10},{4,12},{6,14},{8,16},{10,18},{12,20},{14,22},{16,24},... | collective-permute-start | bytes 786440 | tf_op jit(solution)/shard_map/ppermute | solution.py:917
  631.9 6.1 collective-permute-done.70
  642.5 12.8 %collective-permute-done.66 = bf16[128,1280]{1,0:T(8,128)(2,1)S(1)} collective-permute-done((bf16[128,1280]{1,0:T(8,128)(2,1)S(1)}, bf16[128,1280]{1,0:T(8,128)(2,1)S(1)}, u32[]{:S(2)}, u32[]{:S(2)}) %collective-permute-start.66) | collective-permute-done | bytes 327712 | tf_op jit(solution)/shard_map/ppermute | solution.py:917
  655.5 5.2 collective-permute-start.67
  663.9 6.3 collective-permute-done.67
  680.9 7.7 %collective-permute-done.75.refs_1_ = bf16[1,64,4224]{2,1,0:T(8,128)(2,1)S(1)} collective-permute-done((bf16[1,64,4224]{2,1,0:T(8,128)(2,1)S(1)}, bf16[1,64,4224]{2,1,0:T(8,128)(2,1)S(1)}, u32[]{:S(2)}, u32[]{:S(2)}) %collective-permute-start.75) | collective-permute-done | bytes 540704 | tf_op jit(solution)/shard_map/ppermute | solution.py:914
  688.7 9.1 %collective-permute-done.76.refs_2_ = bf16[1,64,4224]{2,1,0:T(8,128)(2,1)S(1)} collective-permute-done((bf16[1,64,4224]{2,1,0:T(8,128)(2,1)S(1)}, bf16[1,64,4224]{2,1,0:T(8,128)(2,1)S(1)}, u32[]{:S(2)}, u32[]{:S(2)}) %collective-permute-start.76) | collective-permute-done | bytes 540704 | tf_op jit(solution)/shard_map/ppermute | solution.py:914
  (507 shorter events, 215.6 us)
Async XLA Ops:
  7.2 218.4 %all-gather.2.cloned.1.call-start = ((), (), s32[]{:S(2)}) async-start(), calls=%async_computation.1 | async-start | bytes 10813440 | tf_op jit(solution)/shard_map/all_gather | solution.py:1008
  34.9 22.9 %collective-permute-start.15 = (bf16[1,64,4224]{2,1,0:T(8,128)(2,1)S(1)}, bf16[1,64,4224]{2,1,0:T(8,128)(2,1)S(1)}, u32[]{:S(2)}, u32[]{:S(2)}) collective-permute-start(bf16[1,64,4224]{2,1,0:T(8,128)(2,1)S(1)} %get-tuple-element.264), channel_id=1, source_target_pairs={{0,4},{2,6},{4,0},{6,2},{8,12},{10,14},{12,8},{14,10},{16,20},{18,... | collective-permute-start | bytes 1622024 | tf_op jit(solution)/shard_map/ppermute | solution.py:914
  35.4 22.5 %collective-permute-start.14 = (bf16[1,64,4224]{2,1,0:T(8,128)(2,1)S(1)}, bf16[1,64,4224]{2,1,0:T(8,128)(2,1)S(1)}, u32[]{:S(2)}, u32[]{:S(2)}) collective-permute-start(bf16[1,64,4224]{2,1,0:T(8,128)(2,1)S(1)} %get-tuple-element.265), channel_id=1, source_target_pairs={{0,2},{2,0},{4,6},{6,4},{8,10},{10,8},{12,14},{14,12},{16,18},{18,... | collective-permute-start | bytes 1622024 | tf_op jit(solution)/shard_map/ppermute | solution.py:914
  59.9 611.2 %reduce-scatter.2.cloned.1.call-start = ((), (), s32[]{:S(2)}) async-start(), calls=%async_computation.2 | async-start | bytes 10813440 | tf_op jit(solution)/shard_map/reduce_scatter | solution.py:1016
  71.8 29.6 %collective-permute-start.19 = (bf16[256,1280]{1,0:T(8,128)(2,1)S(1)}, bf16[256,1280]{1,0:T(8,128)(2,1)S(1)}, u32[]{:S(2)}, u32[]{:S(2)}) collective-permute-start(bf16[256,1280]{1,0:T(8,128)(2,1)S(1)} %constant_dynamic-update-slice_fusion), channel_id=1, source_target_pairs={{0,4},{2,6},{4,0},{6,2},{8,12},{10,14},{12,8},{14,10},{16,20},{18,... | collective-permute-start | bytes 1966088 | tf_op jit(solution)/shard_map/ppermute | solution.py:914
  72.5 29.7 %collective-permute-start.18 = (bf16[256,1280]{1,0:T(8,128)(2,1)S(1)}, bf16[256,1280]{1,0:T(8,128)(2,1)S(1)}, u32[]{:S(2)}, u32[]{:S(2)}) collective-permute-start(bf16[256,1280]{1,0:T(8,128)(2,1)S(1)} %constant_dynamic-update-slice_fusion), channel_id=1, source_target_pairs={{0,2},{2,0},{4,6},{6,4},{8,10},{10,8},{12,14},{14,12},{16,18},{18,... | collective-permute-start | bytes 1966088 | tf_op jit(solution)/shard_map/ppermute | solution.py:914
  88.2 20.3 %collective-permute-start.11 = (bf16[128,1280]{1,0:T(8,128)(2,1)S(1)}, bf16[128,1280]{1,0:T(8,128)(2,1)S(1)}, u32[]{:S(2)}, u32[]{:S(2)}) collective-permute-start(bf16[128,1280]{1,0:T(8,128)(2,1)S(1)} %slice.117), channel_id=1, source_target_pairs={{0,2},{2,0},{4,6},{6,4},{8,10},{10,8},{12,14},{14,12},{16,18},{18,... | collective-permute-start | bytes 983048 | tf_op jit(solution)/shard_map/ppermute | solution.py:914
  92.5 21.1 %collective-permute-start.24 = (bf16[128,1024]{1,0:T(8,128)(2,1)S(1)}, bf16[128,1024]{1,0:T(8,128)(2,1)S(1)}, u32[]{:S(2)}, u32[]{:S(2)}) collective-permute-start(bf16[128,1024]{1,0:T(8,128)(2,1)S(1)} %collective-permute-done.23), channel_id=1, source_target_pairs={{0,8},{2,10},{4,12},{6,14},{8,16},{10,18},{12,20},{14,22},{16,24},... | collective-permute-start | bytes 786440 | tf_op jit(solution)/shard_map/ppermute | solution.py:917
  120.1 35.7 %collective-permute-start.26 = (bf16[512,1024]{1,0:T(8,128)(2,1)}, bf16[512,1024]{1,0:T(8,128)(2,1)S(1)}, u32[]{:S(2)}, u32[]{:S(2)}) collective-permute-start(bf16[512,1024]{1,0:T(8,128)(2,1)} %shard_map.532), channel_id=1, source_target_pairs={{0,4},{2,6},{4,0},{6,2},{8,12},{10,14},{12,8},{14,10},{16,20},{18,... | collective-permute-start | bytes 3145736 | tf_op jit(solution)/shard_map/ppermute | solution.py:914
  120.7 35.1 %collective-permute-start.25 = (bf16[512,1024]{1,0:T(8,128)(2,1)}, bf16[512,1024]{1,0:T(8,128)(2,1)}, u32[]{:S(2)}, u32[]{:S(2)}) collective-permute-start(bf16[512,1024]{1,0:T(8,128)(2,1)} %shard_map.532), channel_id=1, source_target_pairs={{0,2},{2,0},{4,6},{6,4},{8,10},{10,8},{12,14},{14,12},{16,18},{18,... | collective-permute-start | bytes 3145736 | tf_op jit(solution)/shard_map/ppermute | solution.py:914
  182.8 37.0 %collective-permute-start.31 = (bf16[384,2048]{1,0:T(8,128)(2,1)}, bf16[384,2048]{1,0:T(8,128)(2,1)S(1)}, u32[]{:S(2)}, u32[]{:S(2)}) collective-permute-start(bf16[384,2048]{1,0:T(8,128)(2,1)} %get-tuple-element.148), channel_id=1, source_target_pairs={{0,4},{2,6},{4,0},{6,2},{8,12},{10,14},{12,8},{14,10},{16,20},{18,... | collective-permute-start | bytes 4718600 | tf_op jit(solution)/shard_map/ppermute | solution.py:914
  183.4 36.7 %collective-permute-start.30 = (bf16[384,2048]{1,0:T(8,128)(2,1)}, bf16[384,2048]{1,0:T(8,128)(2,1)S(1)}, u32[]{:S(2)}, u32[]{:S(2)}) collective-permute-start(bf16[384,2048]{1,0:T(8,128)(2,1)} %get-tuple-element.148), channel_id=1, source_target_pairs={{0,2},{2,0},{4,6},{6,4},{8,10},{10,8},{12,14},{14,12},{16,18},{18,... | collective-permute-start | bytes 4718600 | tf_op jit(solution)/shard_map/ppermute | solution.py:914
  225.6 38.3 %collective-permute-start.34 = (bf16[16,64,4224]{2,1,0:T(8,128)(2,1)}, bf16[16,64,4224]{2,1,0:T(8,128)(2,1)}, u32[]{:S(2)}, u32[]{:S(2)}) collective-permute-start(bf16[16,64,4224]{2,1,0:T(8,128)(2,1)} %shard_map.541.own_ref), channel_id=1, source_target_pairs={{0,1},{1,0},{2,3},{3,2},{4,5},{5,4},{6,7},{7,6},{8,9},{9,8},{10,11... | collective-permute-start | bytes 25952264 | tf_op jit(solution)/shard_map/ppermute | solution.py:76
  225.6 37.1 %collective-permute-start.33 = (bf16[384,2048]{1,0:T(8,128)(2,1)}, bf16[384,2048]{1,0:T(8,128)(2,1)}, u32[]{:S(2)}, u32[]{:S(2)}) collective-permute-start(bf16[384,2048]{1,0:T(8,128)(2,1)} %shard_map.538.refs_2_), channel_id=1, source_target_pairs={{0,4},{2,6},{4,0},{6,2},{8,12},{10,14},{12,8},{14,10},{16,20},{18,... | collective-permute-start | bytes 4718600 | tf_op jit(solution)/shard_map/ppermute | solution.py:914
  227.1 36.8 %collective-permute-start.32 = (bf16[384,2048]{1,0:T(8,128)(2,1)}, bf16[384,2048]{1,0:T(8,128)(2,1)}, u32[]{:S(2)}, u32[]{:S(2)}) collective-permute-start(bf16[384,2048]{1,0:T(8,128)(2,1)} %shard_map.538.refs_2_), channel_id=1, source_target_pairs={{0,2},{2,0},{4,6},{6,4},{8,10},{10,8},{12,14},{14,12},{16,18},{18,... | collective-permute-start | bytes 4718600 | tf_op jit(solution)/shard_map/ppermute | solution.py:914
  279.7 27.6 %collective-permute-start.36 = (bf16[192,2048]{1,0:T(8,128)(2,1)S(1)}, bf16[192,2048]{1,0:T(8,128)(2,1)S(1)}, u32[]{:S(2)}, u32[]{:S(2)}) collective-permute-start(bf16[192,2048]{1,0:T(8,128)(2,1)S(1)} %slice.126), channel_id=1, source_target_pairs={{0,4},{2,6},{4,0},{6,2},{8,12},{10,14},{12,8},{14,10},{16,20},{18,... | collective-permute-start | bytes 2359304 | tf_op jit(solution)/shard_map/ppermute | solution.py:914
  280.3 26.9 %collective-permute-start.35 = (bf16[192,2048]{1,0:T(8,128)(2,1)S(1)}, bf16[192,2048]{1,0:T(8,128)(2,1)S(1)}, u32[]{:S(2)}, u32[]{:S(2)}) collective-permute-start(bf16[192,2048]{1,0:T(8,128)(2,1)S(1)} %slice.125), channel_id=1, source_target_pairs={{0,2},{2,0},{4,6},{6,4},{8,10},{10,8},{12,14},{14,12},{16,18},{18,... | collective-permute-start | bytes 2359304 | tf_op jit(solution)/shard_map/ppermute | solution.py:914
  309.2 33.7 %collective-permute-start.37 = (bf16[192,2048]{1,0:T(8,128)(2,1)}, bf16[192,2048]{1,0:T(8,128)(2,1)S(1)}, u32[]{:S(2)}, u32[]{:S(2)}) collective-permute-start(bf16[192,2048]{1,0:T(8,128)(2,1)} %slice.128), channel_id=1, source_target_pairs={{0,2},{2,0},{4,6},{6,4},{8,10},{10,8},{12,14},{14,12},{16,18},{18,... | collective-permute-start | bytes 2359304 | tf_op jit(solution)/shard_map/ppermute | solution.py:914
  309.7 33.2 %collective-permute-start.38 = (bf16[192,2048]{1,0:T(8,128)(2,1)}, bf16[192,2048]{1,0:T(8,128)(2,1)S(1)}, u32[]{:S(2)}, u32[]{:S(2)}) collective-permute-start(bf16[192,2048]{1,0:T(8,128)(2,1)} %slice.129), channel_id=1, source_target_pairs={{0,4},{2,6},{4,0},{6,2},{8,12},{10,14},{12,8},{14,10},{16,20},{18,... | collective-permute-start | bytes 2359304 | tf_op jit(solution)/shard_map/ppermute | solution.py:914
  360.2 23.9 %collective-permute-start.40 = (bf16[192,2048]{1,0:T(8,128)(2,1)S(1)}, bf16[192,2048]{1,0:T(8,128)(2,1)S(1)}, u32[]{:S(2)}, u32[]{:S(2)}) collective-permute-start(bf16[192,2048]{1,0:T(8,128)(2,1)S(1)} %get-tuple-element.172), channel_id=1, source_target_pairs={{0,4},{2,6},{4,0},{6,2},{8,12},{10,14},{12,8},{14,10},{16,20},{18,... | collective-permute-start | bytes 2359304 | tf_op jit(solution)/shard_map/ppermute | solution.py:914
  360.8 23.2 %collective-permute-start.39 = (bf16[192,2048]{1,0:T(8,128)(2,1)S(1)}, bf16[192,2048]{1,0:T(8,128)(2,1)S(1)}, u32[]{:S(2)}, u32[]{:S(2)}) collective-permute-start(bf16[192,2048]{1,0:T(8,128)(2,1)S(1)} %get-tuple-element.168.refs_2_), channel_id=1, source_target_pairs={{0,2},{2,0},{4,6},{6,4},{8,10},{10,8},{12,14},{14,12},{16,18},{18,... | collective-permute-start | bytes 2359304 | tf_op jit(solution)/shard_map/ppermute | solution.py:914
  387.0 45.9 %collective-permute-start.41 = (bf16[384,2048]{1,0:T(8,128)(2,1)S(1)}, bf16[384,2048]{1,0:T(8,128)(2,1)S(1)}, u32[]{:S(2)}, u32[]{:S(2)}) collective-permute-start(bf16[384,2048]{1,0:T(8,128)(2,1)S(1)} %get-tuple-element.173.refs_9_), channel_id=1, source_target_pairs={{0,2},{2,0},{4,6},{6,4},{8,10},{10,8},{12,14},{14,12},{16,18},{18,... | collective-permute-start | bytes 4718600 | tf_op jit(solution)/shard_map/ppermute | solution.py:914
  387.6 45.2 %collective-permute-start.42 = (bf16[384,2048]{1,0:T(8,128)(2,1)S(1)}, bf16[384,2048]{1,0:T(8,128)(2,1)S(1)}, u32[]{:S(2)}, u32[]{:S(2)}) collective-permute-start(bf16[384,2048]{1,0:T(8,128)(2,1)S(1)} %get-tuple-element.174.refs_10_), channel_id=1, source_target_pairs={{0,4},{2,6},{4,0},{6,2},{8,12},{10,14},{12,8},{14,10},{16,20},{18,... | collective-permute-start | bytes 4718600 | tf_op jit(solution)/shard_map/ppermute | solution.py:914
  432.3 39.0 %collective-permute-start.48 = (bf16[16,64,1408]{2,1,0:T(8,128)(2,1)}, bf16[16,64,1408]{2,1,0:T(8,128)(2,1)}, u32[]{:S(2)}, u32[]{:S(2)}) collective-permute-start(bf16[16,64,1408]{2,1,0:T(8,128)(2,1)} %get-tuple-element.186), channel_id=1, source_target_pairs={{0,1},{1,0},{2,3},{3,2},{4,5},{5,4},{6,7},{7,6},{8,9},{9,8},{10,11... | collective-permute-start | bytes 8650760 | tf_op jit(solution)/shard_map/ppermute | solution.py:76
  432.3 40.6 %collective-permute-start.49 = (bf16[16,64,2816]{2,1,0:T(8,128)(2,1)}, bf16[16,64,2816]{2,1,0:T(8,128)(2,1)}, u32[]{:S(2)}, u32[]{:S(2)}) collective-permute-start(bf16[16,64,2816]{2,1,0:T(8,128)(2,1)} %get-tuple-element.188), channel_id=1, source_target_pairs={{0,1},{1,0},{2,3},{3,2},{4,5},{5,4},{6,7},{7,6},{8,9},{9,8},{10,11... | collective-permute-start | bytes 17301512 | tf_op jit(solution)/shard_map/ppermute | solution.py:76
  458.3 39.7 %collective-permute-start.44 = (bf16[192,2048]{1,0:T(8,128)(2,1)}, bf16[192,2048]{1,0:T(8,128)(2,1)}, u32[]{:S(2)}, u32[]{:S(2)}) collective-permute-start(bf16[192,2048]{1,0:T(8,128)(2,1)} %get-tuple-element.181), channel_id=1, source_target_pairs={{0,4},{2,6},{4,0},{6,2},{8,12},{10,14},{12,8},{14,10},{16,20},{18,... | collective-permute-start | bytes 2359304 | tf_op jit(solution)/shard_map/ppermute | solution.py:914
  458.9 40.5 %collective-permute-start.45 = (bf16[192,2048]{1,0:T(8,128)(2,1)}, bf16[192,2048]{1,0:T(8,128)(2,1)S(1)}, u32[]{:S(2)}, u32[]{:S(2)}) collective-permute-start(bf16[192,2048]{1,0:T(8,128)(2,1)} %get-tuple-element.183), channel_id=1, source_target_pairs={{0,2},{2,0},{4,6},{6,4},{8,10},{10,8},{12,14},{14,12},{16,18},{18,... | collective-permute-start | bytes 2359304 | tf_op jit(solution)/shard_map/ppermute | solution.py:914
  460.4 39.7 %collective-permute-start.43 = (bf16[192,2048]{1,0:T(8,128)(2,1)}, bf16[192,2048]{1,0:T(8,128)(2,1)}, u32[]{:S(2)}, u32[]{:S(2)}) collective-permute-start(bf16[192,2048]{1,0:T(8,128)(2,1)} %get-tuple-element.179), channel_id=1, source_target_pairs={{0,2},{2,0},{4,6},{6,4},{8,10},{10,8},{12,14},{14,12},{16,18},{18,... | collective-permute-start | bytes 2359304 | tf_op jit(solution)/shard_map/ppermute | solution.py:914
  471.3 30.2 %collective-permute-start.47 = (bf16[192,2048]{1,0:T(8,128)(2,1)}, bf16[192,2048]{1,0:T(8,128)(2,1)}, u32[]{:S(2)}, u32[]{:S(2)}) collective-permute-start(bf16[192,2048]{1,0:T(8,128)(2,1)} %get-tuple-element.185), channel_id=1, source_target_pairs={{0,4},{2,6},{4,0},{6,2},{8,12},{10,14},{12,8},{14,10},{16,20},{18,... | collective-permute-start | bytes 2359304 | tf_op jit(solution)/shard_map/ppermute | solution.py:914
  497.4 23.3 %collective-permute-start.52 = (bf16[256,1024]{1,0:T(8,128)(2,1)S(1)}, bf16[256,1024]{1,0:T(8,128)(2,1)S(1)}, u32[]{:S(2)}, u32[]{:S(2)}) collective-permute-start(bf16[256,1024]{1,0:T(8,128)(2,1)S(1)} %bitcast.204), channel_id=1, source_target_pairs={{0,4},{2,6},{4,0},{6,2},{8,12},{10,14},{12,8},{14,10},{16,20},{18,... | collective-permute-start | bytes 1572872 | tf_op jit(solution)/shard_map/ppermute | solution.py:914
  498.0 22.7 %collective-permute-start.53 = (bf16[256,1024]{1,0:T(8,128)(2,1)S(1)}, bf16[256,1024]{1,0:T(8,128)(2,1)S(1)}, u32[]{:S(2)}, u32[]{:S(2)}) collective-permute-start(bf16[256,1024]{1,0:T(8,128)(2,1)S(1)} %bitcast.202), channel_id=1, source_target_pairs={{0,2},{2,0},{4,6},{6,4},{8,10},{10,8},{12,14},{14,12},{16,18},{18,... | collective-permute-start | bytes 1572872 | tf_op jit(solution)/shard_map/ppermute | solution.py:914
  499.5 23.9 %collective-permute-start.50 = (bf16[256,1024]{1,0:T(8,128)(2,1)S(1)}, bf16[256,1024]{1,0:T(8,128)(2,1)S(1)}, u32[]{:S(2)}, u32[]{:S(2)}) collective-permute-start(bf16[256,1024]{1,0:T(8,128)(2,1)S(1)} %bitcast.201), channel_id=1, source_target_pairs={{0,2},{2,0},{4,6},{6,4},{8,10},{10,8},{12,14},{14,12},{16,18},{18,... | collective-permute-start | bytes 1572872 | tf_op jit(solution)/shard_map/ppermute | solution.py:914
  500.0 23.3 %collective-permute-start.51 = (bf16[256,1024]{1,0:T(8,128)(2,1)S(1)}, bf16[256,1024]{1,0:T(8,128)(2,1)S(1)}, u32[]{:S(2)}, u32[]{:S(2)}) collective-permute-start(bf16[256,1024]{1,0:T(8,128)(2,1)S(1)} %bitcast.200), channel_id=1, source_target_pairs={{0,4},{2,6},{4,0},{6,2},{8,12},{10,14},{12,8},{14,10},{16,20},{18,... | collective-permute-start | bytes 1572872 | tf_op jit(solution)/shard_map/ppermute | solution.py:914
  521.3 23.3 %collective-permute-start.54 = (bf16[256,1024]{1,0:T(8,128)(2,1)S(1)}, bf16[256,1024]{1,0:T(8,128)(2,1)S(1)}, u32[]{:S(2)}, u32[]{:S(2)}) collective-permute-start(bf16[256,1024]{1,0:T(8,128)(2,1)S(1)} %get-tuple-element.200), channel_id=1, source_target_pairs={{0,2},{2,0},{4,6},{6,4},{8,10},{10,8},{12,14},{14,12},{16,18},{18,... | collective-permute-start | bytes 1572872 | tf_op jit(solution)/shard_map/ppermute | solution.py:914
  522.7 21.8 %collective-permute-start.55 = (bf16[256,1024]{1,0:T(8,128)(2,1)S(1)}, bf16[256,1024]{1,0:T(8,128)(2,1)S(1)}, u32[]{:S(2)}, u32[]{:S(2)}) collective-permute-start(bf16[256,1024]{1,0:T(8,128)(2,1)S(1)} %get-tuple-element.201), channel_id=1, source_target_pairs={{0,4},{2,6},{4,0},{6,2},{8,12},{10,14},{12,8},{14,10},{16,20},{18,... | collective-permute-start | bytes 1572872 | tf_op jit(solution)/shard_map/ppermute | solution.py:914
  575.7 28.0 %collective-permute-start.62 = (bf16[384,2048]{1,0:T(8,128)(2,1)S(1)}, bf16[384,2048]{1,0:T(8,128)(2,1)S(1)}, u32[]{:S(2)}, u32[]{:S(2)}) collective-permute-start(bf16[384,2048]{1,0:T(8,128)(2,1)S(1)} %bitcast.193), channel_id=1, source_target_pairs={{0,1},{1,0},{2,3},{3,2},{4,5},{5,4},{6,7},{7,6},{8,9},{9,8},{10,11... | collective-permute-start | bytes 4718600 | tf_op jit(solution)/shard_map/ppermute | solution.py:76
  578.8 22.9 %collective-permute-start.58 = (bf16[256,1280]{1,0:T(8,128)(2,1)S(1)}, bf16[256,1280]{1,0:T(8,128)(2,1)S(1)}, u32[]{:S(2)}, u32[]{:S(2)}) collective-permute-start(bf16[256,1280]{1,0:T(8,128)(2,1)S(1)} %bitcast.195), channel_id=1, source_target_pairs={{0,2},{2,0},{4,6},{6,4},{8,10},{10,8},{12,14},{14,12},{16,18},{18,... | collective-permute-start | bytes 1966088 | tf_op jit(solution)/shard_map/ppermute | solution.py:914
  579.7 22.0 %collective-permute-start.59 = (bf16[256,1280]{1,0:T(8,128)(2,1)S(1)}, bf16[256,1280]{1,0:T(8,128)(2,1)S(1)}, u32[]{:S(2)}, u32[]{:S(2)}) collective-permute-start(bf16[256,1280]{1,0:T(8,128)(2,1)S(1)} %bitcast.194), channel_id=1, source_target_pairs={{0,4},{2,6},{4,0},{6,2},{8,12},{10,14},{12,8},{14,10},{16,20},{18,... | collective-permute-start | bytes 1966088 | tf_op jit(solution)/shard_map/ppermute | solution.py:914
  593.3 22.8 %collective-permute-start.73 = (bf16[128,1024]{1,0:T(8,128)(2,1)S(1)}, bf16[128,1024]{1,0:T(8,128)(2,1)S(1)}, u32[]{:S(2)}, u32[]{:S(2)}) collective-permute-start(bf16[128,1024]{1,0:T(8,128)(2,1)S(1)} %add_convert_fusion.4), channel_id=1, source_target_pairs={{0,8},{2,10},{4,12},{6,14},{8,16},{10,18},{12,20},{14,22},{16,24},... | collective-permute-start | bytes 786440 | tf_op jit(solution)/shard_map/ppermute | solution.py:917
  602.5 22.3 %collective-permute-start.60 = (bf16[256,1280]{1,0:T(8,128)(2,1)S(1)}, bf16[256,1280]{1,0:T(8,128)(2,1)S(1)}, u32[]{:S(2)}, u32[]{:S(2)}) collective-permute-start(bf16[256,1280]{1,0:T(8,128)(2,1)S(1)} %get-tuple-element.208), channel_id=1, source_target_pairs={{0,2},{2,0},{4,6},{6,4},{8,10},{10,8},{12,14},{14,12},{16,18},{18,... | collective-permute-start | bytes 1966088 | tf_op jit(solution)/shard_map/ppermute | solution.py:914
  603.7 21.0 %collective-permute-start.61 = (bf16[256,1280]{1,0:T(8,128)(2,1)S(1)}, bf16[256,1280]{1,0:T(8,128)(2,1)S(1)}, u32[]{:S(2)}, u32[]{:S(2)}) collective-permute-start(bf16[256,1280]{1,0:T(8,128)(2,1)S(1)} %get-tuple-element.209), channel_id=1, source_target_pairs={{0,4},{2,6},{4,0},{6,2},{8,12},{10,14},{12,8},{14,10},{16,20},{18,... | collective-permute-start | bytes 1966088 | tf_op jit(solution)/shard_map/ppermute | solution.py:914
  617.2 38.3 %collective-permute-start.74 = (bf16[128,1024]{1,0:T(8,128)(2,1)S(1)}, bf16[128,1024]{1,0:T(8,128)(2,1)S(1)}, u32[]{:S(2)}, u32[]{:S(2)}) collective-permute-start(bf16[128,1024]{1,0:T(8,128)(2,1)S(1)} %add_convert_fusion.3), channel_id=1, source_target_pairs={{0,8},{2,10},{4,12},{6,14},{8,16},{10,18},{12,20},{14,22},{16,24},... | collective-permute-start | bytes 786440 | tf_op jit(solution)/shard_map/ppermute | solution.py:917
  630.8 24.5 %collective-permute-start.66 = (bf16[128,1280]{1,0:T(8,128)(2,1)S(1)}, bf16[128,1280]{1,0:T(8,128)(2,1)S(1)}, u32[]{:S(2)}, u32[]{:S(2)}) collective-permute-start(bf16[128,1280]{1,0:T(8,128)(2,1)S(1)} %dynamic-slice_convert_fusion), channel_id=1, source_target_pairs={{0,8},{2,10},{4,12},{6,14},{8,16},{10,18},{12,20},{14,22},{16,24},... | collective-permute-start | bytes 983048 | tf_op jit(solution)/shard_map/ppermute | solution.py:917
  637.9 32.3 %collective-permute-start.64 = (bf16[192,2048]{1,0:T(8,128)(2,1)S(1)}, bf16[192,2048]{1,0:T(8,128)(2,1)S(1)}, u32[]{:S(2)}, u32[]{:S(2)}) collective-permute-start(bf16[192,2048]{1,0:T(8,128)(2,1)S(1)} %get-tuple-element.217), channel_id=1, source_target_pairs={{0,4},{2,6},{4,0},{6,2},{8,12},{10,14},{12,8},{14,10},{16,20},{18,... | collective-permute-start | bytes 2359304 | tf_op jit(solution)/shard_map/ppermute | solution.py:914
  638.6 31.6 %collective-permute-start.65 = (bf16[192,2048]{1,0:T(8,128)(2,1)S(1)}, bf16[192,2048]{1,0:T(8,128)(2,1)S(1)}, u32[]{:S(2)}, u32[]{:S(2)}) collective-permute-start(bf16[192,2048]{1,0:T(8,128)(2,1)S(1)} %get-tuple-element.218), channel_id=1, source_target_pairs={{0,2},{2,0},{4,6},{6,4},{8,10},{10,8},{12,14},{14,12},{16,18},{18,... | collective-permute-start | bytes 2359304 | tf_op jit(solution)/shard_map/ppermute | solution.py:914
  671.1 33.5 %collective-permute-start.71 = (bf16[128,1280]{1,0:T(8,128)(2,1)}, bf16[128,1280]{1,0:T(8,128)(2,1)S(1)}, u32[]{:S(2)}, u32[]{:S(2)}) collective-permute-start(bf16[128,1280]{1,0:T(8,128)(2,1)} %convert_element_type.176), channel_id=1, source_target_pairs={{0,8},{2,10},{4,12},{6,14},{8,16},{10,18},{12,20},{14,22},{16,24},... | collective-permute-start | bytes 983048 | tf_op jit(solution)/shard_map/ppermute | solution.py:917
  675.0 22.8 %collective-permute-start.76 = (bf16[1,64,4224]{2,1,0:T(8,128)(2,1)S(1)}, bf16[1,64,4224]{2,1,0:T(8,128)(2,1)S(1)}, u32[]{:S(2)}, u32[]{:S(2)}) collective-permute-start(bf16[1,64,4224]{2,1,0:T(8,128)(2,1)S(1)} %get-tuple-element.224), channel_id=1, source_target_pairs={{0,4},{2,6},{4,0},{6,2},{8,12},{10,14},{12,8},{14,10},{16,20},{18,... | collective-permute-start | bytes 1622024 | tf_op jit(solution)/shard_map/ppermute | solution.py:914
  677.1 22.5 %collective-permute-start.77 = (bf16[1,64,4224]{2,1,0:T(8,128)(2,1)S(1)}, bf16[1,64,4224]{2,1,0:T(8,128)(2,1)S(1)}, u32[]{:S(2)}, u32[]{:S(2)}) collective-permute-start(bf16[1,64,4224]{2,1,0:T(8,128)(2,1)S(1)} %get-tuple-element.225), channel_id=1, source_target_pairs={{0,6},{2,4},{4,2},{6,0},{8,14},{10,12},{12,10},{14,8},{16,22},{18,... | collective-permute-start | bytes 1622024 | tf_op jit(solution)/shard_map/ppermute | solution.py:914
  (153 other events, 1637.7 us)
Sparse Core Ops, SparseCore 0:
  60.0 165.5 all-gather.1
  482.5 172.7 reduce-scatter.1
